TPU v7x, 128 devices: a whole 4x4x4 slice. The times are simulated.
128 devices in a mesh: dp: 16 (over z, x_hi, core), head: 8 (over y, x_lo).
Axes of the slice: x: 4 (x_hi: 2, x_lo: 2; x = x_hi * 2 + x_lo), y: 4, z: 4, core: 2. Of those that a mesh axis runs over, the one named last changes fastest.
Arguments:
- hidden_in: bfloat16 [8192, 2048], P('dp'), may hold values from -6 to 6
- norm_gain: float32 [2048], replicated, may hold values from 0.5 to 1.5
- w_query: bfloat16 [2048, 2048], P('dp', 'head'), may hold values from -0.125 to 0.125
- w_forget: bfloat16 [2048, 2048], P('dp', 'head'), may hold values from -0.125 to 0.125
- w_input: bfloat16 [2048, 2048], P('dp', 'head'), may hold values from -0.125 to 0.125
- w_outgate: bfloat16 [2048, 2048], P('dp', 'head'), may hold values from -0.125 to 0.125
- lower_bounds: float32 [24, 2048], P(None, 'head'), may hold values from -20 to 1
- layer_index: int32 [1], replicated, may hold values from 1 to 23
- group_gain: float32 [128], replicated, may hold values from 0.5 to 1.5
- w_output: bfloat16 [2048, 2048], P('head', 'dp'), may hold values from -0.25 to 0.25
- ffn_gain: float32 [2048], replicated, may hold values from 0.5 to 1.5
- w_gate: bfloat16 [2048, 5632], P('dp', 'head'), may hold values from -0.125 to 0.125
- w_up: bfloat16 [2048, 5632], P('dp', 'head'), may hold values from -0.125 to 0.125
- w_down: bfloat16 [5632, 2048], P('head', 'dp'), may hold values from -0.15625 to 0.15625
- seq_lengths: int32 [12], replicated, may hold values from 1 to 7840, as said below
- grad_out: bfloat16 [8192, 2048], P('dp'), may hold values from -6 to 6
Outputs:
- block_out: bfloat16 [8192, 2048], P(('dp', 'head'))
- grad_in: float32 [8192, 2048], P(('dp', 'head'))
- grad_norm_gain: float32 [2048], replicated
- grad_query: float32 [2048, 2048], P('dp', 'head')
- grad_forget: float32 [2048, 2048], P('dp', 'head')
- grad_input: float32 [2048, 2048], P('dp', 'head')
- grad_outgate: float32 [2048, 2048], P('dp', 'head')
- grad_bounds: float32 [24, 2048], P(None, 'head')
- grad_group_gain: float32 [128], replicated
- grad_output: float32 [2048, 2048], P('head', 'dp')
- grad_ffn_gain: float32 [2048], replicated
- grad_gate: float32 [2048, 5632], P('dp', 'head')
- grad_up: float32 [2048, 5632], P('dp', 'head')
- grad_down: float32 [5632, 2048], P('head', 'dp')
- forget_mean: float32 [1], replicated
Inputs may be any that keep to these rules, and one draw needn't show every extreme that they name: `seq_lengths`: 12 positive lengths, in order of the packed tokens, summing to 8192; one of them, at a position drawn from the seed, is the longest.
All inputs are finite; a program needn't handle non-finite values.
Results may differ from a plain program's by a relative error of at most 0.029.
Values may be sent and summed in bfloat16 or wider, within the bound.
A program may use at most 128 MiB of HBM per device.

v0:
```python
from functools import partial

import jax
import jax.numpy as jnp
from jax import lax
from jax.sharding import PartitionSpec as P

D = 2048
KDIM = 128
BLOCK = 64


epsilon = 1e-06
topmost_precision = lax.Precision.HIGHEST


def carried_in(part, axis, combine, identity):
    place = lax.axis_index(axis)
    gathered = jax.tree.map(lambda a: lax.all_gather(a, axis), part)
    state = jax.tree.map(lambda a, e: jnp.zeros_like(a) + jnp.asarray(e, a.dtype), part, identity)

    def one(step, state):
        return combine(
            state, jax.tree.map(lambda a: lax.dynamic_index_in_dim(a, step, 0, False), gathered)
        )

    return lax.fori_loop(0, place, one, state)


def prefix(x, axis, combine, identity):
    count, place = (lax.axis_size(axis), lax.axis_index(axis))
    everything = jax.tree.map(
        lambda part, kind: lax.all_gather(part.astype(kind), axis), x, (jnp.bfloat16, jnp.bfloat16)
    )
    start = jax.tree.map(
        lambda part, zero: jnp.broadcast_to(jnp.asarray(zero, part.dtype), part.shape), x, identity
    )

    def step(k, before):
        at = count - 1 - k
        reached = at > place
        new = combine(
            before, jax.tree.map(lambda part, own: part[at].astype(own.dtype), everything, x)
        )
        return jax.tree.map(lambda a, b: jnp.where(reached, a, b), new, before)

    return lax.fori_loop(0, count, step, start)


def normalize(value_rows, weight):
    inverse = lax.rsqrt(jnp.mean(value_rows * value_rows, axis=-1, keepdims=True) + epsilon)
    return (value_rows * inverse * weight, inverse)


def norm_back(grad, value_rows, inverse, weight):
    scaled = grad * weight
    normed = value_rows * inverse
    back = inverse * (scaled - normed * jnp.mean(scaled * normed, axis=-1, keepdims=True))
    return (back, grad * normed)


def contract_last(left, right):
    return lax.dot_general(
        left, right, (((1,), (1,)), ((), ())), preferred_element_type=jnp.float32
    )


def contract_first(left, right):
    return lax.dot_general(
        left, right, (((0,), (0,)), ((), ())), preferred_element_type=jnp.float32
    )


def silu_slope(value_rows):
    logistic = jax.nn.sigmoid(value_rows)
    return logistic * (1.0 + value_rows * (1.0 - logistic))


def chain(earlier, later):
    return (earlier[0] * later[0], later[0][:, :, None] * earlier[1] + later[1])


def rows_of(array, row_start, row_count):
    return lax.dynamic_slice_in_dim(array, row_start, row_count, 0)


def block_step(carry, block):
    recurrent_state, before = carry
    query, keys, value_rows, log_forget, segment = block
    span = segment.shape[0]
    running = jnp.cumsum(log_forget, axis=0)
    ending = running[span - 1]
    causal = lax.broadcasted_iota(jnp.int32, (span, span), 0) >= lax.broadcasted_iota(
        jnp.int32, (span, span), 1
    )
    linked = (causal & (segment[:, None] == segment[None, :])).astype(jnp.float32)
    lifted = query * jnp.exp(running - ending[None])
    lowered = keys * jnp.exp(ending[None] - running)
    scores = jnp.einsum("thk,shk->hts", lifted, lowered, precision=topmost_precision) * linked[None]
    inner = jnp.einsum("hts,shv->thv", scores, value_rows, precision=topmost_precision)
    carried = (segment == before).astype(jnp.float32)[:, None, None]
    reach_extent = query * jnp.exp(running) * carried
    outer_product = jnp.einsum(
        "fmp,mpu->fmu", reach_extent, recurrent_state, precision=topmost_precision
    )
    final = segment[span - 1]
    tail_rows = lowered * (segment == final).astype(jnp.float32)[:, None, None]
    recurrent_state = recurrent_state * (jnp.exp(ending) * carried[span - 1])[:, :, None]
    recurrent_state = recurrent_state + jnp.einsum(
        "jem,jel->eml", tail_rows, value_rows, precision=topmost_precision
    )
    return ((recurrent_state, final), inner + outer_product)


def run_blocks(segment, before, query, keys, value_rows, log_forget, recurrent_state):
    count = query.shape[0] // BLOCK
    heads_here = query.shape[1] // KDIM

    def shaped(array):
        return array.reshape(count, BLOCK, heads_here, KDIM)

    carry, outputs = lax.scan(
        jax.checkpoint(block_step),
        (recurrent_state, before),
        (
            shaped(query),
            shaped(keys),
            shaped(value_rows),
            shaped(log_forget),
            segment.reshape(count, BLOCK),
        ),
    )
    return (outputs.reshape(query.shape[0], heads_here, KDIM), carry[0])


def local(
    hidden_in,
    norm_gain,
    w_query,
    w_forget,
    w_input,
    w_outgate,
    lower_bounds,
    layer_index,
    group_gain,
    w_output,
    ffn_gain,
    w_gate,
    w_up,
    w_down,
    seq_lengths,
    grad_out,
):
    tokens_here = hidden_in.shape[0]
    width_here = w_query.shape[1]
    heads_here = width_here // KDIM
    row_count = tokens_here // lax.axis_size("head")
    row_start = lax.axis_index("head") * row_count
    column_start = lax.axis_index("head") * width_here
    inputs_float = hidden_in.astype(jnp.float32)
    inputs_rows = rows_of(inputs_float, row_start, row_count)
    normed_in, inverse_in = normalize(inputs_float, norm_gain)
    normed_low = normed_in.astype(jnp.bfloat16)
    proj_full = (
        lax.all_gather(w_query, "dp", axis=0, tiled=True),
        lax.all_gather(w_forget, "dp", axis=0, tiled=True),
        lax.all_gather(w_input, "dp", axis=0, tiled=True),
        lax.all_gather(w_outgate, "dp", axis=0, tiled=True),
    )
    rest_full = (
        lax.all_gather(w_output, "dp", axis=1, tiled=True),
        lax.all_gather(w_gate, "dp", axis=0, tiled=True),
        lax.all_gather(w_up, "dp", axis=0, tiled=True),
        lax.all_gather(w_down, "dp", axis=1, tiled=True),
    )
    query_raw = jnp.dot(normed_low, proj_full[0], preferred_element_type=jnp.float32)
    forget_raw = jnp.dot(normed_low, proj_full[1], preferred_element_type=jnp.float32)
    input_raw = jnp.dot(normed_low, proj_full[2], preferred_element_type=jnp.float32)
    outgate_raw = jnp.dot(normed_low, proj_full[3], preferred_element_type=jnp.float32)
    soft_bounds = jax.nn.softmax(lower_bounds, axis=0)
    depth = lax.broadcasted_iota(jnp.int32, (lower_bounds.shape[0], 1), 0)
    picked = ((depth >= 1) & (depth <= layer_index[0])).astype(jnp.float32)
    bound = jnp.sum(soft_bounds * picked, axis=0)
    logistic = jax.nn.sigmoid(forget_raw)
    forget = bound + (1.0 - bound) * logistic
    forget_local = jnp.sum(forget)
    query_float = jax.nn.silu(query_raw).astype(jnp.bfloat16).astype(jnp.float32)
    keys_float = (1.0 - forget).astype(jnp.bfloat16).astype(jnp.float32)
    values_float = input_raw.astype(jnp.bfloat16).astype(jnp.float32)
    log_forget = jnp.log(forget)
    starts = jnp.cumsum(seq_lengths) - seq_lengths
    first_place = lax.axis_index("dp") * tokens_here
    position = first_place + lax.broadcasted_iota(jnp.int32, (tokens_here, 1), 0)
    segment = jnp.sum((starts[None, :] <= position).astype(jnp.int32), axis=1) - 1
    before = jnp.sum((starts <= first_place - 1).astype(jnp.int32)) - 1
    zero_state = jnp.zeros((heads_here, KDIM, KDIM), jnp.float32)
    mixed_on_device, local_end = run_blocks(
        segment, before, query_float, keys_float, values_float, log_forget, zero_state
    )
    count = tokens_here // BLOCK
    inside = jnp.cumsum(log_forget.reshape(count, BLOCK, width_here), axis=1)
    totals = inside[:, BLOCK - 1]
    offsets = jnp.cumsum(totals, axis=0) - totals
    device_run = (inside + offsets[:, None]).reshape(tokens_here, width_here)
    joined = (segment == before).astype(jnp.float32)[:, None]
    reach_extent = (query_float * jnp.exp(device_run) * joined).reshape(
        tokens_here, heads_here, KDIM
    )
    carry_rate = (jnp.exp(device_run[tokens_here - 1]) * joined[tokens_here - 1]).reshape(
        heads_here, KDIM
    )
    incoming_state = carried_in(
        (carry_rate, local_end), "dp", chain, (jnp.ones_like(carry_rate), jnp.zeros_like(local_end))
    )[1]
    mixed_output = mixed_on_device + jnp.einsum(
        "fmp,mpu->fmu", reach_extent, incoming_state, precision=topmost_precision
    )
    outgate_heads = outgate_raw.reshape(tokens_here, heads_here, KDIM)
    group_normed, group_inverse = normalize(mixed_output, group_gain)
    outgate_silu = jax.nn.silu(outgate_heads)
    gated = (group_normed * outgate_silu).reshape(tokens_here, width_here).astype(jnp.bfloat16)
    branch_part = jnp.dot(gated, rest_full[0], preferred_element_type=jnp.float32)
    residual = inputs_float + lax.psum(branch_part, "head")
    normed_mid, inverse_mid = normalize(residual, ffn_gain)
    mid_low = normed_mid.astype(jnp.bfloat16)
    residual_rows = rows_of(residual, row_start, row_count)
    gate_act = jnp.dot(mid_low, rest_full[1], preferred_element_type=jnp.float32)
    up_act = jnp.dot(mid_low, rest_full[2], preferred_element_type=jnp.float32)
    gate_silu = jax.nn.silu(gate_act)
    hidden_low = (gate_silu * up_act).astype(jnp.bfloat16)
    ffn_rows = lax.psum_scatter(
        jnp.dot(hidden_low, rest_full[3], preferred_element_type=jnp.float32).astype(jnp.bfloat16),
        "head",
        scatter_dimension=0,
        tiled=True,
    ).astype(jnp.float32)
    block_out = (residual_rows + ffn_rows).astype(jnp.bfloat16)
    back_full = (
        lax.all_gather(w_query, "dp", axis=0, tiled=True),
        lax.all_gather(w_forget, "dp", axis=0, tiled=True),
        lax.all_gather(w_input, "dp", axis=0, tiled=True),
        lax.all_gather(w_outgate, "dp", axis=0, tiled=True),
        lax.all_gather(w_output, "dp", axis=1, tiled=True),
        lax.all_gather(w_gate, "dp", axis=0, tiled=True),
        lax.all_gather(w_up, "dp", axis=0, tiled=True),
        lax.all_gather(w_down, "dp", axis=1, tiled=True),
    )
    grad_hidden = contract_last(grad_out, back_full[7])
    grad_down = contract_first(hidden_low, grad_out)
    grad_gate_act = (grad_hidden * up_act * silu_slope(gate_act)).astype(jnp.bfloat16)
    grad_up_act = (grad_hidden * gate_silu).astype(jnp.bfloat16)
    grad_gate = contract_first(mid_low, grad_gate_act)
    grad_up = contract_first(mid_low, grad_up_act)
    ffn_grads = (
        lax.psum_scatter(
            grad_gate.astype(jnp.bfloat16), "dp", scatter_dimension=0, tiled=True
        ).astype(jnp.float32),
        lax.psum_scatter(
            grad_up.astype(jnp.bfloat16), "dp", scatter_dimension=0, tiled=True
        ).astype(jnp.float32),
        lax.psum_scatter(
            grad_down.astype(jnp.bfloat16), "dp", scatter_dimension=1, tiled=True
        ).astype(jnp.float32),
    )
    mid_part = contract_last(grad_gate_act, back_full[5]) + contract_last(grad_up_act, back_full[6])
    grad_mid, ffn_terms = norm_back(
        lax.psum(mid_part.astype(jnp.bfloat16), "head").astype(jnp.float32),
        residual,
        inverse_mid,
        ffn_gain,
    )
    grad_residual = grad_out.astype(jnp.float32) + grad_mid
    grad_branch = grad_residual.astype(jnp.bfloat16)
    grad_residual_rows = rows_of(grad_residual, row_start, row_count)
    ffn_terms_rows = rows_of(ffn_terms, row_start, row_count)
    grad_gated = contract_last(grad_branch, back_full[4]).reshape(tokens_here, heads_here, KDIM)
    grad_output = contract_first(gated, grad_branch)
    grad_outgate_act = (
        (grad_gated * group_normed * silu_slope(outgate_heads))
        .reshape(tokens_here, width_here)
        .astype(jnp.bfloat16)
    )
    mixed_gradient, group_terms = norm_back(
        grad_gated * outgate_silu, mixed_output, group_inverse, group_gain
    )
    mixed_gradient = mixed_gradient.astype(jnp.bfloat16).astype(jnp.float32)
    backward_summed = jnp.einsum(
        "crb,cry->rby", reach_extent, mixed_gradient, precision=topmost_precision
    )
    state_out_grad = prefix(
        (carry_rate, backward_summed),
        "dp",
        chain,
        (jnp.ones_like(carry_rate), jnp.zeros_like(backward_summed)),
    )[1]
    recurrent_out, pull_back = jax.vjp(
        partial(run_blocks, segment, before),
        query_float,
        keys_float,
        values_float,
        log_forget,
        incoming_state,
    )
    recurrent_grads = pull_back((mixed_gradient, state_out_grad))
    grad_query_raw = (recurrent_grads[0] * silu_slope(query_raw)).astype(jnp.bfloat16)
    grad_forget_gate = recurrent_grads[3] / forget - recurrent_grads[1]
    grad_forget_raw = (grad_forget_gate * (1.0 - bound) * logistic * (1.0 - logistic)).astype(
        jnp.bfloat16
    )
    grad_input_raw = recurrent_grads[2].astype(jnp.bfloat16)
    bound_terms = jnp.sum(grad_forget_gate * (1.0 - logistic), axis=0)
    bound_full = lax.dynamic_update_slice_in_dim(
        jnp.zeros((D,), jnp.float32), bound_terms, column_start, 0
    )
    attn_grads = (
        lax.psum_scatter(
            contract_first(normed_low, grad_query_raw).astype(jnp.bfloat16),
            "dp",
            scatter_dimension=0,
            tiled=True,
        ).astype(jnp.float32),
        lax.psum_scatter(
            contract_first(normed_low, grad_forget_raw).astype(jnp.bfloat16),
            "dp",
            scatter_dimension=0,
            tiled=True,
        ).astype(jnp.float32),
        lax.psum_scatter(
            contract_first(normed_low, grad_input_raw).astype(jnp.bfloat16),
            "dp",
            scatter_dimension=0,
            tiled=True,
        ).astype(jnp.float32),
        lax.psum_scatter(
            contract_first(normed_low, grad_outgate_act).astype(jnp.bfloat16),
            "dp",
            scatter_dimension=0,
            tiled=True,
        ).astype(jnp.float32),
        lax.psum_scatter(
            grad_output.astype(jnp.bfloat16), "dp", scatter_dimension=1, tiled=True
        ).astype(jnp.float32),
    )
    partial_in = contract_last(grad_query_raw, back_full[0]) + contract_last(
        grad_forget_raw, back_full[1]
    )
    partial_in = (
        partial_in
        + contract_last(grad_input_raw, back_full[2])
        + contract_last(grad_outgate_act, back_full[3])
    )
    grad_normed_in = lax.psum_scatter(
        partial_in.astype(jnp.bfloat16), "head", scatter_dimension=0, tiled=True
    ).astype(jnp.float32)
    grad_first, norm_terms = norm_back(
        grad_normed_in, inputs_rows, rows_of(inverse_in, row_start, row_count), norm_gain
    )
    grad_in = grad_residual_rows + grad_first
    gain_sums = lax.psum(
        (
            jnp.sum(norm_terms, axis=0),
            jnp.sum(ffn_terms_rows, axis=0),
            bound_full,
            jnp.sum(group_terms, axis=(0, 1)),
            forget_local,
        ),
        ("dp", "head"),
    )
    grad_bounds = (
        soft_bounds
        * (picked - bound)
        * lax.dynamic_slice_in_dim(gain_sums[2], column_start, width_here, 0)
    )
    entries = float(tokens_here * lax.axis_size("dp") * width_here * lax.axis_size("head"))
    forget_mean = jnp.reshape(gain_sums[4] / entries, (1,))
    return (
        block_out,
        grad_in,
        gain_sums[0],
        attn_grads[0],
        attn_grads[1],
        attn_grads[2],
        attn_grads[3],
        grad_bounds,
        gain_sums[3],
        attn_grads[4],
        gain_sums[1],
        ffn_grads[0],
        ffn_grads[1],
        ffn_grads[2],
        forget_mean,
    )


def solution(mesh):
    return jax.shard_map(
        local,
        mesh=mesh,
        in_specs=(
            P("dp", None),
            P(),
            P("dp", "head"),
            P("dp", "head"),
            P("dp", "head"),
            P("dp", "head"),
            P(None, "head"),
            P(),
            P(),
            P("head", "dp"),
            P(),
            P("dp", "head"),
            P("dp", "head"),
            P("head", "dp"),
            P(),
            P("dp", None),
        ),
        out_specs=(
            P(("dp", "head"), None),
            P(("dp", "head"), None),
            P(),
            P("dp", "head"),
            P("dp", "head"),
            P("dp", "head"),
            P("dp", "head"),
            P(None, "head"),
            P(),
            P("head", "dp"),
            P(),
            P("dp", "head"),
            P("dp", "head"),
            P("head", "dp"),
            P(),
        ),
        check_vma=False,
    )
```

profile of v0, /device:TPU:1, one launch (start us, length us, event | category | flops | bytes accessed | tf_op | source)
XLA Modules:
  0.0 1632.3 jit_solution(7561269587344868625)
XLA Ops:
  18.8 40.3 %all-gather.13.cloned.1.call-done = bf16[2048,256]{1,0:T(8,128)(2,1)} async-done(((bf16[128,256]{1,0:T(8,128)(2,1)}), bf16[2048,256]{1,0:T(8,128)(2,1)}) %all-gather.13.cloned.1.call-update) | async-done | bytes 1048592 | tf_op jit(solution)/shard_map/all_gather | solution.py:166
  65.2 40.1 %all-gather.15.cloned.1.call-done = bf16[2048,256]{1,0:T(8,128)(2,1)} async-done(((bf16[128,256]{1,0:T(8,128)(2,1)}), bf16[2048,256]{1,0:T(8,128)(2,1)}) %all-gather.15.cloned.1.call-update) | async-done | bytes 1048592 | tf_op jit(solution)/shard_map/all_gather | solution.py:167
  116.2 35.2 %all-gather.17.cloned.1.call-done = bf16[2048,256]{1,0:T(8,128)(2,1)} async-done(((bf16[128,256]{1,0:T(8,128)(2,1)}), bf16[2048,256]{1,0:T(8,128)(2,1)}) %all-gather.17.cloned.1.call-update) | async-done | bytes 1048592 | tf_op jit(solution)/shard_map/all_gather | solution.py:165
  156.8 54.5 %while.84 = (s32[]{:T(128)}, f32[2,128,128]{2,1,0:T(8,128)S(1)}, s32[]{:T(128)}, f32[8,64,2,128]{3,1,0,2:T(8,128)}, f32[8,64,2,128]{3,2,1,0:T(2,128)S(1)}, /*ind...) while((s32[]{:T(128)}, f32[2,128,128]{2,1,0:T(8,128)S(1)}, ...), condition=%wide.region_9.10_spmd.clone, body=%wide.region_7.9_spmd.clone.sunk | while | flops 76816896 | bytes 1712308 | solution.py:122
  219.2 21.4 %all_gather.54 = f32[16,2,128]{2,1,0:T(2,128)S(1)} all-gather(f32[1,2,128]{2,1,0:T(2,128)S(1)} %bitcast.420), channel_id=1, replica_groups=mesh['dp'=16,'head'=8] {'dp'}, dimensions={0}, use_global_device_ids=true | all-gather | bytes 17408 | tf_op jit(solution)/shard_map/all_gather | solution.py:19
  240.6 18.0 %all-gather.29.cloned.1.call-done = f32[32,128,128]{2,1,0:T(8,128)} async-done(((f32[2,128,128]{2,1,0:T(8,128)}), f32[32,128,128]{2,1,0:T(8,128)}) %all-gather.29.cloned.1.call-update) | async-done | bytes 2097168 | tf_op jit(solution)/shard_map/all_gather | solution.py:19
  261.4 43.2 %all-gather.19.cloned.1.call-done = bf16[2048,256]{1,0:T(8,128)(2,1)} async-done(((bf16[128,256]{1,0:T(8,128)(2,1)}), bf16[2048,256]{1,0:T(8,128)(2,1)}) %all-gather.19.cloned.1.call-update) | async-done | bytes 1048592 | tf_op jit(solution)/shard_map/all_gather | solution.py:168
  306.9 41.5 %all-gather.21.cloned.1.call-done = bf16[256,2048]{1,0:T(8,128)(2,1)} async-done(((bf16[256,128]{1,0:T(8,128)(2,1)}), bf16[256,2048]{1,0:T(8,128)(2,1)}) %all-gather.21.cloned.1.call-update) | async-done | bytes 1048592 | tf_op jit(solution)/shard_map/all_gather | solution.py:171
  354.7 179.8 %all-reduce.5.cloned.1.call-done = f32[512,2048]{1,0:T(8,128)} async-done(((f32[512,2048]{1,0:T(8,128)}), f32[512,2048]{1,0:T(8,128)}) %all-reduce.5.cloned.1.call-update) | async-done | bytes 4194320 | tf_op jit(solution)/shard_map/psum | solution.py:223
  542.5 45.8 %all-gather.23.cloned.1.call-done = bf16[2048,704]{0,1:T(8,128)(2,1)} async-done(((bf16[128,704]{0,1:T(8,128)(2,1)}), bf16[2048,704]{0,1:T(8,128)(2,1)}) %all-gather.23.cloned.1.call-update) | async-done | bytes 2883600 | tf_op jit(solution)/shard_map/all_gather | solution.py:172
  588.3 5.2 fusion.111
  593.6 45.6 %all-gather.25.cloned.1.call-done = bf16[2048,704]{0,1:T(8,128)(2,1)} async-done(((bf16[128,704]{0,1:T(8,128)(2,1)}), bf16[2048,704]{0,1:T(8,128)(2,1)}) %all-gather.25.cloned.1.call-update) | async-done | bytes 2883600 | tf_op jit(solution)/shard_map/all_gather | solution.py:173
  639.2 5.3 fusion.112
  644.5 45.4 %all-gather.27.cloned.1.call-done = bf16[704,2048]{1,0:T(8,128)(2,1)} async-done(((bf16[704,128]{1,0:T(8,128)(2,1)}), bf16[704,2048]{1,0:T(8,128)(2,1)}) %all-gather.27.cloned.1.call-update) | async-done | bytes 2883600 | tf_op jit(solution)/shard_map/all_gather | solution.py:174
  689.9 6.5 multiply_convert_fusion.2
  702.5 101.3 %all-reduce.7.cloned.1.call-done = bf16[512,2048]{1,0:T(8,128)(2,1)} async-done(((bf16[512,2048]{1,0:T(8,128)(2,1)}), bf16[512,2048]{1,0:T(8,128)(2,1)}) %all-reduce.7.cloned.1.call-update) | async-done | bytes 2097168 | tf_op jit(solution)/shard_map/psum | solution.py:267
  823.7 5.3 convolution_convert_fusion.3
  829.0 4.8 convolution_convert_fusion.1
  839.2 24.6 %all_gather.62 = bf16[16,2,128]{2,1,0:T(2,128)(2,1)S(1)} all-gather(bf16[1,2,128]{2,1,0:T(2,128)(2,1)S(1)} %convert_element_type.285), channel_id=1, replica_groups=mesh['dp'=16,'head'=8] {'dp'}, dimensions={0}, use_global_device_ids=true | all-gather | bytes 8704 | tf_op jit(solution)/shard_map/all_gather | solution.py:33
  863.7 4.8 convolution_convert_fusion
  873.4 62.3 %while.82 = (s32[]{:T(128)}, f32[2,128,128]{2,1,0:T(8,128)S(1)}, s32[]{:T(128)}, f32[8,2,128,128]{3,2,1,0:T(8,128)}, s32[8]{0:T(128)S(1)}, /*index=5*/f32[8,64,2...) while((s32[]{:T(128)}, f32[2,128,128]{2,1,0:T(8,128)S(1)}, ...), condition=%wide.region_25.26_spmd, body=%wide.region_23.25_spmd.sunk | while | flops 26313156 | bytes 990704 | solution.py:122
  935.8 4.8 convolution_convert_fusion.2
  947.0 16.4 %while.85 = (s32[]{:T(128)}, f32[2,128,128]{2,1,0:T(8,128)S(1)}, s32[]{:T(128)}, bf16[16,2,128]{2,1,0:T(2,128)(2,1)S(1)}, bf16[16,2,128,128]{3,2,1,0:T(8,128)(2,...) while((s32[]{:T(128)}, f32[2,128,128]{2,1,0:T(8,128)S(1)}, s32[]{:T(128)}, ...), condition=%wide.region_22.23_spmd.clone, body=%wide.region_21.22_spmd.clone.sunk | while | flops 164104 | bytes 330415 | solution.py:47
  965.4 120.3 %while.83 = (s32[]{:T(128)}, f32[2,128,128]{2,1,0:T(8,128)S(1)}, f32[8,64,2,128]{3,2,1,0:T(2,128)S(1)}, f32[8,64,2,128]{3,2,1,0:T(2,128)S(1)}, bf16[8,64,2,128]{...) while((s32[]{:T(128)}, f32[2,128,128]{2,1,0:T(8,128)S(1)}, ...), condition=%wide.region_32.33_spmd, body=%wide.region_26.32_spmd.sunk | while | flops 166478848 | bytes 5220093 | solution.py:122
  1114.4 18.4 %reduce-scatter.33.cloned.1.call-done = bf16[128,704]{1,0:T(8,128)(2,1)} async-done(((bf16[2048,704]{1,0:T(8,128)(2,1)}), bf16[128,704]{1,0:T(8,128)(2,1)}) %reduce-scatter.33.cloned.1.call-update) | async-done | bytes 180240
  1134.6 76.4 %reduce-scatter.35.cloned.1.call-done = bf16[128,704]{1,0:T(8,128)(2,1)} async-done(((bf16[2048,704]{1,0:T(8,128)(2,1)}), bf16[128,704]{1,0:T(8,128)(2,1)}) %reduce-scatter.35.cloned.1.call-update) | async-done | bytes 180240
  1212.9 76.4 %reduce-scatter.37.cloned.1.call-done = bf16[128,704]{1,0:T(8,128)(2,1)} async-done(((bf16[2048,704]{1,0:T(8,128)(2,1)}), bf16[128,704]{1,0:T(8,128)(2,1)}) %reduce-scatter.37.cloned.1.call-update) | async-done | bytes 180240
  1291.2 67.1 %reduce-scatter.23.cloned.1.call-done = bf16[128,256]{1,0:T(8,128)(2,1)} async-done(((bf16[2048,256]{1,0:T(8,128)(2,1)}), bf16[128,256]{1,0:T(8,128)(2,1)}) %reduce-scatter.23.cloned.1.call-update) | async-done | bytes 65552 | tf_op jit(solution)/shard_map/reduce_scatter | solution.py:316
  1359.7 68.6 %reduce-scatter.25.cloned.1.call-done = bf16[128,256]{1,0:T(8,128)(2,1)} async-done(((bf16[2048,256]{1,0:T(8,128)(2,1)}), bf16[128,256]{1,0:T(8,128)(2,1)}) %reduce-scatter.25.cloned.1.call-update) | async-done | bytes 65552 | tf_op jit(solution)/shard_map/reduce_scatter | solution.py:322
  1429.8 68.3 %reduce-scatter.27.cloned.1.call-done = bf16[128,256]{1,0:T(8,128)(2,1)} async-done(((bf16[2048,256]{1,0:T(8,128)(2,1)}), bf16[128,256]{1,0:T(8,128)(2,1)}) %reduce-scatter.27.cloned.1.call-update) | async-done | bytes 65552 | tf_op jit(solution)/shard_map/reduce_scatter | solution.py:328
  1499.7 54.1 %reduce-scatter.21.cloned.1.call-done = bf16[64,2048]{1,0:T(8,128)(2,1)} async-done(((bf16[512,2048]{1,0:T(8,128)(2,1)}), bf16[64,2048]{1,0:T(8,128)(2,1)}) %reduce-scatter.21.cloned.1.call-update) | async-done | bytes 262160 | tf_op jit(solution)/shard_map/reduce_scatter | solution.py:352
  1555.2 65.2 %all-reduce.1 = (f32[2048]{0:T(1024)}, f32[2048]{0:T(1024)S(1)}, f32[128]{0:T(128)}, f32[2048]{0:T(1024)}, f32[]{:T(128)}) all-reduce(f32[2048]{0:T(1024)S(1)} %get-tuple-element.761, f32[2048]{0:T(1024)S(1)} %dynamic_update_slice.51, f32[128]{0:T(128)S(1)} %copy-done.50, ...), channel_id=1, replica_groups=mesh['dp'=16,'head'=8] {'dp','head'}, use_global_device_ids=true, to_apply=%region_36.37 | all-reduce | flops 6273 | bytes 50184 | tf_op jit(solution)/shard_map/psum | solution.py:359
  (751 shorter events, 383.2 us)
Async XLA Ops:
  7.2 51.9 %all-gather.13.cloned.1.call-start = ((), (), s32[]{:S(2)}) async-start(), calls=%async_computation.10 | async-start | bytes 1114112 | tf_op jit(solution)/shard_map/all_gather | solution.py:166
  7.9 97.4 %all-gather.15.cloned.1.call-start = ((), (), s32[]{:S(2)}) async-start(), calls=%async_computation.11 | async-start | bytes 1114112 | tf_op jit(solution)/shard_map/all_gather | solution.py:167
  8.7 142.8 %all-gather.17.cloned.1.call-start = ((), (), s32[]{:S(2)}) async-start(), calls=%async_computation.12 | async-start | bytes 1114112 | tf_op jit(solution)/shard_map/all_gather | solution.py:165
  9.4 249.1 %all-gather.29.cloned.1.call-start = ((), (), s32[]{:S(2)}) async-start(), calls=%async_computation.26 | async-start | bytes 2228224 | tf_op jit(solution)/shard_map/all_gather | solution.py:19
  18.8 86.5 %copy-start.40 = (f32[512]{0:T(512)}, f32[512]{0:T(512)S(1)}, u32[]{:S(2)}) copy-start(f32[512]{0:T(512)S(1)} %add_rsqrt_fusion.2) | copy-start | bytes 6148
  18.8 86.5 %copy-start.2 = (bf16[512,2048]{1,0:T(8,128)(2,1)S(1)}, bf16[512,2048]{1,0:T(8,128)(2,1)}, u32[]{:S(2)}) copy-start(bf16[512,2048]{1,0:T(8,128)(2,1)} %param.26) | copy-start | bytes 6291460
  18.8 86.5 %copy-start.29 = (f32[2048]{0:T(1024)S(1)}, f32[2048]{0:T(1024)}, u32[]{:S(2)}) copy-start(f32[2048]{0:T(1024)} %param.27) | copy-start | bytes 24580
  212.0 92.6 %all-gather.19.cloned.1.call-start = ((), (), s32[]{:S(2)}) async-start(), calls=%async_computation.13 | async-start | bytes 1114112 | tf_op jit(solution)/shard_map/all_gather | solution.py:168
  212.6 135.8 %all-gather.21.cloned.1.call-start = ((), (), s32[]{:S(2)}) async-start(), calls=%async_computation.14 | async-start | bytes 1114112 | tf_op jit(solution)/shard_map/all_gather | solution.py:171
  213.2 321.3 %all-reduce.5.cloned.1.call-start = ((), (), s32[]{:S(2)}) async-start(), calls=%async_computation.15 | async-start | bytes 8388608 | tf_op jit(solution)/shard_map/psum | solution.py:223
  261.4 91.0 %copy-start.30 = (f32[512,2]{0,1:T(2,128)}, f32[512,2]{0,1:T(2,128)S(1)}, u32[]{:S(2)}) copy-start(f32[512,2]{0,1:T(2,128)S(1)} %add_rsqrt_fusion) | copy-start | bytes 12292
  352.4 235.9 %all-gather.23.cloned.1.call-start = ((), (), s32[]{:S(2)}) async-start(), calls=%async_computation.16 | async-start | bytes 3063808 | tf_op jit(solution)/shard_map/all_gather | solution.py:172
  353.1 286.0 %all-gather.25.cloned.1.call-start = ((), (), s32[]{:S(2)}) async-start(), calls=%async_computation.17 | async-start | bytes 3063808 | tf_op jit(solution)/shard_map/all_gather | solution.py:173
  353.9 336.0 %all-gather.27.cloned.1.call-start = ((), (), s32[]{:S(2)}) async-start(), calls=%async_computation.18 | async-start | bytes 3063808 | tf_op jit(solution)/shard_map/all_gather | solution.py:174
  354.4 185.0 %copy-start.28 = (f32[2048]{0:T(1024)S(1)}, f32[2048]{0:T(1024)}, u32[]{:S(2)}) copy-start(f32[2048]{0:T(1024)} %param.36) | copy-start | bytes 24580
  354.5 449.4 %all-reduce.7.cloned.1.call-start = ((), (), s32[]{:S(2)}) async-start(), calls=%async_computation.20 | async-start | bytes 4194304 | tf_op jit(solution)/shard_map/psum | solution.py:267
  702.0 245.0 %all-gather.31.cloned.1.call-start = ((), (), s32[]{:S(2)}) async-start(), calls=%async_computation.27 | async-start | bytes 1114112 | tf_op jit(solution)/shard_map/all_gather | solution.py:33
  817.1 292.0 %reduce-scatter.31.cloned.1.call-start = ((), (), s32[]{:S(2)}) async-start(), calls=%async_computation.28 | async-start | bytes 1114112
  821.4 289.3 %reduce-scatter.29.cloned.1.call-start = ((), (), s32[]{:S(2)}) async-start(), calls=%async_computation.25 | async-start | bytes 1114112 | tf_op jit(solution)/shard_map/reduce_scatter | solution.py:334
  823.6 288.9 %reduce-scatter.19.cloned.1.call-start = ((), (), s32[]{:S(2)}) async-start(), calls=%async_computation.19 | async-start | bytes 2359296 | tf_op jit(solution)/shard_map/reduce_scatter | solution.py:231
  829.0 303.8 %reduce-scatter.33.cloned.1.call-start = ((), (), s32[]{:S(2)}) async-start(), calls=%async_computation.29 | async-start | bytes 3342336
  838.5 372.5 %reduce-scatter.35.cloned.1.call-start = ((), (), s32[]{:S(2)}) async-start(), calls=%async_computation.30 | async-start | bytes 3342336
  873.2 416.1 %reduce-scatter.37.cloned.1.call-start = ((), (), s32[]{:S(2)}) async-start(), calls=%async_computation.31 | async-start | bytes 3342336
  945.2 413.0 %reduce-scatter.23.cloned.1.call-start = ((), (), s32[]{:S(2)}) async-start(), calls=%async_computation.22 | async-start | bytes 1114112 | tf_op jit(solution)/shard_map/reduce_scatter | solution.py:316
  1088.9 339.4 %reduce-scatter.25.cloned.1.call-start = ((), (), s32[]{:S(2)}) async-start(), calls=%async_computation.23 | async-start | bytes 1114112 | tf_op jit(solution)/shard_map/reduce_scatter | solution.py:322
  1093.7 404.4 %reduce-scatter.27.cloned.1.call-start = ((), (), s32[]{:S(2)}) async-start(), calls=%async_computation.24 | async-start | bytes 1114112 | tf_op jit(solution)/shard_map/reduce_scatter | solution.py:328
  1096.1 457.7 %reduce-scatter.21.cloned.1.call-start = ((), (), s32[]{:S(2)}) async-start(), calls=%async_computation.21 | async-start | bytes 2359296 | tf_op jit(solution)/shard_map/reduce_scatter | solution.py:352
  1109.1 446.2 %copy-start.50 = (f32[128]{0:T(128)S(1)}, f32[128]{0:T(128)}, u32[]{:S(2)}) copy-start(f32[128]{0:T(128)} %get-tuple-element.763) | copy-start | bytes 1540
  1109.1 511.4 %copy-start.27 = (f32[24,256]{1,0:T(8,128)S(1)}, f32[24,256]{1,0:T(8,128)}, u32[]{:S(2)}) copy-start(f32[24,256]{1,0:T(8,128)} %param.32) | copy-start | bytes 73732
  1109.1 511.4 %copy-start.37 = (f32[256]{0:T(256)S(1)}, f32[256]{0:T(256)}, u32[]{:S(2)}) copy-start(f32[256]{0:T(256)} %copy-done.36) | copy-start | bytes 3076
  1109.1 511.4 %copy-start.39 = (f32[256]{0:T(256)S(1)}, f32[256]{0:T(256)}, u32[]{:S(2)}) copy-start(f32[256]{0:T(256)} %copy-done.38) | copy-start | bytes 3076
  1109.1 511.4 %copy-start.49 = (f32[24]{0:T(128)S(1)}, f32[24]{0:T(128)}, u32[]{:S(2)}) copy-start(f32[24]{0:T(128)} %copy-done.48) | copy-start | bytes 292
  (46 other events, 574.3 us)
Sparse Core Ops, SparseCore 0:
  10.5 48.5 all-gather.12
  61.6 43.6 all-gather.14
  107.7 43.6 all-gather.16
  212.2 46.3 all-gather.28
  260.8 43.7 all-gather.18
  306.8 41.5 all-gather.20
  352.5 182.0 all-reduce.4
  536.9 51.3 all-gather.22
  590.7 48.4 all-gather.24
  641.4 48.4 all-gather.26
  702.2 101.6 all-reduce.6
  817.2 44.8 all-gather.30
  865.8 63.5 reduce-scatter.30
  933.5 66.0 reduce-scatter.28
  1001.9 53.1 reduce-scatter.18
  1059.0 73.7 reduce-scatter.32
  1136.7 74.3 reduce-scatter.34
  1215.0 74.2 reduce-scatter.36
  1293.1 65.1 reduce-scatter.22
  1362.3 65.9 reduce-scatter.24
  1432.1 66.0 reduce-scatter.26
  1500.7 53.0 reduce-scatter.20
where the time goes:
time: 1650 us; the launch traced here: 1630 us
  waiting for transfers between devices  1070 us (65%)
  other arithmetic  148 us (9%)
  local copies, waits for them, and re-layouts  134 us (8%)
  matrix products  130 us (8%)
  blocking collectives  111 us (7%)
  between operations  18.4 us (1%)
  loops' own time  18.3 us (1%)
    psum x1, waiting for transfers between devices, local(): residual = inputs_float + lax.psum(branch_part, 'head')  180 us
    unnamed x26, waiting for transfers between devices  177 us
    psum x1, waiting for transfers between devices, local(): lax.psum(mid_part.astype(jnp.bfloat16), 'head').astype(jnp.float32)  101 us
    reduce_scatter x1, waiting for transfers between devices, local(): lax.psum_scatter(contract_first(normed_low, grad_forget_raw).astype(jnp.b...  68.6 us
    reduce_scatter x1, waiting for transfers between devices, local(): lax.psum_scatter(contract_first(normed_low, grad_input_raw).astype(jnp.bf...  68.3 us
    reduce_scatter x1, waiting for transfers between devices, local(): lax.psum_scatter(contract_first(normed_low, grad_query_raw).astype(jnp.bf...  67.1 us
    psum x1, blocking collectives, local(): lax.psum((jnp.sum(norm_terms, axis=0), jnp.sum(ffn_terms_rows, axis=0), b...  65.2 us
    reduce_scatter x1, waiting for transfers between devices, local(): lax.psum_scatter(partial_in.astype(jnp.bfloat16), 'head', scatter_dimensi...  54.1 us
  transfers between devices with their start and end apart: 22, of which 18 were waited for; matrix products, arithmetic and copies ran while one was open for 19% of the time, Pallas kernels for 0%

commit v1 on v0

v1 whole, which is shorter than its diff:
```python
from functools import partial

import jax
import jax.numpy as jnp
from jax import lax
from jax.experimental import pallas as pl
from jax.experimental.pallas import tpu as pltpu
from jax.sharding import PartitionSpec as P

D = 2048
KDIM = 128
CHUNK = 128
TOK = 512
CHUNKS = TOK // CHUNK
HERE = 256
FFH = 704
NSEQ = 12
NHEAD = 8
ROWS = TOK // NHEAD
EPS = 1e-06
F32 = jnp.float32
BF16 = jnp.bfloat16
MESH = pl.DeviceIdType.MESH
VM = pl.BlockSpec(memory_space=pltpu.VMEM)
SM = pl.BlockSpec(memory_space=pltpu.SMEM)
HB = pl.BlockSpec(memory_space=pl.ANY)


class Spot:
    def __init__(self):
        self.dp = lax.axis_index("dp")
        self.head = lax.axis_index("head")
        self.core = lax.rem(self.dp, 2)
        self.chip = lax.div(self.dp, 2)
        self.xh = lax.rem(self.chip, 2)
        self.z = lax.div(self.chip, 2)

    def at(self, dz, xh, core):
        return (lax.rem(self.z + dz, 4) * 2 + xh) * 2 + core

    @property
    def sibling(self):
        return {"dp": self.chip * 2 + 1 - self.core}

    def chips(self):
        return [{"dp": lax.rem(self.chip + k, 8) * 2 + self.core} for k in range(1, 8)]

    def heads(self):
        return [{"head": lax.rem(self.head + k, NHEAD)} for k in range(1, NHEAD)]


def greet(ids):
    barrier = pltpu.get_barrier_semaphore()
    for one in ids:
        pl.semaphore_signal(barrier, inc=1, device_id=one, device_id_type=MESH)
    pl.semaphore_wait(barrier, len(ids))


def rcopy(src, dst, send, recv, where):
    return pltpu.make_async_remote_copy(
        src_ref=src, dst_ref=dst, send_sem=send, recv_sem=recv, device_id=where, device_id_type=MESH
    )


GATHER_SENDS = 17


class Gather:
    def __init__(self, spot, g, send, recv, half):
        self.spot, self.g, self.s, self.r, self.h = spot, g, send, recv, half

    def block(self, d, start=0, rows=128):
        return self.g.at[pl.ds(pl.multiple_of(d * 128 + start, 64), rows), :]

    def push(self, d, to, k):
        rcopy(self.block(d), self.block(d), self.s.at[k], self.r.at[d], {"dp": to}).start()

    def push_half(self, d, to, k, xh, part):
        b = self.block(d, part * 64, 64)
        rcopy(b, b, self.s.at[k], self.h.at[2 * xh + part], {"dp": to}).start()

    def arrived(self, d):
        b = self.block(d)
        rcopy(b, b, self.s.at[0], self.r.at[d], self.spot.sibling).wait_recv()

    def arrived_halves(self, d, xh):
        for part in range(2):
            b = self.block(d, part * 64, 64)
            rcopy(b, b, self.s.at[0], self.h.at[2 * xh + part], self.spot.sibling).wait_recv()

    def first(self):
        p = self.spot
        self.push(p.dp, p.at(0, 1 - p.xh, p.core), 0)
        self.push(p.dp, p.at(1, p.xh, p.core), 1)
        self.push(p.dp, p.at(3, p.xh, p.core), 2)
        self.push(p.dp, p.at(0, p.xh, 1 - p.core), 3)

    def second(self):
        p = self.spot
        b = p.at(0, 1 - p.xh, p.core)
        self.arrived(b)
        self.push(b, p.at(1, p.xh, p.core), 4)
        self.push(b, p.at(3, p.xh, p.core), 5)
        self.push(b, p.at(0, p.xh, 1 - p.core), 6)

    def third(self):
        p = self.spot
        for i, h in enumerate((p.xh, 1 - p.xh)):
            b = p.at(3, h, p.core)
            self.arrived(b)
            self.push_half(b, p.at(1, p.xh, p.core), 7 + i, h, 0)
            self.push(b, p.at(0, p.xh, 1 - p.core), 9 + i)
            b = p.at(1, h, p.core)
            self.arrived(b)
            self.push_half(b, p.at(3, p.xh, p.core), 11 + i, h, 1)
            self.push(b, p.at(0, p.xh, 1 - p.core), 13 + i)

    def fourth(self):
        p = self.spot
        for i, h in enumerate((p.xh, 1 - p.xh)):
            b = p.at(2, h, p.core)
            self.arrived_halves(b, h)
            self.push(b, p.at(0, p.xh, 1 - p.core), 15 + i)

    def last(self):
        p = self.spot
        for dz in range(4):
            for h in range(2):
                self.arrived(p.at(dz, h, 1 - p.core))
        half = self.block(0, 0, 64)
        for k in range(GATHER_SENDS):
            b = half if k in (7, 8, 11, 12) else self.block(0)
            rcopy(b, b, self.s.at[k], self.r.at[0], p.sibling).wait_send()


def gather_semaphores():
    return [
        pltpu.SemaphoreType.DMA((GATHER_SENDS,)),
        pltpu.SemaphoreType.DMA((16,)),
        pltpu.SemaphoreType.DMA((4,)),
    ]


NN = (((1,), (0,)), ((), ()))
NT = (((1,), (1,)), ((), ()))
TN = (((0,), (0,)), ((), ()))


def mm(a, b, dims):
    return lax.dot_general(a, b, dims, preferred_element_type=F32)


def halves(a):
    high = a.astype(BF16)
    return high, (a - high.astype(F32)).astype(BF16)


def mm2(a, b, dims):
    return mm(a[0], b, dims) + mm(a[1], b, dims)


def mm3(a, b, dims):
    return mm(a[0], b[0], dims) + (mm(a[0], b[1], dims) + mm(a[1], b[0], dims))


def triangle(lower):
    rows = lax.broadcasted_iota(jnp.int32, (CHUNK, CHUNK), 0)
    columns = lax.broadcasted_iota(jnp.int32, (CHUNK, CHUNK), 1)
    return (rows >= columns if lower else rows <= columns).astype(BF16)


def summed_rows(lower, x):
    high = x.astype(BF16)
    rest = x - high.astype(F32)
    middle = rest.astype(BF16)
    low = (rest - middle.astype(F32)).astype(BF16)
    t = triangle(lower)
    return mm(t, high, NN) + (mm(t, middle, NN) + mm(t, low, NN))


class Segments:
    def __init__(self, spot, seq):
        self.starts = []
        total = jnp.int32(0)
        for i in range(NSEQ):
            self.starts.append(total)
            total = total + seq[i]
        self.first = spot.dp * TOK

    def of(self, position):
        found = jnp.where(position >= self.starts[0], 1, 0)
        for s in self.starts[1:]:
            found = found + jnp.where(position >= s, 1, 0)
        return found - 1

    def column(self, c):
        return self.of(self.first + c * CHUNK + lax.broadcasted_iota(jnp.int32, (CHUNK, KDIM), 0))

    def row(self, c):
        return self.of(self.first + c * CHUNK + lax.broadcasted_iota(jnp.int32, (CHUNK, KDIM), 1))

    def before(self, c):
        return self.of(self.first + c * CHUNK - 1)

    def final(self, c):
        return self.of(self.first + (c + 1) * CHUNK - 1)


def lower_bound(lb, layer):
    x = lb[...]
    e = jnp.exp(x - jnp.max(x, axis=0, keepdims=True))
    soft = e / jnp.sum(e, axis=0, keepdims=True)
    depth = lax.broadcasted_iota(jnp.int32, x.shape, 0)
    picked = jnp.where((depth >= 1) & (depth <= layer), 1.0, 0.0)
    return soft, picked, jnp.sum(soft * picked, axis=0, keepdims=True)


def sigmoid(x):
    return lax.logistic(x)


def slope(x, s):
    return s * (1.0 + x * (1.0 - s))


class Exchange:
    def __init__(self, spot, msg, sib, slots, give, take, send, recv, backward):
        self.p, self.msg, self.sib, self.slots = spot, msg, sib, slots
        self.give, self.take, self.s, self.r, self.back = give, take, send, recv, backward

    def to_sibling(self):
        p = self.p
        rcopy(self.msg.at[1 - p.core], self.sib, self.s.at[7], self.r.at[8], p.sibling).start()

    def to_chips(self):
        p = self.p
        rcopy(self.sib, self.sib, self.s.at[7], self.r.at[8], p.sibling).wait_recv()
        mine, other = self.msg[p.core], self.sib[...]
        zero = p.core == 0
        one, two = jnp.where(zero, mine, other), jnp.where(zero, other, mine)
        near, far = (two, one) if self.back else (one, two)
        self.near = near
        state = near[0:128] * far[128:129] + far[0:128]
        self.slots[p.chip, 0:128, :] = state
        self.slots[p.chip, 128:136, :] = near[128:136] * far[128:136]
        for k, to in enumerate(p.chips()):
            rcopy(self.slots.at[p.chip], self.slots.at[p.chip], self.s.at[k], self.r.at[p.chip], to).start()

    def result(self, out):
        p = self.p
        for k in range(1, 8):
            chip = lax.rem(p.chip + k, 8)
            rcopy(self.slots.at[chip], self.slots.at[chip], self.s.at[0], self.r.at[chip], p.sibling).wait_recv()
        state = jnp.zeros((128, 128), F32)
        for k in range(7, 0, -1) if self.back else range(7):
            m = self.slots[k]
            after = state * m[128:129] + m[0:128]
            state = jnp.where(k > p.chip if self.back else k < p.chip, after, state)
        second = state * self.near[128:129] + self.near[0:128]
        is_first = p.core == (1 if self.back else 0)
        self.give[...] = jnp.where(is_first, second, state)
        move = rcopy(self.give, self.take, self.s.at[8], self.r.at[9], p.sibling)
        move.start()
        out[p.core] = jnp.where(is_first, state, second)
        move.wait_recv()
        out[1 - p.core] = self.take[...]

    def finish(self):
        p = self.p
        for k in range(7):
            rcopy(self.slots.at[0], self.slots.at[0], self.s.at[k], self.r.at[0], p.sibling).wait_send()
        rcopy(self.sib, self.sib, self.s.at[7], self.r.at[8], p.sibling).wait_send()
        rcopy(self.give, self.take, self.s.at[8], self.r.at[9], p.sibling).wait_send()


def exchange_scratch():
    return [
        pltpu.VMEM((2, 136, 128), F32),
        pltpu.VMEM((136, 128), F32),
        pltpu.VMEM((8, 136, 128), F32),
        pltpu.VMEM((128, 128), F32),
        pltpu.VMEM((128, 128), F32),
        pltpu.SemaphoreType.DMA((9,)),
        pltpu.SemaphoreType.DMA((10,)),
    ]


def gates(raw, bound, rows):
    query_raw = raw[rows, 0:256]
    logistic = sigmoid(raw[rows, 256:512])
    forget = bound + (1.0 - bound) * logistic
    query = (query_raw * sigmoid(query_raw)).astype(BF16)
    keys = (1.0 - forget).astype(BF16)
    values = raw[rows, 512:768].astype(BF16)
    return logistic, forget, query, keys, values


def mixer_forward(
    hid, gain, wq, wf, wi, wo, wt, lb, layer, seq, group_gain,
    raw, xn, gated, mixed, states, run, total, w_out, wt_out,
    w, wt_all, inner_update, decay, incoming,
    msg, sib, slots, give, take, ex_send, ex_recv,
    gs, gr, gh, hs, hr, hh, local_sem,
):
    p = Spot()
    greet(p.chips() + [p.sibling])
    mine = pl.ds(pl.multiple_of(p.dp * 128, 128), 128)
    for k, one in enumerate((wq, wf, wi, wo)):
        w[mine, 256 * k : 256 * (k + 1)] = one[...]
    gather = Gather(p, w, gs, gr, gh)
    gather.first()
    wt_all[mine, :] = wt[...]
    later = Gather(p, wt_all, hs, hr, hh)

    @pl.loop(0, 8)
    def _(i):
        rows = pl.ds(pl.multiple_of(i * 64, 64), 64)
        x = hid[rows, :].astype(F32)
        scale = lax.rsqrt(jnp.mean(x * x, axis=-1, keepdims=True) + EPS)
        xn[rows, :] = (x * scale * gain[...]).astype(BF16)

    gather.second()
    gather.third()
    gather.fourth()
    later.first()
    gather.last()
    keep = pltpu.make_async_copy(w, w_out, local_sem.at[0])
    keep.start()

    @pl.loop(0, 4)
    def _(j):
        columns = pl.ds(pl.multiple_of(j * 256, 256), 256)
        raw[:, columns] = mm(xn[...], w[:, columns], NN)

    later.second()
    segments = Segments(p, seq)
    bound = lower_bound(lb, layer[0])[2]
    forget_total = jnp.zeros((1, HERE), F32)
    for c in range(CHUNKS):
        rows = slice(c * CHUNK, (c + 1) * CHUNK)
        logistic, forget, query, keys, values = gates(raw, bound, rows)
        forget_total = forget_total + jnp.sum(forget, axis=0, keepdims=True)
        running = summed_rows(True, jnp.log(forget))
        run[rows, :] = running
        middle, ending = running[63:64], running[127:128]
        lifted = query.astype(F32) * jnp.exp(running - middle)
        lowered = keys.astype(F32) * jnp.exp(middle - running)
        tail = keys.astype(F32) * jnp.exp(ending - running)
        column, row = segments.column(c), segments.row(c)
        linked = (column == row) & (
            lax.broadcasted_iota(jnp.int32, (CHUNK, CHUNK), 0)
            >= lax.broadcasted_iota(jnp.int32, (CHUNK, CHUNK), 1)
        )
        final = segments.final(c)
        carried_last = jnp.where(final == segments.before(c), 1.0, 0.0)
        decay[c : c + 1, :] = jnp.exp(ending) * carried_last
        ends = jnp.where(column == final, 1.0, 0.0)
        for h in range(2):
            lanes = slice(h * 128, (h + 1) * 128)
            scores = mm3(halves(lifted[:, lanes]), halves(lowered[:, lanes]), NT)
            scores = jnp.where(linked, scores, 0.0)
            mixed[rows, lanes] = mm2(halves(scores), values[:, lanes], NN)
            high, low = halves(tail[:, lanes] * ends)
            inner_update[h, c] = mm(values[:, lanes], high, TN) + mm(values[:, lanes], low, TN)
    total[...] = forget_total
    for h in range(2):
        lanes = slice(h * 128, (h + 1) * 128)
        state, rate = inner_update[h, 0], decay[0:1, lanes]
        for c in range(1, CHUNKS):
            state = state * decay[c : c + 1, lanes] + inner_update[h, c]
            rate = rate * decay[c : c + 1, lanes]
        msg[h, 0:128, :] = state
        msg[h, 128:136, :] = jnp.broadcast_to(rate, (8, 128))
    exchange = Exchange(p, msg, sib, slots, give, take, ex_send, ex_recv, False)
    exchange.to_sibling()
    exchange.to_chips()
    later.third()
    later.fourth()
    exchange.result(incoming)
    for h in range(2):
        lanes = slice(h * 128, (h + 1) * 128)
        state = incoming[h]
        states[h, 0] = state
        for c in range(CHUNKS):
            state = state * decay[c : c + 1, lanes] + inner_update[h, c]
            states[h, c + 1] = state

    @pl.loop(0, CHUNKS)
    def _(c):
        rows = pl.ds(pl.multiple_of(c * CHUNK, CHUNK), CHUNK)
        carried = jnp.where(segments.column(c) == segments.before(c), 1.0, 0.0)
        for h in range(2):
            lanes = slice(h * 128, (h + 1) * 128)
            query_raw = raw[rows, h * 128 : (h + 1) * 128]
            query = (query_raw * sigmoid(query_raw)).astype(BF16).astype(F32)
            reach = query * jnp.exp(run[rows, lanes]) * carried
            x = mixed[rows, lanes] + mm3(halves(reach), halves(states[h, c]), NT)
            mixed[rows, lanes] = x
            scale = lax.rsqrt(jnp.mean(x * x, axis=-1, keepdims=True) + EPS)
            gate = raw[rows, 768 + h * 128 : 768 + (h + 1) * 128]
            gated[rows, lanes] = (x * scale * group_gain[...] * (gate * sigmoid(gate))).astype(BF16)

    later.last()
    keep_later = pltpu.make_async_copy(wt_all, wt_out, local_sem.at[1])
    keep_later.start()
    exchange.finish()
    keep.wait()
    keep_later.wait()


def call_mixer_forward(hid, gain, wq, wf, wi, wo, wt, lb, layer, seq, group_gain):
    out = jax.ShapeDtypeStruct
    return pl.pallas_call(
        mixer_forward,
        name="mixer_forward",
        out_shape=(
            out((TOK, 1024), F32),
            out((TOK, D), BF16),
            out((TOK, HERE), BF16),
            out((TOK, HERE), F32),
            out((2, CHUNKS + 1, 128, 128), F32),
            out((TOK, HERE), F32),
            out((1, HERE), F32),
            out((D, 1024), BF16),
            out((D, HERE), BF16),
        ),
        in_specs=[VM] * 8 + [SM, SM, VM],
        out_specs=(VM,) * 7 + (HB, HB),
        scratch_shapes=[
            pltpu.VMEM((D, 1024), BF16),
            pltpu.VMEM((D, HERE), BF16),
            pltpu.VMEM((2, CHUNKS, 128, 128), F32),
            pltpu.VMEM((8, HERE), F32),
            pltpu.VMEM((2, 128, 128), F32),
            *exchange_scratch(),
            *gather_semaphores(),
            *gather_semaphores(),
            pltpu.SemaphoreType.DMA((2,)),
        ],
        compiler_params=pltpu.CompilerParams(
            collective_id=0, has_side_effects=True, vmem_limit_bytes=56 * 1024 * 1024
        ),
    )(hid, gain, wq, wf, wi, wo, wt, lb, layer, seq, group_gain)

class HeadSum:
    def __init__(self, spot, ps, slots, send, recv):
        self.p, self.ps, self.slots, self.s, self.r = spot, ps, slots, send, recv

    def send(self):
        p = self.p
        for k in range(1, NHEAD):
            h = lax.rem(p.head + k, NHEAD)
            rcopy(self.ps.at[h], self.slots.at[p.head], self.s.at[k], self.r.at[p.head], {"head": h}).start()

    def collect(self):
        p = self.p
        self.slots[p.head] = self.ps[p.head]
        for k in range(1, NHEAD):
            h = lax.rem(p.head + k, NHEAD)
            rcopy(self.slots.at[h], self.slots.at[h], self.s.at[0], self.r.at[h], p.sibling).wait_recv()

    def rows(self, rows):
        total = self.slots[0, rows, :].astype(F32)
        for h in range(1, NHEAD):
            total = total + self.slots[h, rows, :].astype(F32)
        return total

    def finish(self):
        for k in range(1, NHEAD):
            rcopy(self.ps.at[0], self.slots.at[0], self.s.at[k], self.r.at[0], self.p.sibling).wait_send()


class HeadGather:
    def __init__(self, spot, full, send, recv):
        self.p, self.full, self.s, self.r = spot, full, send, recv

    def block(self, h):
        return self.full.at[pl.ds(pl.multiple_of(h * ROWS, ROWS), ROWS), :]

    def send(self):
        p = self.p
        for k in range(1, NHEAD):
            h = lax.rem(p.head + k, NHEAD)
            rcopy(self.block(p.head), self.block(p.head), self.s.at[k], self.r.at[p.head], {"head": h}).start()

    def collect(self):
        p = self.p
        for k in range(1, NHEAD):
            h = lax.rem(p.head + k, NHEAD)
            rcopy(self.block(h), self.block(h), self.s.at[0], self.r.at[h], p.sibling).wait_recv()

    def finish(self):
        for k in range(1, NHEAD):
            rcopy(self.block(0), self.block(0), self.s.at[k], self.r.at[0], self.p.sibling).wait_send()


def eight():
    return [pltpu.SemaphoreType.DMA((8,)), pltpu.SemaphoreType.DMA((8,))]


def branch(
    gated, wt, hid, gain, wg, wu, wd,
    hn_out, resid, wg_out, wu_out, wd_out,
    ps, slots, hn, g0, g1, g2, rs_s, rs_r, ag_s, ag_r,
    s0, r0, h0, s1, r1, h1, s2, r2, h2, local_sem,
):
    p = Spot()
    greet(p.chips() + [p.sibling] + p.heads())
    mine = pl.ds(pl.multiple_of(p.dp * 128, 128), 128)
    gathers = [Gather(p, g0, s0, r0, h0), Gather(p, g1, s1, r1, h1), Gather(p, g2, s2, r2, h2)]
    for one, full in zip((wg, wu, wd), (g0, g1, g2)):
        full[mine, :] = one[...]
    for g in gathers:
        g.first()

    @pl.loop(0, 8)
    def _(j):
        columns = pl.ds(pl.multiple_of(j * 256, 256), 256)
        part = mm(gated[...], wt[columns, :], NT).astype(BF16)
        for h in range(NHEAD):
            ps[h, :, columns] = part[h * ROWS : (h + 1) * ROWS]

    scatter = HeadSum(p, ps, slots, rs_s, rs_r)
    scatter.send()
    for g in gathers:
        g.second()
    for g in gathers:
        g.third()
    scatter.collect()
    own = pl.multiple_of(p.head * ROWS, ROWS)

    @pl.loop(0, 4)
    def _(i):
        rows = pl.ds(pl.multiple_of(i * 16, 16), 16)
        here = pl.ds(pl.multiple_of(own + i * 16, 16), 16)
        x = hid[here, :].astype(F32) + scatter.rows(rows)
        resid[rows, :] = x
        scale = lax.rsqrt(jnp.mean(x * x, axis=-1, keepdims=True) + EPS)
        hn[here, :] = (x * scale * gain[...]).astype(BF16)

    spread = HeadGather(p, hn, ag_s, ag_r)
    spread.send()
    for g in gathers:
        g.fourth()
    outs = []
    for k, (g, full, out) in enumerate(zip(gathers, (g0, g1, g2), (wg_out, wu_out, wd_out))):
        g.last()
        move = pltpu.make_async_copy(full, out, local_sem.at[k])
        move.start()
        outs.append(move)
    spread.collect()
    move = pltpu.make_async_copy(hn, hn_out, local_sem.at[3])
    move.start()
    outs.append(move)
    scatter.finish()
    spread.finish()
    for move in outs:
        move.wait()


def call_branch(gated, wt, hid, gain, wg, wu, wd):
    out = jax.ShapeDtypeStruct
    return pl.pallas_call(
        branch,
        name="branch",
        out_shape=(
            out((TOK, D), BF16),
            out((ROWS, D), F32),
            out((D, FFH), BF16),
            out((D, FFH), BF16),
            out((D, FFH), BF16),
        ),
        in_specs=[VM] * 7,
        out_specs=(HB, VM, HB, HB, HB),
        scratch_shapes=[
            pltpu.VMEM((NHEAD, ROWS, D), BF16),
            pltpu.VMEM((NHEAD, ROWS, D), BF16),
            pltpu.VMEM((TOK, D), BF16),
            *[pltpu.VMEM((D, FFH), BF16)] * 3,
            *eight(),
            *eight(),
            *gather_semaphores(),
            *gather_semaphores(),
            *gather_semaphores(),
            pltpu.SemaphoreType.DMA((4,)),
        ],
        compiler_params=pltpu.CompilerParams(
            collective_id=1, has_side_effects=True, vmem_limit_bytes=56 * 1024 * 1024
        ),
    )(gated, wt, hid, gain, wg, wu, wd)


class DpSum:
    def __init__(self, spot, gs, cr, zr, xs, xr, send, recv):
        self.p, self.gs, self.cr, self.zr, self.xs, self.xr = spot, gs, cr, zr, xs, xr
        self.s, self.r = send, recv

    def pair(self, i):
        p = self.p
        two = pl.ds(2 * i, 2)
        return rcopy(self.gs.at[1 - p.core, two], self.cr.at[two], self.s.at[i], self.r.at[i], p.sibling)

    def to_sibling(self):
        for i in range(4):
            self.pair(i).start()

    def across(self, d):
        p = self.p
        z = lax.rem(p.z + d, 4)
        where = {"dp": (z * 2 + p.xh) * 2 + p.core}
        return rcopy(self.gs.at[p.core, pl.ds(z * 2, 2)], self.zr.at[d - 1], self.s.at[3 + d], self.r.at[3 + d], where)

    def to_z(self):
        p = self.p
        for i in range(4):
            self.pair(i).wait_recv()

        @pl.loop(0, 8)
        def _(k):
            self.gs[p.core, k] = (self.gs[p.core, k].astype(F32) + self.cr[k].astype(F32)).astype(BF16)

        for d in (1, 3, 2):
            self.across(d).start()

    def last_move(self):
        p = self.p
        where = {"dp": (p.z * 2 + 1 - p.xh) * 2 + p.core}
        return rcopy(self.xs, self.xr, self.s.at[7], self.r.at[7], where)

    def to_x(self, put):
        p = self.p
        for d in (1, 3, 2):
            self.across(d).wait_recv()

        def total(h):
            one = self.gs[p.core, 2 * p.z + h].astype(F32)
            for i in range(3):
                one = one + self.zr[i, h].astype(F32)
            return one

        self.xs[...] = total(1 - p.xh).astype(BF16)
        self.last_move().start()
        put(total(p.xh))

    def end(self, add):
        self.last_move().wait_recv()
        add(self.xr[...].astype(F32))

    def finish(self):
        for i in range(4):
            self.pair(i).wait_send()
        for d in (1, 3, 2):
            self.across(d).wait_send()
        self.last_move().wait_send()


def dp_sum_scratch(n):
    return [
        pltpu.VMEM((2, 8, 128, n), BF16),
        pltpu.VMEM((8, 128, n), BF16),
        pltpu.VMEM((3, 2, 128, n), BF16),
        pltpu.VMEM((128, n), BF16),
        pltpu.VMEM((128, n), BF16),
        *eight(),
    ]


def outer_products(left, right, gs):
    @pl.loop(0, 8)
    def _(k):
        columns = pl.ds(pl.multiple_of(k * 256, 256), 256)
        both = mm(left[:, columns], right[...], TN).astype(BF16)
        gs[0, k] = both[0:128]
        gs[1, k] = both[128:256]


def write(ref):
    def put(x):
        ref[...] = x

    return put


def accumulate(ref):
    def add(x):
        ref[...] += x

    return add


def feed_forward(
    hn, dy, wg_in, wu_in, wd_in, resid, gain,
    down, d_resid, db_out, gain_terms, out_gate, out_up, out_down,
    wg, wu, wd, hidden, dg, du, ps, slots, db, rs_s, rs_r, ag_s, ag_r,
    a0, a1, a2, a3, a4, a5, a6, b0, b1, b2, b3, b4, b5, b6, c0, c1, c2, c3, c4, c5, c6, local_sem,
):
    loads = []
    for k, (one, full) in enumerate(((wg_in, wg), (wu_in, wu), (wd_in, wd))):
        move = pltpu.make_async_copy(one, full, local_sem.at[k])
        move.start()
        loads.append(move)
    p = Spot()
    partners = [{"dp": p.at(k, p.xh, p.core)} for k in (1, 2, 3)]
    partners += [{"dp": p.at(0, 1 - p.xh, p.core)}, p.sibling]
    greet(partners + p.heads())
    for move in loads:
        move.wait()
    for low, high in ((0, 256), (256, 512), (512, FFH)):
        gate = mm(hn[...], wg[:, low:high], NN)
        up = mm(hn[...], wu[:, low:high], NN)
        dh = mm(dy[...], wd[:, low:high], NN)
        s = sigmoid(gate)
        silu = gate * s
        hidden[:, low:high] = (silu * up).astype(BF16)
        dg[:, low:high] = (dh * up * slope(gate, s)).astype(BF16)
        du[:, low:high] = (dh * silu).astype(BF16)

    @pl.loop(0, 8)
    def _(j):
        columns = pl.ds(pl.multiple_of(j * 256, 256), 256)
        part = (mm(dg[...], wg[columns, :], NT) + mm(du[...], wu[columns, :], NT)).astype(BF16)
        for h in range(NHEAD):
            ps[h, :, columns] = part[h * ROWS : (h + 1) * ROWS]

    scatter = HeadSum(p, ps, slots, rs_s, rs_r)
    scatter.send()
    sums = [
        DpSum(p, a0, a1, a2, a3, a4, a5, a6),
        DpSum(p, b0, b1, b2, b3, b4, b5, b6),
        DpSum(p, c0, c1, c2, c3, c4, c5, c6),
    ]
    outer_products(hn, dg, a0)
    sums[0].to_sibling()
    outer_products(hn, du, b0)
    sums[0].to_z()
    sums[1].to_sibling()
    outer_products(dy, hidden, c0)
    sums[1].to_z()
    sums[2].to_sibling()

    @pl.loop(0, 8)
    def _(j):
        columns = pl.ds(pl.multiple_of(j * 256, 256), 256)
        part = mm(hidden[...], wd[columns, :], NT).astype(BF16)
        for h in range(NHEAD):
            down[h, :, columns] = part[h * ROWS : (h + 1) * ROWS]

    sums[2].to_z()
    scatter.collect()
    own = pl.multiple_of(p.head * ROWS, ROWS)
    gain_terms[...] = jnp.zeros_like(gain_terms)

    @pl.loop(0, 4)
    def _(i):
        rows = pl.ds(pl.multiple_of(i * 16, 16), 16)
        here = pl.ds(pl.multiple_of(own + i * 16, 16), 16)
        grad, x = scatter.rows(rows), resid[rows, :]
        inverse = lax.rsqrt(jnp.mean(x * x, axis=-1, keepdims=True) + EPS)
        scaled, normed = grad * gain[...], x * inverse
        back = inverse * (scaled - normed * jnp.mean(scaled * normed, axis=-1, keepdims=True))
        gain_terms[...] += jnp.sum(grad * normed, axis=0, keepdims=True)
        both = dy[here, :].astype(F32) + back
        d_resid[rows, :] = both
        db[here, :] = both.astype(BF16)

    spread = HeadGather(p, db, ag_s, ag_r)
    spread.send()
    results = (out_gate, out_up, out_down)
    for one, out in zip(sums, results):
        one.to_x(write(out))
    for one, out in zip(sums, results):
        one.end(accumulate(out))
    spread.collect()
    move = pltpu.make_async_copy(db, db_out, local_sem.at[0])
    move.start()
    scatter.finish()
    spread.finish()
    for one in sums:
        one.finish()
    move.wait()


def call_feed_forward(hn, dy, wg, wu, wd, resid, gain):
    out = jax.ShapeDtypeStruct
    return pl.pallas_call(
        feed_forward,
        name="feed_forward",
        out_shape=(
            out((NHEAD, ROWS, D), BF16),
            out((ROWS, D), F32),
            out((TOK, D), BF16),
            out((1, D), F32),
            out((128, FFH), F32),
            out((128, FFH), F32),
            out((128, FFH), F32),
        ),
        in_specs=[VM, VM, HB, HB, HB, VM, VM],
        out_specs=(VM, VM, HB, VM, VM, VM, VM),
        scratch_shapes=[
            *[pltpu.VMEM((D, FFH), BF16)] * 3,
            *[pltpu.VMEM((TOK, FFH), BF16)] * 3,
            pltpu.VMEM((NHEAD, ROWS, D), BF16),
            pltpu.VMEM((NHEAD, ROWS, D), BF16),
            pltpu.VMEM((TOK, D), BF16),
            *eight(),
            *eight(),
            *dp_sum_scratch(FFH),
            *dp_sum_scratch(FFH),
            *dp_sum_scratch(FFH),
            pltpu.SemaphoreType.DMA((3,)),
        ],
        compiler_params=pltpu.CompilerParams(
            collective_id=2, has_side_effects=True, vmem_limit_bytes=60 * 1024 * 1024
        ),
    )(hn, dy, wg, wu, wd, resid, gain)


VEC = 40


class Total:
    def __init__(self, spot, vec, h_slots, c_slots, own, other, h_s, h_r, c_s, c_r, k_s, k_r):
        self.p, self.vec, self.hs, self.cs, self.own, self.other = spot, vec, h_slots, c_slots, own, other
        self.h_s, self.h_r, self.c_s, self.c_r, self.k_s, self.k_r = h_s, h_r, c_s, c_r, k_s, k_r

    def send(self):
        p = self.p
        self.hs[p.head] = self.vec[...]
        for k in range(1, NHEAD):
            h = lax.rem(p.head + k, NHEAD)
            rcopy(self.hs.at[p.head], self.hs.at[p.head], self.h_s.at[k], self.h_r.at[p.head], {"head": h}).start()

    def middle(self):
        p = self.p
        for k in range(1, NHEAD):
            h = lax.rem(p.head + k, NHEAD)
            rcopy(self.hs.at[h], self.hs.at[h], self.h_s.at[0], self.h_r.at[h], p.sibling).wait_recv()
        total = self.hs[0]
        for h in range(1, NHEAD):
            total = total + self.hs[h]
        per_head = lax.broadcasted_iota(jnp.int32, (VEC, 128), 0) >= 34
        self.cs[p.chip] = jnp.where(per_head, self.vec[...], total)
        for k, to in enumerate(p.chips()):
            rcopy(self.cs.at[p.chip], self.cs.at[p.chip], self.c_s.at[k], self.c_r.at[p.chip], to).start()

    def result(self):
        p = self.p
        for k in range(1, 8):
            chip = lax.rem(p.chip + k, 8)
            rcopy(self.cs.at[chip], self.cs.at[chip], self.c_s.at[0], self.c_r.at[chip], p.sibling).wait_recv()
        total = self.cs[0]
        for k in range(1, 8):
            total = total + self.cs[k]
        self.own[...] = total
        move = rcopy(self.own, self.other, self.k_s, self.k_r, p.sibling)
        move.start()
        move.wait_recv()
        return total + self.other[...]

    def finish(self):
        p = self.p
        for k in range(1, NHEAD):
            rcopy(self.hs.at[0], self.hs.at[0], self.h_s.at[k], self.h_r.at[0], p.sibling).wait_send()
        for k in range(7):
            rcopy(self.cs.at[0], self.cs.at[0], self.c_s.at[k], self.c_r.at[0], p.sibling).wait_send()
        rcopy(self.own, self.other, self.k_s, self.k_r, p.sibling).wait_send()


def mixer_backward(
    db, wt, raw, run, mixed, states, gated, xn, w_in, d_resid, hid, down, resid, ffn_terms, total,
    gain, group_gain, lb, layer, seq,
    block_out, grad_in, out_query, out_forget, out_input, out_outgate, out_output, out_bounds,
    out_norm, out_group, out_ffn, out_mean,
    w, draw, d_mixed, d_query, d_keys, d_values, back_update, decay, incoming, ps, slots, slots2, vec,
    msg, sib, slots3, give, take, ex_send, ex_recv, rs_s, rs_r, rs2_s, rs2_r,
    a0, a1, a2, a3, a4, a5, a6, b0, b1, b2, b3, b4, b5, b6, c0, c1, c2, c3, c4, c5, c6,
    t0, t1, t2, t3, t4, t5, t6, t7, t8, t9, result_a, result_b, group_total, bound_total, local_sem,
):
    load = pltpu.make_async_copy(w_in, w, local_sem.at[0])
    load.start()
    p = Spot()
    greet(p.chips() + [p.sibling] + p.heads())
    scatter = HeadSum(p, down, slots, rs_s, rs_r)
    scatter.send()
    segments = Segments(p, seq)
    soft, picked, bound = lower_bound(lb, layer[0])
    group_total[...] = jnp.zeros_like(group_total)

    @pl.loop(0, CHUNKS)
    def _(c):
        rows = pl.ds(pl.multiple_of(c * CHUNK, CHUNK), CHUNK)
        d_gated = mm(db[rows, :], wt[...], NN)
        before, final = segments.before(c), segments.final(c)
        carried = jnp.where(segments.column(c) == before, 1.0, 0.0)
        running = run[rows, :]
        rate = jnp.exp(running[127:128]) * jnp.where(final == before, 1.0, 0.0)
        decay[c] = jnp.broadcast_to(rate, (8, HERE))
        for h in range(2):
            lanes = slice(h * 128, (h + 1) * 128)
            x, grad = mixed[rows, lanes], d_gated[:, lanes]
            gate = raw[rows, 768 + h * 128 : 768 + (h + 1) * 128]
            s = sigmoid(gate)
            inverse = lax.rsqrt(jnp.mean(x * x, axis=-1, keepdims=True) + EPS)
            normed = x * inverse
            draw[rows, 768 + h * 128 : 768 + (h + 1) * 128] = (
                grad * (normed * group_gain[...]) * slope(gate, s)
            ).astype(BF16)
            inner = grad * (gate * s)
            scaled = inner * group_gain[...]
            back = inverse * (scaled - normed * jnp.mean(scaled * normed, axis=-1, keepdims=True))
            group_total[...] += jnp.sum(inner * normed, axis=0, keepdims=True)
            back = back.astype(BF16)
            d_mixed[rows, lanes] = back
            query_raw = raw[rows, lanes]
            query = (query_raw * sigmoid(query_raw)).astype(BF16).astype(F32)
            high, low = halves(query * jnp.exp(running[:, lanes]) * carried)
            back_update[h, c] = mm(back, high, TN) + mm(back, low, TN)

    for h in range(2):
        lanes = slice(h * 128, (h + 1) * 128)
        state, rate = back_update[h, CHUNKS - 1], decay[CHUNKS - 1, 0:1, lanes]
        for c in range(CHUNKS - 2, -1, -1):
            state = state * decay[c, 0:1, lanes] + back_update[h, c]
            rate = rate * decay[c, 0:1, lanes]
        msg[h, 0:128, :] = state
        msg[h, 128:136, :] = jnp.broadcast_to(rate, (8, 128))
    exchange = Exchange(p, msg, sib, slots3, give, take, ex_send, ex_recv, True)
    exchange.to_sibling()
    exchange.to_chips()

    @pl.loop(0, CHUNKS)
    def _(c):
        rows = pl.ds(pl.multiple_of(c * CHUNK, CHUNK), CHUNK)
        running = run[rows, :]
        middle = running[63:64]
        _, _, query, keys, values = gates(raw, bound, rows)
        up, down_ = jnp.exp(running - middle), jnp.exp(middle - running)
        lifted = query.astype(F32) * up
        lowered = keys.astype(F32) * down_
        column, row = segments.column(c), segments.row(c)
        carried = jnp.where(column == segments.before(c), 1.0, 0.0)
        linked = (column == row) & (
            lax.broadcasted_iota(jnp.int32, (CHUNK, CHUNK), 0)
            >= lax.broadcasted_iota(jnp.int32, (CHUNK, CHUNK), 1)
        )
        for h in range(2):
            lanes = slice(h * 128, (h + 1) * 128)
            lift, lower = halves(lifted[:, lanes]), halves(lowered[:, lanes])
            scores = halves(jnp.where(linked, mm3(lift, lower, NT), 0.0))
            grad = d_mixed[rows, lanes]
            d_scores = halves(jnp.where(linked, mm(grad, values[:, lanes], NT), 0.0))
            d_values[rows, lanes] = mm(scores[0], grad, TN) + mm(scores[1], grad, TN)
            state = halves(states[h, c])
            outer = mm(grad, state[0], NN) + mm(grad, state[1], NN)
            d_query[rows, lanes] = mm3(d_scores, lower, NN) * up[:, lanes] + outer * jnp.exp(running[:, lanes]) * carried
            d_keys[rows, lanes] = mm3(d_scores, lift, TN) * down_[:, lanes]

    sums = [
        DpSum(p, a0, a1, a2, a3, a4, a5, a6),
        DpSum(p, b0, b1, b2, b3, b4, b5, b6),
        DpSum(p, c0, c1, c2, c3, c4, c5, c6),
    ]
    outer_products(db, gated, c0)
    sums[2].to_sibling()
    exchange.result(incoming)
    sums[2].to_z()
    bound_total[...] = jnp.zeros_like(bound_total)

    @pl.loop(0, CHUNKS)
    def _(i):
        c = CHUNKS - 1 - i
        rows = pl.ds(pl.multiple_of(c * CHUNK, CHUNK), CHUNK)
        running = run[rows, :]
        logistic, forget, query, keys, values = gates(raw, bound, rows)
        keys = keys.astype(F32)
        fade = jnp.exp(running[127:128] - running)
        column, final = segments.column(c), segments.final(c)
        ends = jnp.where(column == final, 1.0, 0.0)
        for h in range(2):
            lanes = slice(h * 128, (h + 1) * 128)
            state = incoming[h]
            pair = halves(state)
            tail = halves(keys[:, lanes] * fade[:, lanes] * ends)
            value_grad = d_values[rows, lanes] + mm3(tail, pair, NT)
            draw[rows, 512 + h * 128 : 512 + (h + 1) * 128] = value_grad.astype(BF16)
            lift = mm(values[:, lanes], pair[0], NN) + mm(values[:, lanes], pair[1], NN)
            key_grad = d_keys[rows, lanes] + lift * fade[:, lanes] * ends
            at_end = jnp.sum(states[h, c + 1] * state, axis=0, keepdims=True)
            query_grad = d_query[rows, lanes]
            step = query[:, lanes].astype(F32) * query_grad - keys[:, lanes] * key_grad
            log_grad = summed_rows(False, step) + at_end
            forget_grad = log_grad / forget[:, lanes] - key_grad
            rest = 1.0 - logistic[:, lanes]
            draw[rows, 256 + h * 128 : 256 + (h + 1) * 128] = (
                forget_grad * (1.0 - bound[:, lanes]) * logistic[:, lanes] * rest
            ).astype(BF16)
            bound_total[:, lanes] += jnp.sum(forget_grad * rest, axis=0, keepdims=True)
            query_raw = raw[rows, lanes]
            draw[rows, lanes] = (query_grad * slope(query_raw, sigmoid(query_raw))).astype(BF16)
            incoming[h] = state * decay[c, 0:1, lanes] + back_update[h, c]

    load.wait()

    @pl.loop(0, 8)
    def _(j):
        columns = pl.ds(pl.multiple_of(j * 256, 256), 256)
        part = mm(draw[...], w[columns, :], NT).astype(BF16)
        for h in range(NHEAD):
            ps[h, :, columns] = part[h * ROWS : (h + 1) * ROWS]

    scatter2 = HeadSum(p, ps, slots2, rs2_s, rs2_r)
    scatter2.send()
    outer_products(xn, draw.at[:, 0:512], a0)
    sums[0].to_sibling()
    outer_products(xn, draw.at[:, 512:1024], b0)
    sums[0].to_z()
    sums[1].to_sibling()
    scatter.collect()

    @pl.loop(0, 4)
    def _(i):
        rows = pl.ds(pl.multiple_of(i * 16, 16), 16)
        block_out[rows, :] = (resid[rows, :] + scatter.rows(rows)).astype(BF16)

    sums[1].to_z()
    sums[2].to_x(write(out_output))
    scatter2.collect()
    own = pl.multiple_of(p.head * ROWS, ROWS)
    out_norm[...] = jnp.zeros_like(out_norm)

    @pl.loop(0, 4)
    def _(i):
        rows = pl.ds(pl.multiple_of(i * 16, 16), 16)
        here = pl.ds(pl.multiple_of(own + i * 16, 16), 16)
        grad, x = scatter2.rows(rows), hid[here, :].astype(F32)
        inverse = lax.rsqrt(jnp.mean(x * x, axis=-1, keepdims=True) + EPS)
        scaled, normed = grad * gain[...], x * inverse
        back = inverse * (scaled - normed * jnp.mean(scaled * normed, axis=-1, keepdims=True))
        out_norm[...] += jnp.sum(grad * normed, axis=0, keepdims=True)
        grad_in[rows, :] = d_resid[rows, :] + back

    vec[...] = jnp.zeros_like(vec)
    for i in range(16):
        vec[i : i + 1, :] = out_norm[:, i * 128 : (i + 1) * 128]
        vec[16 + i : 17 + i, :] = ffn_terms[:, i * 128 : (i + 1) * 128]
    vec[32:33, :] = group_total[...]
    vec[33:34, :] = total[:, 0:128] + total[:, 128:256]
    vec[34:35, :] = bound_total[:, 0:128]
    vec[35:36, :] = bound_total[:, 128:256]
    everywhere = Total(p, vec, t0, t1, t2, t3, t4, t5, t6, t7, t8.at[0], t9.at[0])
    everywhere.send()
    sums[2].end(accumulate(out_output))
    everywhere.middle()
    sums[0].to_x(write(result_a))
    sums[1].to_x(write(result_b))
    vec[...] = everywhere.result()
    for i in range(16):
        out_norm[:, i * 128 : (i + 1) * 128] = vec[i : i + 1, :]
        out_ffn[:, i * 128 : (i + 1) * 128] = vec[16 + i : 17 + i, :]
    out_group[...] = vec[32:33, :]
    mean = jnp.sum(vec[33:34, :], axis=-1, keepdims=True) / float(8192 * D)
    out_mean[...] = jnp.broadcast_to(mean, (1, 128))
    for h in range(2):
        lanes = slice(h * 128, (h + 1) * 128)
        out_bounds[:, lanes] = soft[:, lanes] * (picked[:, lanes] - bound[:, lanes]) * vec[34 + h : 35 + h, :]
    sums[0].end(accumulate(result_a))
    out_query[...] = result_a[:, 0:256]
    out_forget[...] = result_a[:, 256:512]
    sums[1].end(accumulate(result_b))
    out_input[...] = result_b[:, 0:256]
    out_outgate[...] = result_b[:, 256:512]
    scatter.finish()
    scatter2.finish()
    exchange.finish()
    everywhere.finish()
    for one in sums:
        one.finish()


def call_mixer_backward(*arrays):
    out = jax.ShapeDtypeStruct
    return pl.pallas_call(
        mixer_backward,
        name="mixer_backward",
        out_shape=(
            out((ROWS, D), BF16),
            out((ROWS, D), F32),
            out((128, HERE), F32),
            out((128, HERE), F32),
            out((128, HERE), F32),
            out((128, HERE), F32),
            out((128, HERE), F32),
            out((24, HERE), F32),
            out((1, D), F32),
            out((1, KDIM), F32),
            out((1, D), F32),
            out((1, 128), F32),
        ),
        in_specs=[VM] * 8 + [HB] + [VM] * 9 + [SM, SM],
        out_specs=(VM,) * 12,
        scratch_shapes=[
            pltpu.VMEM((D, 1024), BF16),
            pltpu.VMEM((TOK, 1024), BF16),
            pltpu.VMEM((TOK, HERE), BF16),
            *[pltpu.VMEM((TOK, HERE), F32)] * 3,
            pltpu.VMEM((2, CHUNKS, 128, 128), F32),
            pltpu.VMEM((CHUNKS, 8, HERE), F32),
            pltpu.VMEM((2, 128, 128), F32),
            *[pltpu.VMEM((NHEAD, ROWS, D), BF16)] * 3,
            pltpu.VMEM((VEC, 128), F32),
            *exchange_scratch(),
            *eight(),
            *eight(),
            *dp_sum_scratch(512),
            *dp_sum_scratch(512),
            *dp_sum_scratch(HERE),
            pltpu.VMEM((8, VEC, 128), F32),
            pltpu.VMEM((8, VEC, 128), F32),
            pltpu.VMEM((VEC, 128), F32),
            pltpu.VMEM((VEC, 128), F32),
            *eight(),
            *eight(),
            pltpu.SemaphoreType.DMA((1,)),
            pltpu.SemaphoreType.DMA((1,)),
            pltpu.VMEM((128, 512), F32),
            pltpu.VMEM((128, 512), F32),
            pltpu.VMEM((1, 128), F32),
            pltpu.VMEM((1, HERE), F32),
            pltpu.SemaphoreType.DMA((1,)),
        ],
        compiler_params=pltpu.CompilerParams(
            collective_id=3, has_side_effects=True, vmem_limit_bytes=60 * 1024 * 1024
        ),
    )(*arrays)


def local(
    hidden_in, norm_gain, w_query, w_forget, w_input, w_outgate, lower_bounds, layer_index, group_gain,
    w_output, ffn_gain, w_gate, w_up, w_down, seq_lengths, grad_out,
):
    norm_row, ffn_row, group_row = norm_gain.reshape(1, D), ffn_gain.reshape(1, D), group_gain.reshape(1, KDIM)
    raw, xn, gated, mixed, states, run, total, w_all, wt_all = call_mixer_forward(
        hidden_in, norm_row, w_query, w_forget, w_input, w_outgate, w_output.T,
        lower_bounds, layer_index, seq_lengths, group_row,
    )
    hn, resid, wg, wu, wd = call_branch(gated, wt_all, hidden_in, ffn_row, w_gate, w_up, w_down.T)
    down, d_resid, db, ffn_terms, grad_gate, grad_up, grad_down = call_feed_forward(
        hn, grad_out, wg, wu, wd, resid, ffn_row
    )
    (
        block_out, grad_in, grad_query, grad_forget, grad_input, grad_outgate, grad_output, grad_bounds,
        grad_norm, grad_group, grad_ffn, mean,
    ) = call_mixer_backward(
        db, wt_all, raw, run, mixed, states, gated, xn, w_all, d_resid, hidden_in, down, resid, ffn_terms, total,
        norm_row, group_row, lower_bounds, layer_index, seq_lengths,
    )
    return (
        block_out,
        grad_in,
        grad_norm.reshape(D),
        grad_query,
        grad_forget,
        grad_input,
        grad_outgate,
        grad_bounds,
        grad_group.reshape(KDIM),
        grad_output.T,
        grad_ffn.reshape(D),
        grad_gate,
        grad_up,
        grad_down.T,
        mean[0, 0:1],
    )


def solution(mesh):
    return jax.shard_map(
        local,
        mesh=mesh,
        in_specs=(
            P("dp", None),
            P(),
            P("dp", "head"),
            P("dp", "head"),
            P("dp", "head"),
            P("dp", "head"),
            P(None, "head"),
            P(),
            P(),
            P("head", "dp"),
            P(),
            P("dp", "head"),
            P("dp", "head"),
            P("head", "dp"),
            P(),
            P("dp", None),
        ),
        out_specs=(
            P(("dp", "head"), None),
            P(("dp", "head"), None),
            P(),
            P("dp", "head"),
            P("dp", "head"),
            P("dp", "head"),
            P("dp", "head"),
            P(None, "head"),
            P(),
            P("head", "dp"),
            P(),
            P("dp", "head"),
            P("dp", "head"),
            P("head", "dp"),
            P(),
        ),
        check_vma=False,
    )
```

time: 1650 us -> 326 us (0.20); the launches traced: 1630 us -> 326 us
  waiting for transfers between devices: 1070 us -> 0 us
  Pallas kernels: 0 us -> 305 us
  other arithmetic: 148 us -> 0 us
  matrix products: 130 us -> 0 us
  local copies, waits for them, and re-layouts: 134 us -> 17.7 us
  blocking collectives: 111 us -> 0 us
  loops' own time: 18.3 us -> 0 us
    all_gather x10 -> x0, waiting for transfers between devices: 355 us -> none  [the longest x1 45.8 us: local(): lax.all_gather(w_gate, 'dp', axis=0, tiled=True)]
    pallas_call x0 -> x4, Pallas kernels: none -> 305 us  [the longest x1 90.8 us: call_mixer_backward(): pl.pallas_call(mixer_backward, name='mixer_backward', out_shape=(out((ROW...]
    psum x2 -> x0, waiting for transfers between devices: 281 us -> none  [the longest x1 180 us: local(): residual = inputs_float + lax.psum(branch_part, 'head')]
    reduce_scatter x6 -> x0, waiting for transfers between devices: 258 us -> none  [the longest x1 68.6 us: local(): lax.psum_scatter(contract_first(normed_low, grad_forget_raw).astype(jnp.b...]
    unnamed x26 -> x0, waiting for transfers between devices: 177 us -> none
    dot_general x138 -> x0, matrix products: 130 us -> none  [the longest x8 26.6 us: contract_first(): lax.dot_general(left, right, (((0,), (0,)), ((), ())), preferred_element_...]
    psum x1 -> x0, blocking collectives: 65.2 us -> none  [local(): lax.psum((jnp.sum(norm_terms, axis=0), jnp.sum(ffn_terms_rows, axis=0), b...]
    convert_element_type x80 -> x0, other arithmetic: 47.8 us -> none  [the longest x24 20.7 us: block_step(): tail_rows = lowered * (segment == final).astype(jnp.float32)[:, None, None]]
  transfers between devices with their start and end apart: 22 -> 0, of which waited for: 18 -> 0; matrix products, arithmetic and copies ran while one was open for 19% -> 0% of each run, Pallas kernels for 0% -> 0%
where the time goes in v1:
time: 326 us
  Pallas kernels  305 us (94%)
  local copies, waits for them, and re-layouts  17.7 us (5%)
    pallas_call x1, Pallas kernels, call_mixer_backward(): pl.pallas_call(mixer_backward, name='mixer_backward', out_shape=(out((ROW...  90.8 us
    pallas_call x1, Pallas kernels, call_feed_forward(): pl.pallas_call(feed_forward, name='feed_forward', out_shape=(out((NHEAD,...  86 us
    pallas_call x1, Pallas kernels, call_branch(): pl.pallas_call(branch, name='branch', out_shape=(out((TOK, D), BF16), out...  73.5 us
    pallas_call x1, Pallas kernels, call_mixer_forward(): pl.pallas_call(mixer_forward, name='mixer_forward', out_shape=(out((TOK,...  55.1 us
    unnamed x46, local copies, waits for them, and re-layouts  17.7 us

profile of v1, /device:TPU:1, one launch (start us, length us, event | category | flops | bytes accessed | tf_op | source)
XLA Modules:
  0.0 325.7 jit_solution(5868833712513606898)
XLA Ops:
  1.3 1.6 copy.31
  2.9 1.7 copy.33.wg
  4.6 1.7 copy.34.wu
  6.3 1.7 copy.32
  8.1 55.1 %mixer_forward.1 = (f32[512,1024]{1,0:T(8,128)}, bf16[512,2048]{1,0:T(8,128)(2,1)}, bf16[512,256]{1,0:T(8,128)(2,1)}, f32[512,256]{1,0:T(8,128)}, f32[2,5,128,12...) custom-call(bf16[512,2048]{1,0:T(8,128)(2,1)} %hid.5, ...), custom_call_target="tpu_custom_call" | custom-call | tf_op jit(solution)/shard_map/mixer_forward/pallas_call | solution.py:413
  63.2 73.5 %branch.1 = (bf16[512,2048]{1,0:T(8,128)(2,1)}, f32[64,2048]{1,0:T(8,128)}, bf16[2048,704]{1,0:T(8,128)(2,1)}, bf16[2048,704]{1,0:T(8,128)(2,1)}, bf16[2048,704]{1,0:T(8,128)(2,1)}) custom-call(bf16[512,256]{1,0:T(8,128)(2,1)} %get-tuple-element.48.gated, bf16[2048,256]{1,0:T(8,128)(2,1)} %get-tuple-element.49.wt, bf16[512,2048]{1,0:T(8,128)(2,1)} %hid.5, ...), custom_call_target="tpu_custom_call" | custom-call | tf_op jit(solution)/shard_map/branch/pallas_call | solution.py:563
  136.7 86.0 %feed_forward.1 = (bf16[8,64,2048]{2,1,0:T(8,128)(2,1)}, f32[64,2048]{1,0:T(8,128)}, bf16[512,2048]{1,0:T(8,128)(2,1)}, f32[1,2048]{1,0:T(1,128)}, f32[128,704]{...) custom-call(bf16[512,2048]{1,0:T(8,128)(2,1)} %get-tuple-element.50.hn, bf16[512,2048]{1,0:T(8,128)(2,1)} %dy.1, ...), custom_call_target="tpu_custom_call" | custom-call | tf_op jit(solution)/shard_map/feed_forward/pallas_call | solution.py:785
  222.7 0.0 copy-start.3
  222.7 0.0 copy-start.2
  222.8 0.0 copy-start.1
  222.8 90.8 %mixer_backward.1 = (bf16[64,2048]{1,0:T(8,128)(2,1)}, f32[64,2048]{1,0:T(8,128)}, f32[128,256]{1,0:T(8,128)}, f32[128,256]{1,0:T(8,128)}, f32[128,256]{1,0:T(8,...) custom-call(bf16[512,2048]{1,0:T(8,128)(2,1)} %get-tuple-element.55., ...), custom_call_target="tpu_custom_call" | custom-call | tf_op jit(solution)/shard_map/mixer_backward/pallas_call | solution.py:1082
  313.5 0.0 copy-start.4
  313.5 0.0 copy-start
  313.5 0.0 copy-start.11
  313.6 0.0 copy-start.8
  313.6 1.7 copy.35
  315.3 0.0 copy-done.3
  315.3 0.9 copy.36
  316.2 0.0 copy-done.2
  316.2 0.9 copy.37
  317.1 0.9 copy.38
  318.1 0.7 copy.51
  318.8 0.8 copy.52
  319.6 0.6 copy.53
  320.2 0.7 copy.54
  320.8 0.7 copy.55
  321.5 0.7 copy.56
  322.1 0.7 copy.57
  322.8 0.6 copy.58
  323.4 0.0 copy-done.13
  323.4 0.5 copy.59
  323.9 0.6 copy.60
  (18 shorter events, 0.0 us)
Async XLA Ops:
  222.7 92.6 %copy-start.3 = (f32[128,704]{1,0:T(8,128)S(1)}, f32[128,704]{1,0:T(8,128)}, u32[]{:S(2)}) copy-start(f32[128,704]{1,0:T(8,128)} %get-tuple-element.92) | copy-start | bytes 1081348
  222.7 93.5 %copy-start.2 = (f32[128,704]{1,0:T(8,128)S(1)}, f32[128,704]{1,0:T(8,128)}, u32[]{:S(2)}) copy-start(f32[128,704]{1,0:T(8,128)} %get-tuple-element.93) | copy-start | bytes 1081348
  222.8 94.4 %copy-start.1 = (f32[128,704]{1,0:T(8,128)S(1)}, f32[128,704]{1,0:T(8,128)}, u32[]{:S(2)}) copy-start(f32[128,704]{1,0:T(8,128)} %get-tuple-element.79) | copy-start | bytes 1081348
  313.5 4.5 %copy-start.4 = (bf16[64,2048]{1,0:T(8,128)(2,1)S(1)}, bf16[64,2048]{1,0:T(8,128)(2,1)}, u32[]{:S(2)}) copy-start(bf16[64,2048]{1,0:T(8,128)(2,1)} %get-tuple-element.111) | copy-start | bytes 786436
  313.5 5.2 %copy-start = (f32[64,2048]{1,0:T(8,128)S(1)}, f32[64,2048]{1,0:T(8,128)}, u32[]{:S(2)}) copy-start(f32[64,2048]{1,0:T(8,128)} %get-tuple-element.112) | copy-start | bytes 1572868
  313.5 6.0 %copy-start.11 = (f32[1,2048]{1,0:T(1,128)S(1)}, f32[1,2048]{1,0:T(1,128)}, u32[]{:S(2)}) copy-start(f32[1,2048]{1,0:T(1,128)} %get-tuple-element.68) | copy-start | bytes 24580
  313.6 6.6 %copy-start.8 = (f32[128,256]{1,0:T(8,128)S(1)}, f32[128,256]{1,0:T(8,128)}, u32[]{:S(2)}) copy-start(f32[128,256]{1,0:T(8,128)} %get-tuple-element.114) | copy-start | bytes 393220
  315.3 5.5 %copy-start.7 = (f32[128,256]{1,0:T(8,128)S(1)}, f32[128,256]{1,0:T(8,128)}, u32[]{:S(2)}) copy-start(f32[128,256]{1,0:T(8,128)} %get-tuple-element.115) | copy-start | bytes 393220
  315.3 6.2 %copy-start.6 = (f32[128,256]{1,0:T(8,128)S(1)}, f32[128,256]{1,0:T(8,128)}, u32[]{:S(2)}) copy-start(f32[128,256]{1,0:T(8,128)} %get-tuple-element.116) | copy-start | bytes 393220
  316.2 5.9 %copy-start.5 = (f32[128,256]{1,0:T(8,128)S(1)}, f32[128,256]{1,0:T(8,128)}, u32[]{:S(2)}) copy-start(f32[128,256]{1,0:T(8,128)} %get-tuple-element.117) | copy-start | bytes 393220
  316.2 6.6 %copy-start.9 = (f32[24,256]{1,0:T(8,128)S(1)}, f32[24,256]{1,0:T(8,128)}, u32[]{:S(2)}) copy-start(f32[24,256]{1,0:T(8,128)} %get-tuple-element.118) | copy-start | bytes 73732
  316.2 7.2 %copy-start.13 = (f32[1,128]{1,0:T(1,128)S(1)}, f32[1,128]{1,0:T(1,128)}, u32[]{:S(2)}) copy-start(f32[1,128]{1,0:T(1,128)} %get-tuple-element.74) | copy-start | bytes 1540
  316.2 7.7 %copy-start.10 = (f32[1,2048]{1,0:T(1,128)S(1)}, f32[1,2048]{1,0:T(1,128)}, u32[]{:S(2)}) copy-start(f32[1,2048]{1,0:T(1,128)} %get-tuple-element.76) | copy-start | bytes 24580
  316.2 8.3 %copy-start.12 = (f32[1,128]{1,0:T(1,128)S(1)}, f32[1,128]{1,0:T(1,128)}, u32[]{:S(2)}) copy-start(f32[1,128]{1,0:T(1,128)} %get-tuple-element.80) | copy-start | bytes 1540

commit v2 on v1

v2 whole, which is shorter than its diff:
```python
from functools import partial

import jax
import jax.numpy as jnp
from jax import lax
from jax.experimental import pallas as pl
from jax.experimental.pallas import tpu as pltpu
from jax.sharding import PartitionSpec as P

D = 2048
KDIM = 128
CHUNK = 128
TOK = 512
CHUNKS = TOK // CHUNK
HERE = 256
FFH = 704
NSEQ = 12
NHEAD = 8
ROWS = TOK // NHEAD
EPS = 1e-06
F32 = jnp.float32
BF16 = jnp.bfloat16
MESH = pl.DeviceIdType.MESH
VM = pl.BlockSpec(memory_space=pltpu.VMEM)
SM = pl.BlockSpec(memory_space=pltpu.SMEM)
HB = pl.BlockSpec(memory_space=pl.ANY)


class Spot:
    def __init__(self):
        self.dp = lax.axis_index("dp")
        self.head = lax.axis_index("head")
        self.core = lax.rem(self.dp, 2)
        self.chip = lax.div(self.dp, 2)
        self.xh = lax.rem(self.chip, 2)
        self.z = lax.div(self.chip, 2)

    def at(self, dz, xh, core):
        return (lax.rem(self.z + dz, 4) * 2 + xh) * 2 + core

    @property
    def sibling(self):
        return {"dp": self.chip * 2 + 1 - self.core}

    def chips(self):
        return [{"dp": lax.rem(self.chip + k, 8) * 2 + self.core} for k in range(1, 8)]

    def heads(self):
        return [{"head": lax.rem(self.head + k, NHEAD)} for k in range(1, NHEAD)]


def greet(ids):
    barrier = pltpu.get_barrier_semaphore()
    for one in ids:
        pl.semaphore_signal(barrier, inc=1, device_id=one, device_id_type=MESH)
    pl.semaphore_wait(barrier, len(ids))


def rcopy(src, dst, send, recv, where):
    return pltpu.make_async_remote_copy(
        src_ref=src, dst_ref=dst, send_sem=send, recv_sem=recv, device_id=where, device_id_type=MESH
    )


GATHER_SENDS = 17


class Gather:
    def __init__(self, spot, g, send, recv, half, columns=0):
        self.spot, self.g, self.s, self.r, self.h = spot, g, send, recv, half
        self.columns, self.middle = columns, (columns or 128) // 2

    def block(self, d, start=0, rows=0):
        if self.columns:
            rows = rows or self.columns
            return self.g.at[pl.ds(start, rows), pl.ds(pl.multiple_of(d * 128, 128), 128)]
        return self.g.at[pl.ds(pl.multiple_of(d * 128 + start, 64), rows or 128), :]

    def push(self, d, to, k):
        rcopy(self.block(d), self.block(d), self.s.at[k], self.r.at[d], {"dp": to}).start()

    def push_half(self, d, to, k, xh, part):
        b = self.block(d, part * self.middle, self.middle)
        rcopy(b, b, self.s.at[k], self.h.at[2 * xh + part], {"dp": to}).start()

    def arrived(self, d):
        b = self.block(d)
        rcopy(b, b, self.s.at[0], self.r.at[d], self.spot.sibling).wait_recv()

    def arrived_halves(self, d, xh):
        for part in range(2):
            b = self.block(d, part * self.middle, self.middle)
            rcopy(b, b, self.s.at[0], self.h.at[2 * xh + part], self.spot.sibling).wait_recv()

    def first(self):
        p = self.spot
        self.push(p.dp, p.at(0, 1 - p.xh, p.core), 0)
        self.push(p.dp, p.at(1, p.xh, p.core), 1)
        self.push(p.dp, p.at(3, p.xh, p.core), 2)
        self.push(p.dp, p.at(0, p.xh, 1 - p.core), 3)

    def second(self):
        p = self.spot
        b = p.at(0, 1 - p.xh, p.core)
        self.arrived(b)
        self.push(b, p.at(1, p.xh, p.core), 4)
        self.push(b, p.at(3, p.xh, p.core), 5)
        self.push(b, p.at(0, p.xh, 1 - p.core), 6)

    def third(self):
        p = self.spot
        for i, h in enumerate((p.xh, 1 - p.xh)):
            b = p.at(3, h, p.core)
            self.arrived(b)
            self.push_half(b, p.at(1, p.xh, p.core), 7 + i, h, 0)
            self.push(b, p.at(0, p.xh, 1 - p.core), 9 + i)
            b = p.at(1, h, p.core)
            self.arrived(b)
            self.push_half(b, p.at(3, p.xh, p.core), 11 + i, h, 1)
            self.push(b, p.at(0, p.xh, 1 - p.core), 13 + i)

    def fourth(self):
        p = self.spot
        for i, h in enumerate((p.xh, 1 - p.xh)):
            b = p.at(2, h, p.core)
            self.arrived_halves(b, h)
            self.push(b, p.at(0, p.xh, 1 - p.core), 15 + i)

    def last(self):
        p = self.spot
        for dz in range(4):
            for h in range(2):
                self.arrived(p.at(dz, h, 1 - p.core))
        half = self.block(0, 0, self.middle)
        for k in range(GATHER_SENDS):
            b = half if k in (7, 8, 11, 12) else self.block(0)
            rcopy(b, b, self.s.at[k], self.r.at[0], p.sibling).wait_send()


def gather_semaphores():
    return [
        pltpu.SemaphoreType.DMA((GATHER_SENDS,)),
        pltpu.SemaphoreType.DMA((16,)),
        pltpu.SemaphoreType.DMA((4,)),
    ]


NN = (((1,), (0,)), ((), ()))
NT = (((1,), (1,)), ((), ()))
TN = (((0,), (0,)), ((), ()))


def mm(a, b, dims):
    return lax.dot_general(a, b, dims, preferred_element_type=F32)


def halves(a):
    high = a.astype(BF16)
    return high, (a - high.astype(F32)).astype(BF16)


def mm2(a, b, dims):
    return mm(a[0], b, dims) + mm(a[1], b, dims)


def mm3(a, b, dims):
    return mm(a[0], b[0], dims) + (mm(a[0], b[1], dims) + mm(a[1], b[0], dims))


def triangle(lower):
    rows = lax.broadcasted_iota(jnp.int32, (CHUNK, CHUNK), 0)
    columns = lax.broadcasted_iota(jnp.int32, (CHUNK, CHUNK), 1)
    return (rows >= columns if lower else rows <= columns).astype(BF16)


def summed_rows(lower, x):
    high = x.astype(BF16)
    rest = x - high.astype(F32)
    middle = rest.astype(BF16)
    low = (rest - middle.astype(F32)).astype(BF16)
    t = triangle(lower)
    return mm(t, high, NN) + (mm(t, middle, NN) + mm(t, low, NN))


class Segments:
    def __init__(self, spot, seq):
        self.starts = []
        total = jnp.int32(0)
        for i in range(NSEQ):
            self.starts.append(total)
            total = total + seq[i]
        self.first = spot.dp * TOK

    def of(self, position):
        found = jnp.where(position >= self.starts[0], 1, 0)
        for s in self.starts[1:]:
            found = found + jnp.where(position >= s, 1, 0)
        return found - 1

    def column(self, c):
        return self.of(self.first + c * CHUNK + lax.broadcasted_iota(jnp.int32, (CHUNK, KDIM), 0))

    def row(self, c):
        return self.of(self.first + c * CHUNK + lax.broadcasted_iota(jnp.int32, (CHUNK, KDIM), 1))

    def before(self, c):
        return self.of(self.first + c * CHUNK - 1)

    def final(self, c):
        return self.of(self.first + (c + 1) * CHUNK - 1)


def lower_bound(lb, layer):
    x = lb[...]
    e = jnp.exp(x - jnp.max(x, axis=0, keepdims=True))
    soft = e / jnp.sum(e, axis=0, keepdims=True)
    depth = lax.broadcasted_iota(jnp.int32, x.shape, 0)
    picked = jnp.where((depth >= 1) & (depth <= layer), 1.0, 0.0)
    return soft, picked, jnp.sum(soft * picked, axis=0, keepdims=True)


def sigmoid(x):
    return lax.logistic(x)


def slope(x, s):
    return s * (1.0 + x * (1.0 - s))


class Exchange:
    def __init__(self, spot, msg, sib, slots, give, take, send, recv, backward):
        self.p, self.msg, self.sib, self.slots = spot, msg, sib, slots
        self.give, self.take, self.s, self.r, self.back = give, take, send, recv, backward

    def to_sibling(self):
        p = self.p
        rcopy(self.msg.at[1 - p.core], self.sib, self.s.at[7], self.r.at[8], p.sibling).start()

    def to_chips(self):
        p = self.p
        rcopy(self.sib, self.sib, self.s.at[7], self.r.at[8], p.sibling).wait_recv()
        mine, other = self.msg[p.core], self.sib[...]
        zero = p.core == 0
        one, two = jnp.where(zero, mine, other), jnp.where(zero, other, mine)
        near, far = (two, one) if self.back else (one, two)
        self.near = near
        state = near[0:128] * far[128:129] + far[0:128]
        self.slots[p.chip, 0:128, :] = state
        self.slots[p.chip, 128:136, :] = near[128:136] * far[128:136]
        for k, to in enumerate(p.chips()):
            rcopy(self.slots.at[p.chip], self.slots.at[p.chip], self.s.at[k], self.r.at[p.chip], to).start()

    def result(self, out):
        p = self.p
        for k in range(1, 8):
            chip = lax.rem(p.chip + k, 8)
            rcopy(self.slots.at[chip], self.slots.at[chip], self.s.at[0], self.r.at[chip], p.sibling).wait_recv()
        state = jnp.zeros((128, 128), F32)
        for k in range(7, 0, -1) if self.back else range(7):
            m = self.slots[k]
            after = state * m[128:129] + m[0:128]
            state = jnp.where(k > p.chip if self.back else k < p.chip, after, state)
        second = state * self.near[128:129] + self.near[0:128]
        is_first = p.core == (1 if self.back else 0)
        self.give[...] = jnp.where(is_first, second, state)
        move = rcopy(self.give, self.take, self.s.at[8], self.r.at[9], p.sibling)
        move.start()
        out[p.core] = jnp.where(is_first, state, second)
        move.wait_recv()
        out[1 - p.core] = self.take[...]

    def finish(self):
        p = self.p
        for k in range(7):
            rcopy(self.slots.at[0], self.slots.at[0], self.s.at[k], self.r.at[0], p.sibling).wait_send()
        rcopy(self.sib, self.sib, self.s.at[7], self.r.at[8], p.sibling).wait_send()
        rcopy(self.give, self.take, self.s.at[8], self.r.at[9], p.sibling).wait_send()


def exchange_scratch():
    return [
        pltpu.VMEM((2, 136, 128), F32),
        pltpu.VMEM((136, 128), F32),
        pltpu.VMEM((8, 136, 128), F32),
        pltpu.VMEM((128, 128), F32),
        pltpu.VMEM((128, 128), F32),
        pltpu.SemaphoreType.DMA((9,)),
        pltpu.SemaphoreType.DMA((10,)),
    ]


def gates(raw, bound, rows):
    query_raw = raw[rows, 0:256]
    logistic = sigmoid(raw[rows, 256:512])
    forget = bound + (1.0 - bound) * logistic
    query = (query_raw * sigmoid(query_raw)).astype(BF16)
    keys = (1.0 - forget).astype(BF16)
    values = raw[rows, 512:768].astype(BF16)
    return logistic, forget, query, keys, values


def eighth(ref, h):
    return ref.at[pl.ds(pl.multiple_of(h * ROWS, ROWS), ROWS), :]


class HeadSum:
    def __init__(self, spot, ps, slots, send, recv):
        self.p, self.ps, self.slots, self.s, self.r = spot, ps, slots, send, recv

    def send(self):
        p = self.p
        for k in range(1, NHEAD):
            h = lax.rem(p.head + k, NHEAD)
            rcopy(eighth(self.ps, h), eighth(self.slots, p.head), self.s.at[k], self.r.at[p.head], {"head": h}).start()

    def collect(self):
        p = self.p
        mine = pl.ds(pl.multiple_of(p.head * ROWS, ROWS), ROWS)
        self.slots[mine, :] = self.ps[mine, :]
        for k in range(1, NHEAD):
            h = lax.rem(p.head + k, NHEAD)
            one = eighth(self.slots, h)
            rcopy(one, one, self.s.at[0], self.r.at[h], p.sibling).wait_recv()

    def rows(self, start, count):
        total = None
        for h in range(NHEAD):
            one = self.slots[pl.ds(pl.multiple_of(h * ROWS + start, 16), count), :].astype(F32)
            total = one if total is None else total + one
        return total

    def finish(self):
        for k in range(1, NHEAD):
            one = eighth(self.ps, 0)
            rcopy(one, one, self.s.at[k], self.r.at[0], self.p.sibling).wait_send()


class HeadGather:
    def __init__(self, spot, full, send, recv):
        self.p, self.full, self.s, self.r = spot, full, send, recv

    def block(self, h):
        return self.full.at[pl.ds(pl.multiple_of(h * ROWS, ROWS), ROWS), :]

    def send(self):
        p = self.p
        for k in range(1, NHEAD):
            h = lax.rem(p.head + k, NHEAD)
            rcopy(self.block(p.head), self.block(p.head), self.s.at[k], self.r.at[p.head], {"head": h}).start()

    def collect(self):
        p = self.p
        for k in range(1, NHEAD):
            h = lax.rem(p.head + k, NHEAD)
            rcopy(self.block(h), self.block(h), self.s.at[0], self.r.at[h], p.sibling).wait_recv()

    def finish(self):
        for k in range(1, NHEAD):
            rcopy(self.block(0), self.block(0), self.s.at[k], self.r.at[0], self.p.sibling).wait_send()


def eight():
    return [pltpu.SemaphoreType.DMA((8,)), pltpu.SemaphoreType.DMA((8,))]


class DpSum:
    def __init__(self, spot, rows, gs, cr, zr, xs, xr, send, recv):
        n = pl.ds(0, rows)
        self.rows, self.p = rows, spot
        self.gs, self.cr, self.zr = gs.at[:, :, n, :], cr.at[:, n, :], zr.at[:, :, n, :]
        self.xs, self.xr, self.s, self.r = xs.at[n, :], xr.at[n, :], send, recv

    def pair(self, i):
        p = self.p
        two = pl.ds(2 * i, 2)
        return rcopy(self.gs.at[1 - p.core, two], self.cr.at[two], self.s.at[i], self.r.at[i], p.sibling)

    def to_sibling(self):
        for i in range(4):
            self.pair(i).start()

    def across(self, d):
        p = self.p
        z = lax.rem(p.z + d, 4)
        where = {"dp": (z * 2 + p.xh) * 2 + p.core}
        return rcopy(self.gs.at[p.core, pl.ds(z * 2, 2)], self.zr.at[d - 1], self.s.at[3 + d], self.r.at[3 + d], where)

    def to_z(self):
        p = self.p
        for i in range(4):
            self.pair(i).wait_recv()

        @pl.loop(0, 8)
        def _(k):
            self.gs[p.core, k] = (self.gs[p.core, k].astype(F32) + self.cr[k].astype(F32)).astype(BF16)

        for d in (1, 3, 2):
            self.across(d).start()

    def last_move(self):
        p = self.p
        where = {"dp": (p.z * 2 + 1 - p.xh) * 2 + p.core}
        return rcopy(self.xs, self.xr, self.s.at[7], self.r.at[7], where)

    def to_x(self, put):
        p = self.p
        for d in (1, 3, 2):
            self.across(d).wait_recv()

        def total(h):
            one = self.gs[p.core, 2 * p.z + h].astype(F32)
            for i in range(3):
                one = one + self.zr[i, h].astype(F32)
            return one

        self.xs[...] = total(1 - p.xh).astype(BF16)
        self.last_move().start()
        put(total(p.xh))

    def end(self, add):
        self.last_move().wait_recv()
        add(self.xr[...].astype(F32))

    def finish(self):
        for i in range(4):
            self.pair(i).wait_send()
        for d in (1, 3, 2):
            self.across(d).wait_send()
        self.last_move().wait_send()


def dp_sum_scratch(rows):
    return [
        pltpu.VMEM((2, 8, rows, 128), BF16),
        pltpu.VMEM((8, rows, 128), BF16),
        pltpu.VMEM((3, 2, rows, 128), BF16),
        pltpu.VMEM((rows, 128), BF16),
        pltpu.VMEM((rows, 128), BF16),
        *eight(),
    ]


def products(left_turned, right, gs):
    @pl.loop(0, 8)
    def _(k):
        columns = pl.ds(pl.multiple_of(k * 256, 256), 256)
        both = mm(left_turned[...], right[:, columns], NN).astype(BF16)
        gs[0, k] = both[:, 0:128]
        gs[1, k] = both[:, 128:256]


def products_turned(left, right, gs):
    @pl.loop(0, 8)
    def _(k):
        columns = pl.ds(pl.multiple_of(k * 256, 256), 256)
        both = mm(left[:, columns], right[...], TN).astype(BF16)
        for q in range(4):
            gs[0, k, 128 * q : 128 * (q + 1), :] = both[0:128, 128 * q : 128 * (q + 1)]
            gs[1, k, 128 * q : 128 * (q + 1), :] = both[128:256, 128 * q : 128 * (q + 1)]


def write(ref):
    def put(x):
        ref[...] = x

    return put


def accumulate(ref):
    def add(x):
        ref[...] += x

    return add


VEC = 40


class Total:
    def __init__(self, spot, vec, h_slots, c_slots, own, other, h_s, h_r, c_s, c_r, k_s, k_r):
        self.p, self.vec, self.hs, self.cs, self.own, self.other = spot, vec, h_slots, c_slots, own, other
        self.h_s, self.h_r, self.c_s, self.c_r, self.k_s, self.k_r = h_s, h_r, c_s, c_r, k_s, k_r

    def send(self):
        p = self.p
        self.hs[p.head] = self.vec[...]
        for k in range(1, NHEAD):
            h = lax.rem(p.head + k, NHEAD)
            rcopy(self.hs.at[p.head], self.hs.at[p.head], self.h_s.at[k], self.h_r.at[p.head], {"head": h}).start()

    def middle(self):
        p = self.p
        for k in range(1, NHEAD):
            h = lax.rem(p.head + k, NHEAD)
            rcopy(self.hs.at[h], self.hs.at[h], self.h_s.at[0], self.h_r.at[h], p.sibling).wait_recv()
        total = self.hs[0]
        for h in range(1, NHEAD):
            total = total + self.hs[h]
        per_head = lax.broadcasted_iota(jnp.int32, (VEC, 128), 0) >= 34
        self.cs[p.chip] = jnp.where(per_head, self.vec[...], total)
        for k, to in enumerate(p.chips()):
            rcopy(self.cs.at[p.chip], self.cs.at[p.chip], self.c_s.at[k], self.c_r.at[p.chip], to).start()

    def result(self):
        p = self.p
        for k in range(1, 8):
            chip = lax.rem(p.chip + k, 8)
            rcopy(self.cs.at[chip], self.cs.at[chip], self.c_s.at[0], self.c_r.at[chip], p.sibling).wait_recv()
        total = self.cs[0]
        for k in range(1, 8):
            total = total + self.cs[k]
        self.own[...] = total
        move = rcopy(self.own, self.other, self.k_s, self.k_r, p.sibling)
        move.start()
        move.wait_recv()
        return total + self.other[...]

    def finish(self):
        p = self.p
        for k in range(1, NHEAD):
            rcopy(self.hs.at[0], self.hs.at[0], self.h_s.at[k], self.h_r.at[0], p.sibling).wait_send()
        for k in range(7):
            rcopy(self.cs.at[0], self.cs.at[0], self.c_s.at[k], self.c_r.at[0], p.sibling).wait_send()
        rcopy(self.own, self.other, self.k_s, self.k_r, p.sibling).wait_send()


def forward(
    hid, gain, wq, wf, wi, wo, w_output, lb, layer, seq, group_gain, ffn_gain, wg, wu, wd,
    raw, xn_out, gated, mixed, states, run, total, w_out, wt_out, hn_out, resid, wg_out, wu_out, wd_out,
    xn, w, wt, g0, g1, g2, hn, ps, slots, inner_update, decay, incoming,
    msg, sib, slots3, give, take, ex_send, ex_recv, rs_s, rs_r, ag_s, ag_r,
    ws, wr, wh, os, or_, oh, s0, r0, h0, s1, r1, h1, s2, r2, h2, local_sem,
):
    p = Spot()
    mine = pl.ds(pl.multiple_of(p.dp * 128, 128), 128)
    for k, one in enumerate((wq, wf, wi, wo)):
        w[mine, 256 * k : 256 * (k + 1)] = one[...]
    greet(p.chips() + [p.sibling] + p.heads())
    gather = Gather(p, w, ws, wr, wh)
    gather.first()
    wt[:, mine] = w_output[...]
    later = Gather(p, wt, os, or_, oh, HERE)
    for one, full in zip((wg, wu, wd), (g0, g1, g2)):
        full[:, mine] = one[...]
    gathers = [Gather(p, g0, s0, r0, h0, FFH), Gather(p, g1, s1, r1, h1, FFH), Gather(p, g2, s2, r2, h2, FFH)]

    @pl.loop(0, 8)
    def _(i):
        rows = pl.ds(pl.multiple_of(i * 64, 64), 64)
        x = hid[rows, :].astype(F32)
        scale = lax.rsqrt(jnp.mean(x * x, axis=-1, keepdims=True) + EPS)
        xn[rows, :] = (x * scale * gain[...]).astype(BF16)

    keeps = []

    def keep(source, out):
        move = pltpu.make_async_copy(source, out, local_sem.at[len(keeps)])
        move.start()
        keeps.append(move)

    keep(xn, xn_out)
    gather.second()
    gather.third()
    gather.fourth()
    later.first()
    gathers[0].first()
    gather.last()
    keep(w, w_out)

    @pl.loop(0, 4)
    def _(j):
        columns = pl.ds(pl.multiple_of(j * 256, 256), 256)
        raw[:, columns] = mm(xn[...], w[:, columns], NN)

    later.second()
    segments = Segments(p, seq)
    bound = lower_bound(lb, layer[0])[2]
    total[...] = jnp.zeros_like(total)

    @pl.loop(0, CHUNKS)
    def _(c):
        rows = pl.ds(pl.multiple_of(c * CHUNK, CHUNK), CHUNK)
        logistic, forget, query, keys, values = gates(raw, bound, rows)
        total[...] += jnp.sum(forget, axis=0, keepdims=True)
        running = summed_rows(True, jnp.log(forget))
        run[rows, :] = running
        middle, ending = running[63:64], running[127:128]
        lifted = query.astype(F32) * jnp.exp(running - middle)
        lowered = keys.astype(F32) * jnp.exp(middle - running)
        tail = keys.astype(F32) * jnp.exp(ending - running)
        column, row = segments.column(c), segments.row(c)
        linked = (column == row) & (
            lax.broadcasted_iota(jnp.int32, (CHUNK, CHUNK), 0)
            >= lax.broadcasted_iota(jnp.int32, (CHUNK, CHUNK), 1)
        )
        final = segments.final(c)
        rate = jnp.exp(ending) * jnp.where(final == segments.before(c), 1.0, 0.0)
        decay[c] = jnp.broadcast_to(rate, (8, HERE))
        ends = jnp.where(column == final, 1.0, 0.0)
        for h in range(2):
            lanes = slice(h * 128, (h + 1) * 128)
            scores = mm3(halves(lifted[:, lanes]), halves(lowered[:, lanes]), NT)
            scores = jnp.where(linked, scores, 0.0)
            mixed[rows, lanes] = mm2(halves(scores), values[:, lanes], NN)
            high, low = halves(tail[:, lanes] * ends)
            inner_update[h, c] = mm(values[:, lanes], high, TN) + mm(values[:, lanes], low, TN)

    for h in range(2):
        lanes = slice(h * 128, (h + 1) * 128)
        state, rate = inner_update[h, 0], decay[0, 0:1, lanes]
        for c in range(1, CHUNKS):
            state = state * decay[c, 0:1, lanes] + inner_update[h, c]
            rate = rate * decay[c, 0:1, lanes]
        msg[h, 0:128, :] = state
        msg[h, 128:136, :] = jnp.broadcast_to(rate, (8, 128))
    exchange = Exchange(p, msg, sib, slots3, give, take, ex_send, ex_recv, False)
    exchange.to_sibling()
    exchange.to_chips()
    later.third()
    gathers[1].first()
    gathers[2].first()
    gathers[0].second()
    later.fourth()
    exchange.result(incoming)
    for h in range(2):
        lanes = slice(h * 128, (h + 1) * 128)
        state = incoming[h]
        states[h, 0] = state
        for c in range(CHUNKS):
            state = state * decay[c, 0:1, lanes] + inner_update[h, c]
            states[h, c + 1] = state

    @pl.loop(0, CHUNKS)
    def _(c):
        rows = pl.ds(pl.multiple_of(c * CHUNK, CHUNK), CHUNK)
        carried = jnp.where(segments.column(c) == segments.before(c), 1.0, 0.0)
        for h in range(2):
            lanes = slice(h * 128, (h + 1) * 128)
            query_raw = raw[rows, h * 128 : (h + 1) * 128]
            query = (query_raw * sigmoid(query_raw)).astype(BF16).astype(F32)
            reach = query * jnp.exp(run[rows, lanes]) * carried
            x = mixed[rows, lanes] + mm3(halves(reach), halves(states[h, c]), NT)
            mixed[rows, lanes] = x
            scale = lax.rsqrt(jnp.mean(x * x, axis=-1, keepdims=True) + EPS)
            gate = raw[rows, 768 + h * 128 : 768 + (h + 1) * 128]
            gated[rows, lanes] = (x * scale * group_gain[...] * (gate * sigmoid(gate))).astype(BF16)

    gathers[1].second()
    gathers[2].second()
    later.last()
    keep(wt, wt_out)

    @pl.loop(0, 8)
    def _(j):
        columns = pl.ds(pl.multiple_of(j * 256, 256), 256)
        ps[:, columns] = mm(gated[...], wt[:, columns], NN).astype(BF16)

    scatter = HeadSum(p, ps, slots, rs_s, rs_r)
    scatter.send()
    for g in gathers:
        g.third()
    for g in gathers:
        g.fourth()
    scatter.collect()
    own = pl.multiple_of(p.head * ROWS, ROWS)

    @pl.loop(0, 4)
    def _(i):
        rows = pl.ds(pl.multiple_of(i * 16, 16), 16)
        here = pl.ds(pl.multiple_of(own + i * 16, 16), 16)
        x = hid[here, :].astype(F32) + scatter.rows(i * 16, 16)
        resid[rows, :] = x
        scale = lax.rsqrt(jnp.mean(x * x, axis=-1, keepdims=True) + EPS)
        hn[here, :] = (x * scale * ffn_gain[...]).astype(BF16)

    spread = HeadGather(p, hn, ag_s, ag_r)
    spread.send()
    for g, full, out in zip(gathers, (g0, g1, g2), (wg_out, wu_out, wd_out)):
        g.last()
        keep(full, out)
    exchange.finish()
    scatter.finish()
    spread.collect()
    keep(hn, hn_out)
    spread.finish()
    for move in keeps:
        move.wait()


def call_forward(*arrays):
    out = jax.ShapeDtypeStruct
    return pl.pallas_call(
        forward,
        name="forward",
        out_shape=(
            out((TOK, 1024), F32),
            out((TOK, D), BF16),
            out((TOK, HERE), BF16),
            out((TOK, HERE), F32),
            out((2, CHUNKS + 1, 128, 128), F32),
            out((TOK, HERE), F32),
            out((1, HERE), F32),
            out((D, 1024), BF16),
            out((HERE, D), BF16),
            out((TOK, D), BF16),
            out((ROWS, D), F32),
            out((FFH, D), BF16),
            out((FFH, D), BF16),
            out((FFH, D), BF16),
        ),
        in_specs=[VM] * 8 + [SM, SM] + [VM] * 5,
        out_specs=(VM, HB, VM, VM, VM, VM, VM, HB, HB, HB, VM, HB, HB, HB),
        scratch_shapes=[
            pltpu.VMEM((TOK, D), BF16),
            pltpu.VMEM((D, 1024), BF16),
            pltpu.VMEM((HERE, D), BF16),
            *[pltpu.VMEM((FFH, D), BF16)] * 3,
            *[pltpu.VMEM((TOK, D), BF16)] * 3,
            pltpu.VMEM((2, CHUNKS, 128, 128), F32),
            pltpu.VMEM((CHUNKS, 8, HERE), F32),
            pltpu.VMEM((2, 128, 128), F32),
            *exchange_scratch(),
            *eight(),
            *eight(),
            *gather_semaphores(),
            *gather_semaphores(),
            *gather_semaphores(),
            *gather_semaphores(),
            *gather_semaphores(),
            pltpu.SemaphoreType.DMA((7,)),
        ],
        compiler_params=pltpu.CompilerParams(
            collective_id=0, has_side_effects=True, vmem_limit_bytes=58 * 1024 * 1024
        ),
    )(*arrays)


def backward(
    hn_in, dy_in, wg_in, wu_in, wd_in, resid, ffn_gain, wt, raw_in, run, mixed, states, gated, xn_in, w_in, hid,
    total, gain, group_gain, lb, layer, seq,
    block_out, grad_in, out_query, out_forget, out_input, out_outgate, out_output, out_bounds,
    out_norm, out_group, out_ffn, out_mean, out_gate, out_up, out_down,
    hn, dy, wg, wu, wd, hidden, dg, du, hidden_t, dg_t, du_t, gated_t, ps, slots, db, d_resid, hid_rows, raw,
    draw, d_mixed, d_query, d_keys, d_values, back_update, decay, incoming, vec,
    norm_terms, ffn_terms, group_total, bound_total,
    msg, sib, slots3, give, take, ex_send, ex_recv, rs_s, rs_r, ag_s, ag_r, rs1_s, rs1_r, rs2_s, rs2_r,
    a0, a1, a2, a3, a4, a5, a6, b0, b1, b2, b3, b4, b5, b6, c0, c1, c2, c3, c4, c5, c6,
    e0, e1, e2, e3, e4, e5, e6, f3, f4, f5, f6, g3, g4, g5, g6,
    t0, t1, t2, t3, t4, t5, t6, t7, t8, t9, local_sem,
):
    def load(source, to, k):
        move = pltpu.make_async_copy(source, to, local_sem.at[k])
        move.start()
        return move

    def quarter(ref, j):
        return ref.at[pl.ds(256 * j, 256), :]

    def place(ref, j):
        row, column = lax.rem(j, 2) * 256, lax.div(j, 2) * 1024
        return ref.at[pl.ds(pl.multiple_of(row, 256), 256), pl.ds(pl.multiple_of(column, 1024), 1024)]

    p = Spot()
    own = pl.multiple_of(p.head * ROWS, ROWS)
    loads = [load(one, full, k) for k, (one, full) in enumerate(((wg_in, wg), (hn_in, hn), (wu_in, wu), (wd_in, wd), (dy_in, dy)))]
    late = [load(hid.at[pl.ds(own, ROWS), :], hid_rows, 5), load(raw_in, raw, 6)]
    greet(p.chips() + [p.sibling] + p.heads())
    for move in loads:
        move.wait()
    for low, high in ((0, 256), (256, 512), (512, FFH)):
        gate = mm(hn[...], wg[low:high, :], NT)
        up = mm(hn[...], wu[low:high, :], NT)
        dh = mm(dy[...], wd[low:high, :], NT)
        s = sigmoid(gate)
        silu = gate * s
        hidden[:, low:high] = (silu * up).astype(BF16)
        dg[:, low:high] = (dh * up * slope(gate, s)).astype(BF16)
        du[:, low:high] = (dh * silu).astype(BF16)

    @pl.loop(0, 8)
    def _(j):
        columns = pl.ds(pl.multiple_of(j * 256, 256), 256)
        ps[:, columns] = (mm(dg[...], wg[:, columns], NN) + mm(du[...], wu[:, columns], NN)).astype(BF16)

    scatter = HeadSum(p, ps, slots, rs_s, rs_r)
    scatter.send()
    sums = [
        DpSum(p, FFH, a0, a1, a2, a3, a4, a5, a6),
        DpSum(p, FFH, b0, b1, b2, b3, b4, b5, b6),
        DpSum(p, FFH, c0, c1, c2, c3, c4, c5, c6),
    ]
    dg_t[...] = dg[...].T
    products(dg_t, hn, a0)
    sums[0].to_sibling()
    du_t[...] = du[...].T
    products(du_t, hn, b0)
    sums[0].to_z()
    sums[1].to_sibling()
    hidden_t[...] = hidden[...].T
    products(hidden_t, dy, c0)
    sums[1].to_z()
    sums[2].to_sibling()

    @pl.loop(0, 8)
    def _(j):
        columns = pl.ds(pl.multiple_of(j * 256, 256), 256)
        wu[0:TOK, columns] = mm(hidden[...], wd[:, columns], NN).astype(BF16)

    sums[2].to_z()
    late.append(load(xn_in, hn, 7))
    late += [load(quarter(w_in, j), place(wd, j), 8 + j) for j in range(4)]
    scatter.collect()
    ffn_terms[...] = jnp.zeros_like(ffn_terms)

    @pl.loop(0, 4)
    def _(i):
        rows = pl.ds(pl.multiple_of(i * 16, 16), 16)
        here = pl.ds(pl.multiple_of(own + i * 16, 16), 16)
        grad, x = scatter.rows(i * 16, 16), resid[rows, :]
        inverse = lax.rsqrt(jnp.mean(x * x, axis=-1, keepdims=True) + EPS)
        scaled, normed = grad * ffn_gain[...], x * inverse
        back = inverse * (scaled - normed * jnp.mean(scaled * normed, axis=-1, keepdims=True))
        ffn_terms[...] += jnp.sum(grad * normed, axis=0, keepdims=True)
        both = dy[here, :].astype(F32) + back
        d_resid[rows, :] = both
        db[here, :] = both.astype(BF16)

    spread = HeadGather(p, db, ag_s, ag_r)
    spread.send()
    late += [load(quarter(w_in, 4 + j), place(dy, j), 12 + j) for j in range(4)]
    segments = Segments(p, seq)
    soft, picked, bound = lower_bound(lb, layer[0])
    group_total[...] = jnp.zeros_like(group_total)
    scatter.finish()
    gated_t[...] = gated[...].T
    for move in late:
        move.wait()
    spread.collect()
    scatter1 = HeadSum(p, wu, wg, rs1_s, rs1_r)
    scatter1.send()

    @pl.loop(0, CHUNKS)
    def _(c):
        rows = pl.ds(pl.multiple_of(c * CHUNK, CHUNK), CHUNK)
        d_gated = mm(db[rows, :], wt[...], NT)
        before, final = segments.before(c), segments.final(c)
        carried = jnp.where(segments.column(c) == before, 1.0, 0.0)
        running = run[rows, :]
        rate = jnp.exp(running[127:128]) * jnp.where(final == before, 1.0, 0.0)
        decay[c] = jnp.broadcast_to(rate, (8, HERE))
        for h in range(2):
            lanes = slice(h * 128, (h + 1) * 128)
            x, grad = mixed[rows, lanes], d_gated[:, lanes]
            gate = raw[rows, 768 + h * 128 : 768 + (h + 1) * 128]
            s = sigmoid(gate)
            inverse = lax.rsqrt(jnp.mean(x * x, axis=-1, keepdims=True) + EPS)
            normed = x * inverse
            draw[rows, 768 + h * 128 : 768 + (h + 1) * 128] = (
                grad * (normed * group_gain[...]) * slope(gate, s)
            ).astype(BF16)
            inner = grad * (gate * s)
            scaled = inner * group_gain[...]
            back = inverse * (scaled - normed * jnp.mean(scaled * normed, axis=-1, keepdims=True))
            group_total[...] += jnp.sum(inner * normed, axis=0, keepdims=True)
            back = back.astype(BF16)
            d_mixed[rows, lanes] = back
            query_raw = raw[rows, lanes]
            query = (query_raw * sigmoid(query_raw)).astype(BF16).astype(F32)
            high, low = halves(query * jnp.exp(running[:, lanes]) * carried)
            back_update[h, c] = mm(back, high, TN) + mm(back, low, TN)

    for h in range(2):
        lanes = slice(h * 128, (h + 1) * 128)
        state, rate = back_update[h, CHUNKS - 1], decay[CHUNKS - 1, 0:1, lanes]
        for c in range(CHUNKS - 2, -1, -1):
            state = state * decay[c, 0:1, lanes] + back_update[h, c]
            rate = rate * decay[c, 0:1, lanes]
        msg[h, 0:128, :] = state
        msg[h, 128:136, :] = jnp.broadcast_to(rate, (8, 128))
    exchange = Exchange(p, msg, sib, slots3, give, take, ex_send, ex_recv, True)
    exchange.to_sibling()
    results = (out_gate, out_up, out_down)
    for one, out in zip(sums, results):
        one.to_x(write(out))
    exchange.to_chips()

    @pl.loop(0, CHUNKS)
    def _(c):
        rows = pl.ds(pl.multiple_of(c * CHUNK, CHUNK), CHUNK)
        running = run[rows, :]
        middle = running[63:64]
        _, _, query, keys, values = gates(raw, bound, rows)
        up, down_ = jnp.exp(running - middle), jnp.exp(middle - running)
        lifted = query.astype(F32) * up
        lowered = keys.astype(F32) * down_
        column, row = segments.column(c), segments.row(c)
        carried = jnp.where(column == segments.before(c), 1.0, 0.0)
        linked = (column == row) & (
            lax.broadcasted_iota(jnp.int32, (CHUNK, CHUNK), 0)
            >= lax.broadcasted_iota(jnp.int32, (CHUNK, CHUNK), 1)
        )
        for h in range(2):
            lanes = slice(h * 128, (h + 1) * 128)
            lift, lower = halves(lifted[:, lanes]), halves(lowered[:, lanes])
            scores = halves(jnp.where(linked, mm3(lift, lower, NT), 0.0))
            grad = d_mixed[rows, lanes]
            d_scores = halves(jnp.where(linked, mm(grad, values[:, lanes], NT), 0.0))
            d_values[rows, lanes] = mm(scores[0], grad, TN) + mm(scores[1], grad, TN)
            state = halves(states[h, c])
            outer = mm(grad, state[0], NN) + mm(grad, state[1], NN)
            d_query[rows, lanes] = mm3(d_scores, lower, NN) * up[:, lanes] + outer * jnp.exp(running[:, lanes]) * carried
            d_keys[rows, lanes] = mm3(d_scores, lift, TN) * down_[:, lanes]

    for one, out in zip(sums, results):
        one.end(accumulate(out))
    third = DpSum(p, HERE, e0, e1, e2, e3, e4, e5, e6)
    products(gated_t, db, e0)
    third.to_sibling()
    exchange.result(incoming)
    third.to_z()
    bound_total[...] = jnp.zeros_like(bound_total)

    @pl.loop(0, CHUNKS)
    def _(i):
        c = CHUNKS - 1 - i
        rows = pl.ds(pl.multiple_of(c * CHUNK, CHUNK), CHUNK)
        running = run[rows, :]
        logistic, forget, query, keys, values = gates(raw, bound, rows)
        keys = keys.astype(F32)
        fade = jnp.exp(running[127:128] - running)
        column, final = segments.column(c), segments.final(c)
        ends = jnp.where(column == final, 1.0, 0.0)
        for h in range(2):
            lanes = slice(h * 128, (h + 1) * 128)
            state = incoming[h]
            pair = halves(state)
            tail = halves(keys[:, lanes] * fade[:, lanes] * ends)
            value_grad = d_values[rows, lanes] + mm3(tail, pair, NT)
            draw[rows, 512 + h * 128 : 512 + (h + 1) * 128] = value_grad.astype(BF16)
            lift = mm(values[:, lanes], pair[0], NN) + mm(values[:, lanes], pair[1], NN)
            key_grad = d_keys[rows, lanes] + lift * fade[:, lanes] * ends
            at_end = jnp.sum(states[h, c + 1] * state, axis=0, keepdims=True)
            query_grad = d_query[rows, lanes]
            step = query[:, lanes].astype(F32) * query_grad - keys[:, lanes] * key_grad
            log_grad = summed_rows(False, step) + at_end
            forget_grad = log_grad / forget[:, lanes] - key_grad
            rest = 1.0 - logistic[:, lanes]
            draw[rows, 256 + h * 128 : 256 + (h + 1) * 128] = (
                forget_grad * (1.0 - bound[:, lanes]) * logistic[:, lanes] * rest
            ).astype(BF16)
            bound_total[:, lanes] += jnp.sum(forget_grad * rest, axis=0, keepdims=True)
            query_raw = raw[rows, lanes]
            draw[rows, lanes] = (query_grad * slope(query_raw, sigmoid(query_raw))).astype(BF16)
            incoming[h] = state * decay[c, 0:1, lanes] + back_update[h, c]

    for first_column, part in ((0, wd), (1024, dy)):

        @pl.loop(0, 4)
        def _(j):
            columns = pl.ds(pl.multiple_of(first_column + j * 256, 256), 256)
            ps[:, columns] = mm(draw[...], place(part, j)[...], NT).astype(BF16)

    scatter2 = HeadSum(p, ps, slots, rs2_s, rs2_r)
    scatter2.send()
    for one in sums:
        one.finish()
    first = DpSum(p, 512, a0, a1, a2, f3, f4, f5, f6)
    second = DpSum(p, 512, b0, b1, b2, g3, g4, g5, g6)
    products_turned(hn, draw.at[:, 0:512], a0)
    first.to_sibling()
    products_turned(hn, draw.at[:, 512:1024], b0)
    first.to_z()
    second.to_sibling()
    scatter1.collect()

    @pl.loop(0, 4)
    def _(i):
        rows = pl.ds(pl.multiple_of(i * 16, 16), 16)
        block_out[rows, :] = (resid[rows, :] + scatter1.rows(i * 16, 16)).astype(BF16)

    second.to_z()
    third.to_x(write(out_output))
    scatter2.collect()
    norm_terms[...] = jnp.zeros_like(norm_terms)

    @pl.loop(0, 4)
    def _(i):
        rows = pl.ds(pl.multiple_of(i * 16, 16), 16)
        grad, x = scatter2.rows(i * 16, 16), hid_rows[rows, :].astype(F32)
        inverse = lax.rsqrt(jnp.mean(x * x, axis=-1, keepdims=True) + EPS)
        scaled, normed = grad * gain[...], x * inverse
        back = inverse * (scaled - normed * jnp.mean(scaled * normed, axis=-1, keepdims=True))
        norm_terms[...] += jnp.sum(grad * normed, axis=0, keepdims=True)
        grad_in[rows, :] = d_resid[rows, :] + back

    vec[...] = jnp.zeros_like(vec)
    for i in range(16):
        vec[i : i + 1, :] = norm_terms[:, i * 128 : (i + 1) * 128]
        vec[16 + i : 17 + i, :] = ffn_terms[:, i * 128 : (i + 1) * 128]
    vec[32:33, :] = group_total[...]
    vec[33:34, :] = total[:, 0:128] + total[:, 128:256]
    vec[34:35, :] = bound_total[:, 0:128]
    vec[35:36, :] = bound_total[:, 128:256]
    everywhere = Total(p, vec, t0, t1, t2, t3, t4, t5, t6, t7, t8.at[0], t9.at[0])
    everywhere.send()
    third.end(accumulate(out_output))
    everywhere.middle()

    def put_first(x):
        out_query[:, 0:128], out_query[:, 128:256] = x[0:128], x[128:256]
        out_forget[:, 0:128], out_forget[:, 128:256] = x[256:384], x[384:512]

    def put_second(x):
        out_input[:, 0:128], out_input[:, 128:256] = x[0:128], x[128:256]
        out_outgate[:, 0:128], out_outgate[:, 128:256] = x[256:384], x[384:512]

    def add_to(low, high):
        def add(x):
            low[:, 0:128] += x[0:128]
            low[:, 128:256] += x[128:256]
            high[:, 0:128] += x[256:384]
            high[:, 128:256] += x[384:512]

        return add

    first.to_x(put_first)
    second.to_x(put_second)
    all_of = everywhere.result()
    out_norm[...] = all_of[0:16]
    out_ffn[...] = all_of[16:32]
    out_group[...] = all_of[32:33]
    mean = jnp.sum(all_of[33:34], axis=-1, keepdims=True) / float(8192 * D)
    out_mean[...] = jnp.broadcast_to(mean, (1, 128))
    for h in range(2):
        lanes = slice(h * 128, (h + 1) * 128)
        out_bounds[:, lanes] = soft[:, lanes] * (picked[:, lanes] - bound[:, lanes]) * all_of[34 + h : 35 + h]
    first.end(add_to(out_query, out_forget))
    second.end(add_to(out_input, out_outgate))
    spread.finish()
    scatter1.finish()
    scatter2.finish()
    exchange.finish()
    everywhere.finish()
    for one in (first, second, third):
        one.finish()


OUTS = (
    ((ROWS, D), BF16),
    ((ROWS, D), F32),
    ((128, HERE), F32),
    ((128, HERE), F32),
    ((128, HERE), F32),
    ((128, HERE), F32),
    ((HERE, 128), F32),
    ((24, HERE), F32),
    ((16, 128), F32),
    ((1, KDIM), F32),
    ((16, 128), F32),
    ((1, 128), F32),
    ((FFH, 128), F32),
    ((FFH, 128), F32),
    ((FFH, 128), F32),
)


def call_backward(*arrays):
    sums = dp_sum_scratch(FFH)
    again = [pltpu.VMEM((512, 128), BF16)] * 2 + eight()
    return pl.pallas_call(
        backward,
        name="backward",
        out_shape=[jax.ShapeDtypeStruct(*one) for one in OUTS],
        in_specs=[HB, HB, HB, HB, HB, VM, VM, VM, HB, VM, VM, VM, VM, HB, HB, HB, VM, VM, VM, VM, SM, SM],
        out_specs=[VM] * len(OUTS),
        scratch_shapes=[
            *[pltpu.VMEM((TOK, D), BF16)] * 2,
            *[pltpu.VMEM((FFH, D), BF16)] * 3,
            *[pltpu.VMEM((TOK, FFH), BF16)] * 3,
            *[pltpu.VMEM((FFH, TOK), BF16)] * 3,
            pltpu.VMEM((HERE, TOK), BF16),
            *[pltpu.VMEM((TOK, D), BF16)] * 3,
            pltpu.VMEM((ROWS, D), F32),
            pltpu.VMEM((ROWS, D), BF16),
            pltpu.VMEM((TOK, 1024), F32),
            pltpu.VMEM((TOK, 1024), BF16),
            pltpu.VMEM((TOK, HERE), BF16),
            *[pltpu.VMEM((TOK, HERE), F32)] * 3,
            pltpu.VMEM((2, CHUNKS, 128, 128), F32),
            pltpu.VMEM((CHUNKS, 8, HERE), F32),
            pltpu.VMEM((2, 128, 128), F32),
            pltpu.VMEM((VEC, 128), F32),
            pltpu.VMEM((1, D), F32),
            pltpu.VMEM((1, D), F32),
            pltpu.VMEM((1, 128), F32),
            pltpu.VMEM((1, HERE), F32),
            *exchange_scratch(),
            *eight(),
            *eight(),
            *eight(),
            *eight(),
            *sums,
            *sums,
            *sums,
            *dp_sum_scratch(HERE),
            *again,
            *again,
            pltpu.VMEM((8, VEC, 128), F32),
            pltpu.VMEM((8, VEC, 128), F32),
            pltpu.VMEM((VEC, 128), F32),
            pltpu.VMEM((VEC, 128), F32),
            *eight(),
            *eight(),
            pltpu.SemaphoreType.DMA((1,)),
            pltpu.SemaphoreType.DMA((1,)),
            pltpu.SemaphoreType.DMA((16,)),
        ],
        compiler_params=pltpu.CompilerParams(
            collective_id=1, has_side_effects=True, vmem_limit_bytes=60 * 1024 * 1024
        ),
    )(*arrays)


def results(*refs):
    half = len(refs) // 2
    for one, out in zip(refs[:half], refs[half:]):
        out[...] = one[...]


def call_results(arrays):
    return pl.pallas_call(
        results,
        name="results",
        out_shape=[jax.ShapeDtypeStruct(*one) for one in OUTS],
        in_specs=[VM] * len(OUTS),
        out_specs=[VM] * len(OUTS),
    )(*arrays)


def local(
    hidden_in, norm_gain, w_query, w_forget, w_input, w_outgate, lower_bounds, layer_index, group_gain,
    w_output, ffn_gain, w_gate, w_up, w_down, seq_lengths, grad_out,
):
    norm_row, ffn_row, group_row = norm_gain.reshape(1, D), ffn_gain.reshape(1, D), group_gain.reshape(1, KDIM)
    raw, xn, gated, mixed, states, run, total, w_all, wt_all, hn, resid, wg, wu, wd = call_forward(
        hidden_in, norm_row, w_query, w_forget, w_input, w_outgate, w_output, lower_bounds, layer_index, seq_lengths,
        group_row, ffn_row, w_gate.T, w_up.T, w_down,
    )
    (
        block_out, grad_in, grad_query, grad_forget, grad_input, grad_outgate, grad_output, grad_bounds,
        grad_norm, grad_group, grad_ffn, mean, grad_gate, grad_up, grad_down,
    ) = call_results(call_backward(
        hn, grad_out, wg, wu, wd, resid, ffn_row, wt_all, raw, run, mixed, states, gated, xn, w_all, hidden_in,
        total, norm_row, group_row, lower_bounds, layer_index, seq_lengths,
    ))
    return (
        block_out,
        grad_in,
        grad_norm.reshape(D),
        grad_query,
        grad_forget,
        grad_input,
        grad_outgate,
        grad_bounds,
        grad_group.reshape(KDIM),
        grad_output,
        grad_ffn.reshape(D),
        grad_gate.T,
        grad_up.T,
        grad_down,
        mean[0, 0:1],
    )


def solution(mesh):
    return jax.shard_map(
        local,
        mesh=mesh,
        in_specs=(
            P("dp", None),
            P(),
            P("dp", "head"),
            P("dp", "head"),
            P("dp", "head"),
            P("dp", "head"),
            P(None, "head"),
            P(),
            P(),
            P("head", "dp"),
            P(),
            P("dp", "head"),
            P("dp", "head"),
            P("head", "dp"),
            P(),
            P("dp", None),
        ),
        out_specs=(
            P(("dp", "head"), None),
            P(("dp", "head"), None),
            P(),
            P("dp", "head"),
            P("dp", "head"),
            P("dp", "head"),
            P("dp", "head"),
            P(None, "head"),
            P(),
            P("head", "dp"),
            P(),
            P("dp", "head"),
            P("dp", "head"),
            P("head", "dp"),
            P(),
        ),
        check_vma=False,
    )
```

time: 326 us -> 287 us (0.88)
  Pallas kernels: 305 us -> 283 us
  local copies, waits for them, and re-layouts: 17.7 us -> 0 us
    pallas_call x4 -> x3, Pallas kernels: 305 us -> 283 us  [the longest x1 166 us: call_backward(): pl.pallas_call(backward, name='backward', out_shape=[jax.ShapeDtypeStruct...]
    unnamed x46 -> x0, local copies, waits for them, and re-layouts: 17.7 us -> none
where the time goes in v2:
time: 287 us; the launch traced here: 285 us
  Pallas kernels  283 us (99%)
    pallas_call x1, Pallas kernels, call_backward(): pl.pallas_call(backward, name='backward', out_shape=[jax.ShapeDtypeStruct...  166 us
    pallas_call x1, Pallas kernels, call_forward(): pl.pallas_call(forward, name='forward', out_shape=(out((TOK, 1024), F32),...  114 us

profile of v2, /device:TPU:1, one launch (start us, length us, event | category | flops | bytes accessed | tf_op | source)
XLA Modules:
  0.0 284.5 jit_solution(2235922943821972573)
XLA Ops:
  1.3 113.8 %forward.1 = (f32[512,1024]{1,0:T(8,128)}, bf16[512,2048]{1,0:T(8,128)(2,1)}, bf16[512,256]{1,0:T(8,128)(2,1)}, f32[512,256]{1,0:T(8,128)}, f32[2,5,128,128]{3,2...) custom-call(bf16[512,2048]{1,0:T(8,128)(2,1)} %hid.3, ...), custom_call_target="tpu_custom_call" | custom-call | tf_op jit(solution)/shard_map/forward/pallas_call | solution.py:692
  115.1 166.0 %backward.1 = (bf16[64,2048]{1,0:T(8,128)(2,1)}, f32[64,2048]{1,0:T(8,128)}, f32[128,256]{1,0:T(8,128)}, f32[128,256]{1,0:T(8,128)}, f32[128,256]{1,0:T(8,128)},...) custom-call(bf16[512,2048]{1,0:T(8,128)(2,1)} %get-tuple-element.59., ...), custom_call_target="tpu_custom_call" | custom-call | tf_op jit(solution)/shard_map/backward/pallas_call | solution.py:1070
  281.2 3.2 %results.1 = (bf16[64,2048]{1,0:T(8,128)(2,1)}, f32[64,2048]{1,0:T(8,128)}, f32[128,256]{1,0:T(8,128)}, f32[128,256]{1,0:T(8,128)}, f32[128,256]{1,0:T(8,128)}, ...) custom-call(bf16[64,2048]{1,0:T(8,128)(2,1)} %get-tuple-element.73.r, ...), custom_call_target="tpu_custom_call" | custom-call | tf_op jit(solution)/shard_map/results/pallas_call | solution.py:1131

commit v3 on v2

--- a/solution.py
+++ b/solution.py
@@ -34,9 +34,21 @@
         self.chip = lax.div(self.dp, 2)
         self.xh = lax.rem(self.chip, 2)
         self.z = lax.div(self.chip, 2)
+        self.xl = lax.rem(self.head, 2)
+        self.y = lax.div(self.head, 2)
 
     def at(self, dz, xh, core):
         return (lax.rem(self.z + dz, 4) * 2 + xh) * 2 + core
+
+    def y_at(self, k):
+        return lax.rem(self.y + k, 4)
+
+    @property
+    def beside(self):
+        return {"head": self.y * 2 + 1 - self.xl}
+
+    def lines(self):
+        return [self.beside] + [{"head": self.y_at(k) * 2 + self.xl} for k in (1, 2, 3)]
 
     @property
     def sibling(self):
@@ -299,64 +311,209 @@
     return logistic, forget, query, keys, values
 
 
-def eighth(ref, h):
-    return ref.at[pl.ds(pl.multiple_of(h * ROWS, ROWS), ROWS), :]
+HALF = D // 2
 
 
 class HeadSum:
     def __init__(self, spot, ps, slots, send, recv):
         self.p, self.ps, self.slots, self.s, self.r = spot, ps, slots, send, recv
 
+    def left_of(self, start, rows=ROWS):
+        return self.slots.at[pl.ds(start, rows), pl.ds(0, HALF)]
+
+    def right_of(self, start, rows=ROWS):
+        return self.slots.at[pl.ds(start, rows), pl.ds(HALF, HALF)]
+
+    def part(self, h, rows, right):
+        return self.ps.at[pl.ds(pl.multiple_of(h * ROWS, ROWS), rows), pl.ds(HALF if right else 0, HALF)]
+
+    def left_x(self, k):
+        p = self.p
+        h = p.y_at(k) * 2 + 1 - p.xl
+        return rcopy(self.part(h, ROWS, False), self.left_of(64 * k), self.s.at[k], self.r.at[k], p.beside)
+
+    def left_y(self, k):
+        p = self.p
+        to = {"head": p.y_at(k) * 2 + p.xl}
+        return rcopy(self.left_of(64 * k), self.left_of(192 + 64 * k), self.s.at[3 + k], self.r.at[3 + k], to)
+
+    def right_y(self, k):
+        p = self.p
+        to = {"head": p.y_at(k) * 2 + p.xl}
+        return rcopy(
+            self.part(p.y_at(k) * 2, 128, True), self.right_of(128 * k - 128, 128), self.s.at[6 + k], self.r.at[6 + k], to
+        )
+
+    def right_x(self):
+        return rcopy(self.right_of(384), self.right_of(448), self.s.at[10], self.r.at[10], self.p.beside)
+
+    def send_left(self):
+        for k in (2, 1, 3, 0):
+            self.left_x(k).start()
+
+    def send_right(self):
+        for k in (2, 1, 3):
+            self.right_y(k).start()
+
     def send(self):
-        p = self.p
-        for k in range(1, NHEAD):
-            h = lax.rem(p.head + k, NHEAD)
-            rcopy(eighth(self.ps, h), eighth(self.slots, p.head), self.s.at[k], self.r.at[p.head], {"head": h}).start()
+        self.send_right()
+        self.send_left()
+
+    def middle(self):
+        p = self.p
+        for k in (2, 1, 3, 0):
+            self.left_x(k).wait_recv()
+            mine = self.part(p.y_at(k) * 2 + p.xl, ROWS, False)
+            one = self.left_of(64 * k)
+            one[...] = (one[...].astype(F32) + mine[...].astype(F32)).astype(BF16)
+            if k:
+                self.left_y(k).start()
+        for k in (1, 3, 2):
+            self.right_y(k).wait_recv()
+
+        def total(xl):
+            one = self.part(p.y * 2 + xl, ROWS, True)[...].astype(F32)
+            for k in range(3):
+                rows = pl.ds(pl.multiple_of(128 * k + xl * ROWS, ROWS), ROWS)
+                one = one + self.slots[rows, HALF:].astype(F32)
+            return one.astype(BF16)
+
+        self.slots[384:448, HALF:] = total(1 - p.xl)
+        self.right_x().start()
+        self.slots[448:512, 0:HALF] = total(p.xl)
 
     def collect(self):
-        p = self.p
-        mine = pl.ds(pl.multiple_of(p.head * ROWS, ROWS), ROWS)
-        self.slots[mine, :] = self.ps[mine, :]
-        for k in range(1, NHEAD):
-            h = lax.rem(p.head + k, NHEAD)
-            one = eighth(self.slots, h)
-            rcopy(one, one, self.s.at[0], self.r.at[h], p.sibling).wait_recv()
+        for k in (1, 3, 2):
+            self.left_y(k).wait_recv()
+        self.right_x().wait_recv()
 
     def rows(self, start, count):
-        total = None
-        for h in range(NHEAD):
-            one = self.slots[pl.ds(pl.multiple_of(h * ROWS + start, 16), count), :].astype(F32)
-            total = one if total is None else total + one
-        return total
+        def at(row, left):
+            rows = pl.ds(pl.multiple_of(row + start, 16), count)
+            return self.slots[rows, 0:HALF].astype(F32) if left else self.slots[rows, HALF:].astype(F32)
+
+        left = (at(0, True) + at(256, True)) + (at(320, True) + at(384, True))
+        return jnp.concatenate([left, at(448, True) + at(448, False)], axis=1)
 
     def finish(self):
-        for k in range(1, NHEAD):
-            one = eighth(self.ps, 0)
-            rcopy(one, one, self.s.at[k], self.r.at[0], self.p.sibling).wait_send()
+        for k in range(4):
+            self.left_x(k).wait_send()
+        for k in (1, 2, 3):
+            self.left_y(k).wait_send()
+            self.right_y(k).wait_send()
+        self.right_x().wait_send()
+
+
+class LateHeadSum:
+    def __init__(self, spot, ps, slots, send, recv):
+        self.p, self.ps, self.slots, self.s, self.r = spot, ps, slots, send, recv
+
+    def block(self, ref, start, rows=ROWS):
+        return ref.at[pl.ds(pl.multiple_of(start, ROWS), rows), :]
+
+    def along_y(self, k):
+        p = self.p
+        y = p.y_at(k)
+        return rcopy(
+            self.block(self.ps, y * 128, 128), self.block(self.slots, 128 * k - 128, 128),
+            self.s.at[k], self.r.at[k], {"head": y * 2 + p.xl},
+        )
+
+    def along_x(self):
+        return rcopy(self.block(self.slots, 384), self.block(self.slots, 448), self.s.at[0], self.r.at[0], self.p.beside)
+
+    def send(self):
+        for k in (2, 1, 3):
+            self.along_y(k).start()
+
+    def part(self, xl, start, count):
+        p = self.p
+        one = self.ps[pl.ds(pl.multiple_of((p.y * 2 + xl) * ROWS + start, 16), count), :].astype(F32)
+        for k in range(3):
+            rows = pl.ds(pl.multiple_of(128 * k + xl * ROWS + start, 16), count)
+            one = one + self.slots[rows, :].astype(F32)
+        return one
+
+    def middle(self):
+        for k in (1, 3, 2):
+            self.along_y(k).wait_recv()
+
+        @pl.loop(0, 4)
+        def _(i):
+            rows = pl.ds(pl.multiple_of(384 + i * 16, 16), 16)
+            self.slots[rows, :] = self.part(1 - self.p.xl, i * 16, 16).astype(BF16)
+
+        self.along_x().start()
+
+    def collect(self):
+        self.along_x().wait_recv()
+
+    def rows(self, start, count):
+        rows = pl.ds(pl.multiple_of(448 + start, 16), count)
+        return self.part(self.p.xl, start, count) + self.slots[rows, :].astype(F32)
+
+    def finish(self):
+        for k in (1, 2, 3):
+            self.along_y(k).wait_send()
+        self.along_x().wait_send()
 
 
 class HeadGather:
     def __init__(self, spot, full, send, recv):
         self.p, self.full, self.s, self.r = spot, full, send, recv
 
-    def block(self, h):
-        return self.full.at[pl.ds(pl.multiple_of(h * ROWS, ROWS), ROWS), :]
+    def block(self, h, right):
+        return self.full.at[pl.ds(pl.multiple_of(h * ROWS, ROWS), ROWS), pl.ds(HALF if right else 0, HALF)]
+
+    def along_y(self, k, xl, right, i):
+        p = self.p
+        b = self.block(p.y * 2 + xl, right)
+        return rcopy(b, b, self.s.at[i + k], self.r.at[i + k], {"head": p.y_at(k) * 2 + p.xl})
+
+    def beside(self, k, right, i):
+        p = self.p
+        b = self.block(p.y_at(k) * 2 + p.xl, right)
+        return rcopy(b, b, self.s.at[i + k], self.r.at[i + k], p.beside)
 
     def send(self):
         p = self.p
-        for k in range(1, NHEAD):
-            h = lax.rem(p.head + k, NHEAD)
-            rcopy(self.block(p.head), self.block(p.head), self.s.at[k], self.r.at[p.head], {"head": h}).start()
+        self.beside(0, False, 0).start()
+        for k in (2, 1, 3):
+            self.along_y(k, p.xl, True, 0).start()
+        self.beside(0, True, 4).start()
+        for k in (2, 1, 3):
+            self.along_y(k, p.xl, False, 8).start()
+
+    def middle(self):
+        p = self.p
+        self.beside(0, False, 0).wait_recv()
+        for k in (2, 1, 3):
+            self.along_y(k, 1 - p.xl, False, 11).start()
+        for k in (1, 3, 2):
+            self.along_y(4 - k, p.xl, True, 0).wait_recv()
+            self.beside(k, True, 4).start()
 
     def collect(self):
         p = self.p
-        for k in range(1, NHEAD):
-            h = lax.rem(p.head + k, NHEAD)
-            rcopy(self.block(h), self.block(h), self.s.at[0], self.r.at[h], p.sibling).wait_recv()
+        self.beside(0, True, 4).wait_recv()
+        for k in (1, 3, 2):
+            self.along_y(k, p.xl, False, 8).wait_recv()
+            self.along_y(k, 1 - p.xl, False, 11).wait_recv()
+            self.beside(k, True, 4).wait_recv()
 
     def finish(self):
-        for k in range(1, NHEAD):
-            rcopy(self.block(0), self.block(0), self.s.at[k], self.r.at[0], self.p.sibling).wait_send()
+        p = self.p
+        self.beside(0, False, 0).wait_send()
+        for k in range(4):
+            self.beside(k, True, 4).wait_send()
+        for k in (1, 2, 3):
+            self.along_y(k, p.xl, True, 0).wait_send()
+            self.along_y(k, p.xl, False, 8).wait_send()
+            self.along_y(k, 1 - p.xl, False, 11).wait_send()
+
+
+def sixteen():
+    return [pltpu.SemaphoreType.DMA((16,)), pltpu.SemaphoreType.DMA((16,))]
 
 
 def eight():
@@ -379,11 +536,24 @@
         for i in range(4):
             self.pair(i).start()
 
-    def across(self, d):
-        p = self.p
-        z = lax.rem(p.z + d, 4)
-        where = {"dp": (z * 2 + p.xh) * 2 + p.core}
-        return rcopy(self.gs.at[p.core, pl.ds(z * 2, 2)], self.zr.at[d - 1], self.s.at[3 + d], self.r.at[3 + d], where)
+    def half(self, part):
+        return pl.ds(part * (self.rows // 2), self.rows // 2)
+
+    def along_z(self, d, block, part, slot, i):
+        p = self.p
+        z = lax.rem(p.z + block, 4)
+        where = {"dp": (lax.rem(p.z + d, 4) * 2 + p.xh) * 2 + p.core}
+        source = self.gs.at[p.core, pl.ds(z * 2, 2), self.half(part), :]
+        return rcopy(source, self.zr.at[slot, :, self.half(part), :], self.s.at[4 + i], self.r.at[4 + i], where)
+
+    def far(self, part):
+        return self.along_z(3 if part else 1, 2, part, 2, part)
+
+    def near(self, part):
+        return self.along_z(3, 3, 0, 1, 2) if part else self.along_z(1, 1, 1, 0, 3)
+
+    def joined(self, part):
+        return self.along_z(3, 3, 1, 1, 4) if part else self.along_z(1, 1, 0, 0, 5)
 
     def to_z(self):
         p = self.p
@@ -394,22 +564,36 @@
         def _(k):
             self.gs[p.core, k] = (self.gs[p.core, k].astype(F32) + self.cr[k].astype(F32)).astype(BF16)
 
-        for d in (1, 3, 2):
-            self.across(d).start()
+        for part in range(2):
+            self.far(part).start()
+        for part in range(2):
+            self.near(part).start()
+
+    def join(self):
+        p = self.p
+        for part in range(2):
+            self.far(part).wait_recv()
+            z = lax.rem(p.z + (3 if part else 1), 4)
+            for h in range(2):
+                mine = self.gs.at[p.core, z * 2 + h, self.half(part), :]
+                other = self.zr.at[2, h, self.half(part), :]
+                mine[...] = (mine[...].astype(F32) + other[...].astype(F32)).astype(BF16)
+            self.joined(part).start()
 
     def last_move(self):
         p = self.p
         where = {"dp": (p.z * 2 + 1 - p.xh) * 2 + p.core}
-        return rcopy(self.xs, self.xr, self.s.at[7], self.r.at[7], where)
+        return rcopy(self.xs, self.xr, self.s.at[10], self.r.at[10], where)
 
     def to_x(self, put):
         p = self.p
-        for d in (1, 3, 2):
-            self.across(d).wait_recv()
+        for part in range(2):
+            self.near(part).wait_recv()
+            self.joined(part).wait_recv()
 
         def total(h):
             one = self.gs[p.core, 2 * p.z + h].astype(F32)
-            for i in range(3):
+            for i in range(2):
                 one = one + self.zr[i, h].astype(F32)
             return one
 
@@ -424,8 +608,10 @@
     def finish(self):
         for i in range(4):
             self.pair(i).wait_send()
-        for d in (1, 3, 2):
-            self.across(d).wait_send()
+        for part in range(2):
+            self.far(part).wait_send()
+            self.near(part).wait_send()
+            self.joined(part).wait_send()
         self.last_move().wait_send()
 
 
@@ -436,7 +622,7 @@
         pltpu.VMEM((3, 2, rows, 128), BF16),
         pltpu.VMEM((rows, 128), BF16),
         pltpu.VMEM((rows, 128), BF16),
-        *eight(),
+        *sixteen(),
     ]
 
 
@@ -535,7 +721,7 @@
     mine = pl.ds(pl.multiple_of(p.dp * 128, 128), 128)
     for k, one in enumerate((wq, wf, wi, wo)):
         w[mine, 256 * k : 256 * (k + 1)] = one[...]
-    greet(p.chips() + [p.sibling] + p.heads())
+    greet(p.chips() + [p.sibling] + p.lines())
     gather = Gather(p, w, ws, wr, wh)
     gather.first()
     wt[:, mine] = w_output[...]
@@ -650,15 +836,18 @@
     later.last()
     keep(wt, wt_out)
 
-    @pl.loop(0, 8)
-    def _(j):
-        columns = pl.ds(pl.multiple_of(j * 256, 256), 256)
-        ps[:, columns] = mm(gated[...], wt[:, columns], NN).astype(BF16)
-
     scatter = HeadSum(p, ps, slots, rs_s, rs_r)
-    scatter.send()
+    for start, send in ((HALF, scatter.send_right), (0, scatter.send_left)):
+
+        @pl.loop(0, 4)
+        def _(j):
+            columns = pl.ds(pl.multiple_of(start + j * 256, 256), 256)
+            ps[:, columns] = mm(gated[...], wt[:, columns], NN).astype(BF16)
+
+        send()
     for g in gathers:
         g.third()
+    scatter.middle()
     for g in gathers:
         g.fourth()
     scatter.collect()
@@ -675,6 +864,7 @@
 
     spread = HeadGather(p, hn, ag_s, ag_r)
     spread.send()
+    spread.middle()
     for g, full, out in zip(gathers, (g0, g1, g2), (wg_out, wu_out, wd_out)):
         g.last()
         keep(full, out)
@@ -720,8 +910,8 @@
             pltpu.VMEM((CHUNKS, 8, HERE), F32),
             pltpu.VMEM((2, 128, 128), F32),
             *exchange_scratch(),
-            *eight(),
-            *eight(),
+            *sixteen(),
+            *sixteen(),
             *gather_semaphores(),
             *gather_semaphores(),
             *gather_semaphores(),
@@ -777,13 +967,15 @@
         dg[:, low:high] = (dh * up * slope(gate, s)).astype(BF16)
         du[:, low:high] = (dh * silu).astype(BF16)
 
-    @pl.loop(0, 8)
-    def _(j):
-        columns = pl.ds(pl.multiple_of(j * 256, 256), 256)
-        ps[:, columns] = (mm(dg[...], wg[:, columns], NN) + mm(du[...], wu[:, columns], NN)).astype(BF16)
-
     scatter = HeadSum(p, ps, slots, rs_s, rs_r)
-    scatter.send()
+    for start, send in ((HALF, scatter.send_right), (0, scatter.send_left)):
+
+        @pl.loop(0, 4)
+        def _(j):
+            columns = pl.ds(pl.multiple_of(start + j * 256, 256), 256)
+            ps[:, columns] = (mm(dg[...], wg[:, columns], NN) + mm(du[...], wu[:, columns], NN)).astype(BF16)
+
+        send()
     sums = [
         DpSum(p, FFH, a0, a1, a2, a3, a4, a5, a6),
         DpSum(p, FFH, b0, b1, b2, b3, b4, b5, b6),
@@ -796,10 +988,12 @@
     products(du_t, hn, b0)
     sums[0].to_z()
     sums[1].to_sibling()
+    scatter.middle()
     hidden_t[...] = hidden[...].T
     products(hidden_t, dy, c0)
     sums[1].to_z()
     sums[2].to_sibling()
+    sums[0].join()
 
     @pl.loop(0, 8)
     def _(j):
@@ -825,18 +1019,21 @@
         d_resid[rows, :] = both
         db[here, :] = both.astype(BF16)
 
+    scatter.finish()
     spread = HeadGather(p, db, ag_s, ag_r)
     spread.send()
+    spread.middle()
+    sums[1].join()
     late += [load(quarter(w_in, 4 + j), place(dy, j), 12 + j) for j in range(4)]
     segments = Segments(p, seq)
     soft, picked, bound = lower_bound(lb, layer[0])
     group_total[...] = jnp.zeros_like(group_total)
-    scatter.finish()
     gated_t[...] = gated[...].T
     for move in late:
         move.wait()
+    sums[2].join()
     spread.collect()
-    scatter1 = HeadSum(p, wu, wg, rs1_s, rs1_r)
+    scatter1 = LateHeadSum(p, wu, wg, rs1_s, rs1_r)
     scatter1.send()
 
     @pl.loop(0, CHUNKS)
@@ -918,6 +1115,7 @@
     third.to_sibling()
     exchange.result(incoming)
     third.to_z()
+    third.join()
     bound_total[...] = jnp.zeros_like(bound_total)
 
     @pl.loop(0, CHUNKS)
@@ -953,15 +1151,15 @@
             draw[rows, lanes] = (query_grad * slope(query_raw, sigmoid(query_raw))).astype(BF16)
             incoming[h] = state * decay[c, 0:1, lanes] + back_update[h, c]
 
-    for first_column, part in ((0, wd), (1024, dy)):
+    scatter2 = HeadSum(p, ps, slots, rs2_s, rs2_r)
+    for start, part, send in ((HALF, dy, scatter2.send_right), (0, wd, scatter2.send_left)):
 
         @pl.loop(0, 4)
         def _(j):
-            columns = pl.ds(pl.multiple_of(first_column + j * 256, 256), 256)
+            columns = pl.ds(pl.multiple_of(start + j * 256, 256), 256)
             ps[:, columns] = mm(draw[...], place(part, j)[...], NT).astype(BF16)
 
-    scatter2 = HeadSum(p, ps, slots, rs2_s, rs2_r)
-    scatter2.send()
+        send()
     for one in sums:
         one.finish()
     first = DpSum(p, 512, a0, a1, a2, f3, f4, f5, f6)
@@ -971,6 +1169,9 @@
     products_turned(hn, draw.at[:, 512:1024], b0)
     first.to_z()
     second.to_sibling()
+    scatter1.middle()
+    scatter2.middle()
+    second.to_z()
     scatter1.collect()
 
     @pl.loop(0, 4)
@@ -978,7 +1179,7 @@
         rows = pl.ds(pl.multiple_of(i * 16, 16), 16)
         block_out[rows, :] = (resid[rows, :] + scatter1.rows(i * 16, 16)).astype(BF16)
 
-    second.to_z()
+    first.join()
     third.to_x(write(out_output))
     scatter2.collect()
     norm_terms[...] = jnp.zeros_like(norm_terms)
@@ -1003,6 +1204,7 @@
     vec[35:36, :] = bound_total[:, 128:256]
     everywhere = Total(p, vec, t0, t1, t2, t3, t4, t5, t6, t7, t8.at[0], t9.at[0])
     everywhere.send()
+    second.join()
     third.end(accumulate(out_output))
     everywhere.middle()
 
@@ -1066,7 +1268,7 @@
 
 def call_backward(*arrays):
     sums = dp_sum_scratch(FFH)
-    again = [pltpu.VMEM((512, 128), BF16)] * 2 + eight()
+    again = [pltpu.VMEM((512, 128), BF16)] * 2 + sixteen()
     return pl.pallas_call(
         backward,
         name="backward",
@@ -1095,10 +1297,10 @@
             pltpu.VMEM((1, 128), F32),
             pltpu.VMEM((1, HERE), F32),
             *exchange_scratch(),
+            *sixteen(),
+            *sixteen(),
             *eight(),
-            *eight(),
-            *eight(),
-            *eight(),
+            *sixteen(),
             *sums,
             *sums,
             *sums,

time: 287 us -> 246 us (0.86)
  Pallas kernels: 283 us -> 245 us
    pallas_call x1, Pallas kernels: 166 us -> 135 us  [call_backward(): pl.pallas_call(backward, name='backward', out_shape=[jax.ShapeDtypeStruct...]
    pallas_call x1, Pallas kernels: 114 us -> 107 us  [call_forward(): pl.pallas_call(forward, name='forward', out_shape=(out((TOK, 1024), F32),...]
where the time goes in v3:
time: 246 us
  Pallas kernels  245 us (100%)
    pallas_call x1, Pallas kernels, call_backward(): pl.pallas_call(backward, name='backward', out_shape=[jax.ShapeDtypeStruct...  135 us
    pallas_call x1, Pallas kernels, call_forward(): pl.pallas_call(forward, name='forward', out_shape=(out((TOK, 1024), F32),...  107 us

profile of v3, /device:TPU:1, one launch (start us, length us, event | category | flops | bytes accessed | tf_op | source)
XLA Modules:
  0.0 246.2 jit_solution(7506872991808149903)
XLA Ops:
  1.3 106.5 %forward.1 = (f32[512,1024]{1,0:T(8,128)}, bf16[512,2048]{1,0:T(8,128)(2,1)}, bf16[512,256]{1,0:T(8,128)(2,1)}, f32[512,256]{1,0:T(8,128)}, f32[2,5,128,128]{3,2...) custom-call(bf16[512,2048]{1,0:T(8,128)(2,1)} %hid.3, ...), custom_call_target="tpu_custom_call" | custom-call | tf_op jit(solution)/shard_map/forward/pallas_call | solution.py:882
  107.8 134.9 %backward.1 = (bf16[64,2048]{1,0:T(8,128)(2,1)}, f32[64,2048]{1,0:T(8,128)}, f32[128,256]{1,0:T(8,128)}, f32[128,256]{1,0:T(8,128)}, f32[128,256]{1,0:T(8,128)},...) custom-call(bf16[512,2048]{1,0:T(8,128)(2,1)} %get-tuple-element.59., ...), custom_call_target="tpu_custom_call" | custom-call | tf_op jit(solution)/shard_map/backward/pallas_call | solution.py:1272
  242.8 3.2 %results.1 = (bf16[64,2048]{1,0:T(8,128)(2,1)}, f32[64,2048]{1,0:T(8,128)}, f32[128,256]{1,0:T(8,128)}, f32[128,256]{1,0:T(8,128)}, f32[128,256]{1,0:T(8,128)}, ...) custom-call(bf16[64,2048]{1,0:T(8,128)(2,1)} %get-tuple-element.73.r, ...), custom_call_target="tpu_custom_call" | custom-call | tf_op jit(solution)/shard_map/results/pallas_call | solution.py:1333

commit v4 on v3

--- a/solution.py
+++ b/solution.py
@@ -65,7 +65,7 @@
     barrier = pltpu.get_barrier_semaphore()
     for one in ids:
         pl.semaphore_signal(barrier, inc=1, device_id=one, device_id_type=MESH)
-    pl.semaphore_wait(barrier, len(ids))
+    return lambda: pl.semaphore_wait(barrier, len(ids))
 
 
 def rcopy(src, dst, send, recv, where):
@@ -257,8 +257,10 @@
         near, far = (two, one) if self.back else (one, two)
         self.near = near
         state = near[0:128] * far[128:129] + far[0:128]
-        self.slots[p.chip, 0:128, :] = state
-        self.slots[p.chip, 128:136, :] = near[128:136] * far[128:136]
+        rate = near[128:136] * far[128:136]
+        high = rate.astype(BF16).astype(F32)
+        self.slots[p.chip, 0:128, :] = state.astype(BF16)
+        self.slots[p.chip, 128:144, :] = jnp.concatenate([high, rate - high], axis=0).astype(BF16)
         for k, to in enumerate(p.chips()):
             rcopy(self.slots.at[p.chip], self.slots.at[p.chip], self.s.at[k], self.r.at[p.chip], to).start()
 
@@ -269,8 +271,8 @@
             rcopy(self.slots.at[chip], self.slots.at[chip], self.s.at[0], self.r.at[chip], p.sibling).wait_recv()
         state = jnp.zeros((128, 128), F32)
         for k in range(7, 0, -1) if self.back else range(7):
-            m = self.slots[k]
-            after = state * m[128:129] + m[0:128]
+            m = self.slots[k].astype(F32)
+            after = state * (m[128:129] + m[136:137]) + m[0:128]
             state = jnp.where(k > p.chip if self.back else k < p.chip, after, state)
         second = state * self.near[128:129] + self.near[0:128]
         is_first = p.core == (1 if self.back else 0)
@@ -293,7 +295,7 @@
     return [
         pltpu.VMEM((2, 136, 128), F32),
         pltpu.VMEM((136, 128), F32),
-        pltpu.VMEM((8, 136, 128), F32),
+        pltpu.VMEM((8, 144, 128), BF16),
         pltpu.VMEM((128, 128), F32),
         pltpu.VMEM((128, 128), F32),
         pltpu.SemaphoreType.DMA((9,)),
@@ -635,14 +637,16 @@
         gs[1, k] = both[:, 128:256]
 
 
-def products_turned(left, right, gs):
+def products_turned(left, first, second, gs):
     @pl.loop(0, 8)
     def _(k):
-        columns = pl.ds(pl.multiple_of(k * 256, 256), 256)
-        both = mm(left[:, columns], right[...], TN).astype(BF16)
-        for q in range(4):
-            gs[0, k, 128 * q : 128 * (q + 1), :] = both[0:128, 128 * q : 128 * (q + 1)]
-            gs[1, k, 128 * q : 128 * (q + 1), :] = both[128:256, 128 * q : 128 * (q + 1)]
+        turned = left[:, pl.ds(pl.multiple_of(k * 256, 256), 256)]
+        for i, right in enumerate((first, second)):
+            both = mm(turned, right[...], TN).astype(BF16)
+            for q in range(2):
+                rows = slice(256 * i + 128 * q, 256 * i + 128 * (q + 1))
+                gs[0, k, rows, :] = both[0:128, 128 * q : 128 * (q + 1)]
+                gs[1, k, rows, :] = both[128:256, 128 * q : 128 * (q + 1)]
 
 
 def write(ref):
@@ -669,12 +673,30 @@
 
     def send(self):
         p = self.p
-        self.hs[p.head] = self.vec[...]
+        self.cs[p.chip] = self.vec[...]
+        for k, to in enumerate(p.chips()):
+            rcopy(self.cs.at[p.chip], self.cs.at[p.chip], self.c_s.at[k], self.c_r.at[p.chip], to).start()
+
+    def middle(self):
+        p = self.p
+        for k in range(1, 8):
+            chip = lax.rem(p.chip + k, 8)
+            rcopy(self.cs.at[chip], self.cs.at[chip], self.c_s.at[0], self.c_r.at[chip], p.sibling).wait_recv()
+        total = self.cs[0]
+        for k in range(1, 8):
+            total = total + self.cs[k]
+        self.own[...] = total
+        rcopy(self.own, self.other, self.k_s, self.k_r, p.sibling).start()
+
+    def late(self):
+        p = self.p
+        rcopy(self.own, self.other, self.k_s, self.k_r, p.sibling).wait_recv()
+        self.hs[p.head] = self.own[...] + self.other[...]
         for k in range(1, NHEAD):
             h = lax.rem(p.head + k, NHEAD)
             rcopy(self.hs.at[p.head], self.hs.at[p.head], self.h_s.at[k], self.h_r.at[p.head], {"head": h}).start()
 
-    def middle(self):
+    def result(self):
         p = self.p
         for k in range(1, NHEAD):
             h = lax.rem(p.head + k, NHEAD)
@@ -683,23 +705,7 @@
         for h in range(1, NHEAD):
             total = total + self.hs[h]
         per_head = lax.broadcasted_iota(jnp.int32, (VEC, 128), 0) >= 34
-        self.cs[p.chip] = jnp.where(per_head, self.vec[...], total)
-        for k, to in enumerate(p.chips()):
-            rcopy(self.cs.at[p.chip], self.cs.at[p.chip], self.c_s.at[k], self.c_r.at[p.chip], to).start()
-
-    def result(self):
-        p = self.p
-        for k in range(1, 8):
-            chip = lax.rem(p.chip + k, 8)
-            rcopy(self.cs.at[chip], self.cs.at[chip], self.c_s.at[0], self.c_r.at[chip], p.sibling).wait_recv()
-        total = self.cs[0]
-        for k in range(1, 8):
-            total = total + self.cs[k]
-        self.own[...] = total
-        move = rcopy(self.own, self.other, self.k_s, self.k_r, p.sibling)
-        move.start()
-        move.wait_recv()
-        return total + self.other[...]
+        return jnp.where(per_head, self.hs[p.head], total)
 
     def finish(self):
         p = self.p
@@ -718,10 +724,11 @@
     ws, wr, wh, os, or_, oh, s0, r0, h0, s1, r1, h1, s2, r2, h2, local_sem,
 ):
     p = Spot()
+    arrive = greet(p.chips() + [p.sibling] + p.lines())
     mine = pl.ds(pl.multiple_of(p.dp * 128, 128), 128)
     for k, one in enumerate((wq, wf, wi, wo)):
         w[mine, 256 * k : 256 * (k + 1)] = one[...]
-    greet(p.chips() + [p.sibling] + p.lines())
+    arrive()
     gather = Gather(p, w, ws, wr, wh)
     gather.first()
     wt[:, mine] = w_output[...]
@@ -808,6 +815,8 @@
     gathers[0].second()
     later.fourth()
     exchange.result(incoming)
+    gathers[1].second()
+    gathers[2].second()
     for h in range(2):
         lanes = slice(h * 128, (h + 1) * 128)
         state = incoming[h]
@@ -831,8 +840,6 @@
             gate = raw[rows, 768 + h * 128 : 768 + (h + 1) * 128]
             gated[rows, lanes] = (x * scale * group_gain[...] * (gate * sigmoid(gate))).astype(BF16)
 
-    gathers[1].second()
-    gathers[2].second()
     later.last()
     keep(wt, wt_out)
 
@@ -845,11 +852,9 @@
             ps[:, columns] = mm(gated[...], wt[:, columns], NN).astype(BF16)
 
         send()
+    scatter.middle()
     for g in gathers:
         g.third()
-    scatter.middle()
-    for g in gathers:
-        g.fourth()
     scatter.collect()
     own = pl.multiple_of(p.head * ROWS, ROWS)
 
@@ -865,6 +870,8 @@
     spread = HeadGather(p, hn, ag_s, ag_r)
     spread.send()
     spread.middle()
+    for g in gathers:
+        g.fourth()
     for g, full, out in zip(gathers, (g0, g1, g2), (wg_out, wu_out, wd_out)):
         g.last()
         keep(full, out)
@@ -950,11 +957,27 @@
         row, column = lax.rem(j, 2) * 256, lax.div(j, 2) * 1024
         return ref.at[pl.ds(pl.multiple_of(row, 256), 256), pl.ds(pl.multiple_of(column, 1024), 1024)]
 
+    def put(low, high):
+        def write_four(x):
+            low[:, 0:128], low[:, 128:256] = x[0:128], x[128:256]
+            high[:, 0:128], high[:, 128:256] = x[256:384], x[384:512]
+
+        return write_four
+
+    def add_to(low, high):
+        def add(x):
+            low[:, 0:128] += x[0:128]
+            low[:, 128:256] += x[128:256]
+            high[:, 0:128] += x[256:384]
+            high[:, 128:256] += x[384:512]
+
+        return add
+
     p = Spot()
     own = pl.multiple_of(p.head * ROWS, ROWS)
     loads = [load(one, full, k) for k, (one, full) in enumerate(((wg_in, wg), (hn_in, hn), (wu_in, wu), (wd_in, wd), (dy_in, dy)))]
     late = [load(hid.at[pl.ds(own, ROWS), :], hid_rows, 5), load(raw_in, raw, 6)]
-    greet(p.chips() + [p.sibling] + p.heads())
+    arrive = greet(p.chips() + [p.sibling] + p.heads())
     for move in loads:
         move.wait()
     for low, high in ((0, 256), (256, 512), (512, FFH)):
@@ -967,6 +990,7 @@
         dg[:, low:high] = (dh * up * slope(gate, s)).astype(BF16)
         du[:, low:high] = (dh * silu).astype(BF16)
 
+    arrive()
     scatter = HeadSum(p, ps, slots, rs_s, rs_r)
     for start, send in ((HALF, scatter.send_right), (0, scatter.send_left)):
 
@@ -1077,7 +1101,7 @@
     exchange = Exchange(p, msg, sib, slots3, give, take, ex_send, ex_recv, True)
     exchange.to_sibling()
     results = (out_gate, out_up, out_down)
-    for one, out in zip(sums, results):
+    for one, out in zip(sums[:2], results):
         one.to_x(write(out))
     exchange.to_chips()
 
@@ -1105,17 +1129,24 @@
             d_values[rows, lanes] = mm(scores[0], grad, TN) + mm(scores[1], grad, TN)
             state = halves(states[h, c])
             outer = mm(grad, state[0], NN) + mm(grad, state[1], NN)
-            d_query[rows, lanes] = mm3(d_scores, lower, NN) * up[:, lanes] + outer * jnp.exp(running[:, lanes]) * carried
+            query_grad = mm3(d_scores, lower, NN) * up[:, lanes] + outer * jnp.exp(running[:, lanes]) * carried
+            d_query[rows, lanes] = query_grad
+            query_raw = raw[rows, lanes]
+            draw[rows, lanes] = (query_grad * slope(query_raw, sigmoid(query_raw))).astype(BF16)
             d_keys[rows, lanes] = mm3(d_scores, lift, TN) * down_[:, lanes]
 
-    for one, out in zip(sums, results):
+    for one in sums[:2]:
+        one.finish()
+    first = DpSum(p, 512, a0, a1, a2, f3, f4, f5, f6)
+    second = DpSum(p, 512, b0, b1, b2, g3, g4, g5, g6)
+    third = DpSum(p, HERE, e0, e1, e2, e3, e4, e5, e6)
+    products_turned(hn, draw.at[:, 0:256], draw.at[:, 768:1024], a0)
+    exchange.result(incoming)
+    first.to_sibling()
+    sums[2].to_x(write(out_down))
+    for one, out in zip(sums[:2], results):
         one.end(accumulate(out))
-    third = DpSum(p, HERE, e0, e1, e2, e3, e4, e5, e6)
-    products(gated_t, db, e0)
-    third.to_sibling()
-    exchange.result(incoming)
-    third.to_z()
-    third.join()
+    first.to_z()
     bound_total[...] = jnp.zeros_like(bound_total)
 
     @pl.loop(0, CHUNKS)
@@ -1147,8 +1178,6 @@
                 forget_grad * (1.0 - bound[:, lanes]) * logistic[:, lanes] * rest
             ).astype(BF16)
             bound_total[:, lanes] += jnp.sum(forget_grad * rest, axis=0, keepdims=True)
-            query_raw = raw[rows, lanes]
-            draw[rows, lanes] = (query_grad * slope(query_raw, sigmoid(query_raw))).astype(BF16)
             incoming[h] = state * decay[c, 0:1, lanes] + back_update[h, c]
 
     scatter2 = HeadSum(p, ps, slots, rs2_s, rs2_r)
@@ -1160,39 +1189,15 @@
             ps[:, columns] = mm(draw[...], place(part, j)[...], NT).astype(BF16)
 
         send()
-    for one in sums:
-        one.finish()
-    first = DpSum(p, 512, a0, a1, a2, f3, f4, f5, f6)
-    second = DpSum(p, 512, b0, b1, b2, g3, g4, g5, g6)
-    products_turned(hn, draw.at[:, 0:512], a0)
-    first.to_sibling()
-    products_turned(hn, draw.at[:, 512:1024], b0)
-    first.to_z()
+    products_turned(hn, draw.at[:, 256:512], draw.at[:, 512:768], b0)
     second.to_sibling()
-    scatter1.middle()
-    scatter2.middle()
-    second.to_z()
-    scatter1.collect()
-
-    @pl.loop(0, 4)
-    def _(i):
-        rows = pl.ds(pl.multiple_of(i * 16, 16), 16)
-        block_out[rows, :] = (resid[rows, :] + scatter1.rows(i * 16, 16)).astype(BF16)
-
     first.join()
-    third.to_x(write(out_output))
-    scatter2.collect()
-    norm_terms[...] = jnp.zeros_like(norm_terms)
-
-    @pl.loop(0, 4)
-    def _(i):
-        rows = pl.ds(pl.multiple_of(i * 16, 16), 16)
-        grad, x = scatter2.rows(i * 16, 16), hid_rows[rows, :].astype(F32)
-        inverse = lax.rsqrt(jnp.mean(x * x, axis=-1, keepdims=True) + EPS)
-        scaled, normed = grad * gain[...], x * inverse
-        back = inverse * (scaled - normed * jnp.mean(scaled * normed, axis=-1, keepdims=True))
-        norm_terms[...] += jnp.sum(grad * normed, axis=0, keepdims=True)
-        grad_in[rows, :] = d_resid[rows, :] + back
+
+    @pl.loop(0, 8)
+    def _(j):
+        columns = pl.ds(pl.multiple_of(j * 256, 256), 256)
+        terms = ps[:, columns].astype(F32) * hn[:, columns].astype(F32)
+        norm_terms[:, columns] = jnp.sum(terms, axis=0, keepdims=True) / gain[:, columns]
 
     vec[...] = jnp.zeros_like(vec)
     for i in range(16):
@@ -1204,29 +1209,38 @@
     vec[35:36, :] = bound_total[:, 128:256]
     everywhere = Total(p, vec, t0, t1, t2, t3, t4, t5, t6, t7, t8.at[0], t9.at[0])
     everywhere.send()
+    second.to_z()
+    scatter2.middle()
+    products(gated_t, db, e0)
+    third.to_sibling()
+    everywhere.middle()
+    third.to_z()
+    everywhere.late()
+    scatter1.middle()
     second.join()
-    third.end(accumulate(out_output))
-    everywhere.middle()
-
-    def put_first(x):
-        out_query[:, 0:128], out_query[:, 128:256] = x[0:128], x[128:256]
-        out_forget[:, 0:128], out_forget[:, 128:256] = x[256:384], x[384:512]
-
-    def put_second(x):
-        out_input[:, 0:128], out_input[:, 128:256] = x[0:128], x[128:256]
-        out_outgate[:, 0:128], out_outgate[:, 128:256] = x[256:384], x[384:512]
-
-    def add_to(low, high):
-        def add(x):
-            low[:, 0:128] += x[0:128]
-            low[:, 128:256] += x[128:256]
-            high[:, 0:128] += x[256:384]
-            high[:, 128:256] += x[384:512]
-
-        return add
-
-    first.to_x(put_first)
-    second.to_x(put_second)
+    sums[2].end(accumulate(out_down))
+    first.to_x(put(out_query, out_outgate))
+    third.join()
+    scatter2.collect()
+
+    @pl.loop(0, 4)
+    def _(i):
+        rows = pl.ds(pl.multiple_of(i * 16, 16), 16)
+        grad, x = scatter2.rows(i * 16, 16), hid_rows[rows, :].astype(F32)
+        inverse = lax.rsqrt(jnp.mean(x * x, axis=-1, keepdims=True) + EPS)
+        scaled, normed = grad * gain[...], x * inverse
+        back = inverse * (scaled - normed * jnp.mean(scaled * normed, axis=-1, keepdims=True))
+        grad_in[rows, :] = d_resid[rows, :] + back
+
+    scatter1.collect()
+
+    @pl.loop(0, 4)
+    def _(i):
+        rows = pl.ds(pl.multiple_of(i * 16, 16), 16)
+        block_out[rows, :] = (resid[rows, :] + scatter1.rows(i * 16, 16)).astype(BF16)
+
+    second.to_x(put(out_forget, out_input))
+    third.to_x(write(out_output))
     all_of = everywhere.result()
     out_norm[...] = all_of[0:16]
     out_ffn[...] = all_of[16:32]
@@ -1236,14 +1250,16 @@
     for h in range(2):
         lanes = slice(h * 128, (h + 1) * 128)
         out_bounds[:, lanes] = soft[:, lanes] * (picked[:, lanes] - bound[:, lanes]) * all_of[34 + h : 35 + h]
-    first.end(add_to(out_query, out_forget))
-    second.end(add_to(out_input, out_outgate))
+
+    first.end(add_to(out_query, out_outgate))
+    second.end(add_to(out_forget, out_input))
+    third.end(accumulate(out_output))
     spread.finish()
     scatter1.finish()
     scatter2.finish()
     exchange.finish()
     everywhere.finish()
-    for one in (first, second, third):
+    for one in (first, second, third, sums[2]):
         one.finish()
 
 

time: 246 us -> 231 us (0.939)
  Pallas kernels: 245 us -> 229 us
    pallas_call x1, Pallas kernels: 135 us -> 126 us  [call_backward(): pl.pallas_call(backward, name='backward', out_shape=[jax.ShapeDtypeStruct...]
    pallas_call x1, Pallas kernels: 107 us -> 100 us  [call_forward(): pl.pallas_call(forward, name='forward', out_shape=(out((TOK, 1024), F32),...]
where the time goes in v4:
time: 231 us; the launch traced here: 230 us
  Pallas kernels  229 us (99%)
    pallas_call x1, Pallas kernels, call_backward(): pl.pallas_call(backward, name='backward', out_shape=[jax.ShapeDtypeStruct...  126 us
    pallas_call x1, Pallas kernels, call_forward(): pl.pallas_call(forward, name='forward', out_shape=(out((TOK, 1024), F32),...  100 us

profile of v4, /device:TPU:1, one launch (start us, length us, event | category | flops | bytes accessed | tf_op | source)
XLA Modules:
  0.0 230.3 jit_solution(11692542170112477277)
XLA Ops:
  1.3 100.0 %forward.1 = (f32[512,1024]{1,0:T(8,128)}, bf16[512,2048]{1,0:T(8,128)(2,1)}, bf16[512,256]{1,0:T(8,128)(2,1)}, f32[512,256]{1,0:T(8,128)}, f32[2,5,128,128]{3,2...) custom-call(bf16[512,2048]{1,0:T(8,128)(2,1)} %hid.3, ...), custom_call_target="tpu_custom_call" | custom-call | tf_op jit(solution)/shard_map/forward/pallas_call | solution.py:889
  101.3 125.7 %backward.1 = (bf16[64,2048]{1,0:T(8,128)(2,1)}, f32[64,2048]{1,0:T(8,128)}, f32[128,256]{1,0:T(8,128)}, f32[128,256]{1,0:T(8,128)}, f32[128,256]{1,0:T(8,128)},...) custom-call(bf16[512,2048]{1,0:T(8,128)(2,1)} %get-tuple-element.59., ...), custom_call_target="tpu_custom_call" | custom-call | tf_op jit(solution)/shard_map/backward/pallas_call | solution.py:1288
  227.0 3.2 %results.1 = (bf16[64,2048]{1,0:T(8,128)(2,1)}, f32[64,2048]{1,0:T(8,128)}, f32[128,256]{1,0:T(8,128)}, f32[128,256]{1,0:T(8,128)}, f32[128,256]{1,0:T(8,128)}, ...) custom-call(bf16[64,2048]{1,0:T(8,128)(2,1)} %get-tuple-element.73.r, ...), custom_call_target="tpu_custom_call" | custom-call | tf_op jit(solution)/shard_map/results/pallas_call | solution.py:1349

commit v5 on v4

--- a/solution.py
+++ b/solution.py
@@ -149,6 +149,16 @@
             rcopy(b, b, self.s.at[k], self.r.at[0], p.sibling).wait_send()
 
 
+class WideGather(Gather):
+    def block(self, d, start=0, rows=0):
+        row, column = lax.rem(d, 8) * 128 + start, lax.div(d, 8) * 1024
+        return self.g.at[pl.ds(pl.multiple_of(row, 64), rows or 128), pl.ds(pl.multiple_of(column, 1024), 1024)]
+
+    def tile(self, d, k):
+        row, column = lax.rem(d, 8) * 128, lax.div(d, 8) * 1024 + 256 * k
+        return self.g.at[pl.ds(pl.multiple_of(row, 128), 128), pl.ds(pl.multiple_of(column, 256), 256)]
+
+
 def gather_semaphores():
     return [
         pltpu.SemaphoreType.DMA((GATHER_SENDS,)),
@@ -716,58 +726,89 @@
         rcopy(self.own, self.other, self.k_s, self.k_r, p.sibling).wait_send()
 
 
-def forward(
-    hid, gain, wq, wf, wi, wo, w_output, lb, layer, seq, group_gain, ffn_gain, wg, wu, wd,
-    raw, xn_out, gated, mixed, states, run, total, w_out, wt_out, hn_out, resid, wg_out, wu_out, wd_out,
-    xn, w, wt, g0, g1, g2, hn, ps, slots, inner_update, decay, incoming,
-    msg, sib, slots3, give, take, ex_send, ex_recv, rs_s, rs_r, ag_s, ag_r,
-    ws, wr, wh, os, or_, oh, s0, r0, h0, s1, r1, h1, s2, r2, h2, local_sem,
+def layer_block(
+    hid, dy_in, wq, wf, wi, wo, w_output, wg_in, wu_in, wd_in, gain, lb, group_gain, ffn_gain, layer, seq,
+    block_out, grad_in, out_query, out_forget, out_input, out_outgate, out_output, out_bounds,
+    out_norm, out_group, out_ffn, out_mean, out_gate, out_up, out_down, xn_out, w_out,
+    ps, slots, hn, wide, wg, wu, wd, wt, raw, hid_rows, gated, gated_t, mixed, run, states, update, resid, d_resid,
+    hidden, dg, du, hidden_t, dg_t, du_t, draw, d_mixed, d_query, d_keys, d_values, decay, incoming, vec,
+    norm_terms, ffn_terms, group_total, bound_total, total,
+    msg, sib, slots3, give, take, ex_send, ex_recv, msg2, sib2, slots4, give2, take2, ex2_send, ex2_recv,
+    rs0_s, rs0_r, ag0_s, ag0_r, rs_s, rs_r, ag_s, ag_r, rs1_s, rs1_r, rs2_s, rs2_r,
+    ws, wr, wh, os, or_, oh, s0, r0, h0, s1, r1, h1, s2, r2, h2,
+    a0, a1, a2, a3, a4, a5, a6, b0, b1, b2, b3, b4, b5, b6, c0, c1, c2, c3, c4, c5, c6,
+    e0, e1, e2, e3, e4, e5, e6, f3, f4, f5, f6, g3, g4, g5, g6,
+    t0, t1, t2, t3, t4, t5, t6, t7, t8, t9, local_sem,
 ):
+    dy, db, xn = wide.at[0:TOK], wide.at[TOK : 2 * TOK], hn
+    used = []
+
+    def load(source, to):
+        move = pltpu.make_async_copy(source, to, local_sem.at[len(used)])
+        move.start()
+        used.append(move)
+        return move
+
+    def put(low, high):
+        def write_four(x):
+            low[:, 0:128], low[:, 128:256] = x[0:128], x[128:256]
+            high[:, 0:128], high[:, 128:256] = x[256:384], x[384:512]
+
+        return write_four
+
+    def add_to(low, high):
+        def add(x):
+            low[:, 0:128] += x[0:128]
+            low[:, 128:256] += x[128:256]
+            high[:, 0:128] += x[256:384]
+            high[:, 128:256] += x[384:512]
+
+        return add
+
     p = Spot()
-    arrive = greet(p.chips() + [p.sibling] + p.lines())
+    arrive = greet(p.chips() + [p.sibling] + p.heads())
+    own = pl.multiple_of(p.head * ROWS, ROWS)
     mine = pl.ds(pl.multiple_of(p.dp * 128, 128), 128)
-    for k, one in enumerate((wq, wf, wi, wo)):
-        w[mine, 256 * k : 256 * (k + 1)] = one[...]
+    gather = WideGather(p, wide, ws, wr, wh)
+    loads = [load(one, gather.tile(p.dp, k)) for k, one in enumerate((wq, wf, wi, wo))]
+    loads.append(load(hid, ps))
+    own_blocks = [load(w_output, wt.at[:, mine])]
+    own_blocks += [load(one, full.at[:, mine]) for one, full in ((wg_in, wg), (wu_in, wu), (wd_in, wd))]
+    own_rows = load(hid.at[pl.ds(own, ROWS), :], hid_rows)
+    for move in loads[:4]:
+        move.wait()
     arrive()
-    gather = Gather(p, w, ws, wr, wh)
     gather.first()
-    wt[:, mine] = w_output[...]
+    loads[4].wait()
     later = Gather(p, wt, os, or_, oh, HERE)
-    for one, full in zip((wg, wu, wd), (g0, g1, g2)):
-        full[:, mine] = one[...]
-    gathers = [Gather(p, g0, s0, r0, h0, FFH), Gather(p, g1, s1, r1, h1, FFH), Gather(p, g2, s2, r2, h2, FFH)]
+    gathers = [Gather(p, wg, s0, r0, h0, FFH), Gather(p, wu, s1, r1, h1, FFH), Gather(p, wd, s2, r2, h2, FFH)]
 
     @pl.loop(0, 8)
     def _(i):
         rows = pl.ds(pl.multiple_of(i * 64, 64), 64)
-        x = hid[rows, :].astype(F32)
+        x = ps[rows, :].astype(F32)
         scale = lax.rsqrt(jnp.mean(x * x, axis=-1, keepdims=True) + EPS)
         xn[rows, :] = (x * scale * gain[...]).astype(BF16)
 
-    keeps = []
-
-    def keep(source, out):
-        move = pltpu.make_async_copy(source, out, local_sem.at[len(keeps)])
-        move.start()
-        keeps.append(move)
-
-    keep(xn, xn_out)
     gather.second()
     gather.third()
     gather.fourth()
+    for move in own_blocks:
+        move.wait()
     later.first()
     gathers[0].first()
     gather.last()
-    keep(w, w_out)
+    spills = [load(xn, xn_out), load(wide, w_out)]
 
     @pl.loop(0, 4)
     def _(j):
         columns = pl.ds(pl.multiple_of(j * 256, 256), 256)
-        raw[:, columns] = mm(xn[...], w[:, columns], NN)
+        other = pl.ds(pl.multiple_of(1024 + j * 256, 256), 256)
+        raw[:, columns] = mm(xn[:, 0:1024], wide[:, columns], NN) + mm(xn[:, 1024:2048], wide[:, other], NN)
 
     later.second()
     segments = Segments(p, seq)
-    bound = lower_bound(lb, layer[0])[2]
+    soft, picked, bound = lower_bound(lb, layer[0])
     total[...] = jnp.zeros_like(total)
 
     @pl.loop(0, CHUNKS)
@@ -796,13 +837,13 @@
             scores = jnp.where(linked, scores, 0.0)
             mixed[rows, lanes] = mm2(halves(scores), values[:, lanes], NN)
             high, low = halves(tail[:, lanes] * ends)
-            inner_update[h, c] = mm(values[:, lanes], high, TN) + mm(values[:, lanes], low, TN)
+            update[h, c] = mm(values[:, lanes], high, TN) + mm(values[:, lanes], low, TN)
 
     for h in range(2):
         lanes = slice(h * 128, (h + 1) * 128)
-        state, rate = inner_update[h, 0], decay[0, 0:1, lanes]
+        state, rate = update[h, 0], decay[0, 0:1, lanes]
         for c in range(1, CHUNKS):
-            state = state * decay[c, 0:1, lanes] + inner_update[h, c]
+            state = state * decay[c, 0:1, lanes] + update[h, c]
             rate = rate * decay[c, 0:1, lanes]
         msg[h, 0:128, :] = state
         msg[h, 128:136, :] = jnp.broadcast_to(rate, (8, 128))
@@ -822,7 +863,7 @@
         state = incoming[h]
         states[h, 0] = state
         for c in range(CHUNKS):
-            state = state * decay[c, 0:1, lanes] + inner_update[h, c]
+            state = state * decay[c, 0:1, lanes] + update[h, c]
             states[h, c + 1] = state
 
     @pl.loop(0, CHUNKS)
@@ -841,10 +882,12 @@
             gated[rows, lanes] = (x * scale * group_gain[...] * (gate * sigmoid(gate))).astype(BF16)
 
     later.last()
-    keep(wt, wt_out)
-
-    scatter = HeadSum(p, ps, slots, rs_s, rs_r)
-    for start, send in ((HALF, scatter.send_right), (0, scatter.send_left)):
+
+    for move in spills:
+        move.wait()
+    dy_load = load(dy_in, dy)
+    scatter0 = HeadSum(p, ps, slots, rs0_s, rs0_r)
+    for start, send in ((HALF, scatter0.send_right), (0, scatter0.send_left)):
 
         @pl.loop(0, 4)
         def _(j):
@@ -852,134 +895,34 @@
             ps[:, columns] = mm(gated[...], wt[:, columns], NN).astype(BF16)
 
         send()
-    scatter.middle()
+    scatter0.middle()
     for g in gathers:
         g.third()
-    scatter.collect()
-    own = pl.multiple_of(p.head * ROWS, ROWS)
+    scatter0.collect()
+    own_rows.wait()
 
     @pl.loop(0, 4)
     def _(i):
         rows = pl.ds(pl.multiple_of(i * 16, 16), 16)
         here = pl.ds(pl.multiple_of(own + i * 16, 16), 16)
-        x = hid[here, :].astype(F32) + scatter.rows(i * 16, 16)
+        x = hid_rows[rows, :].astype(F32) + scatter0.rows(i * 16, 16)
         resid[rows, :] = x
         scale = lax.rsqrt(jnp.mean(x * x, axis=-1, keepdims=True) + EPS)
         hn[here, :] = (x * scale * ffn_gain[...]).astype(BF16)
 
-    spread = HeadGather(p, hn, ag_s, ag_r)
-    spread.send()
-    spread.middle()
+    scatter0.finish()
+    spread0 = HeadGather(p, hn, ag0_s, ag0_r)
+    spread0.send()
+    spread0.middle()
     for g in gathers:
         g.fourth()
-    for g, full, out in zip(gathers, (g0, g1, g2), (wg_out, wu_out, wd_out)):
+    for g in gathers:
         g.last()
-        keep(full, out)
+    dy_load.wait()
+    gated_t[...] = gated[...].T
     exchange.finish()
-    scatter.finish()
-    spread.collect()
-    keep(hn, hn_out)
-    spread.finish()
-    for move in keeps:
-        move.wait()
-
-
-def call_forward(*arrays):
-    out = jax.ShapeDtypeStruct
-    return pl.pallas_call(
-        forward,
-        name="forward",
-        out_shape=(
-            out((TOK, 1024), F32),
-            out((TOK, D), BF16),
-            out((TOK, HERE), BF16),
-            out((TOK, HERE), F32),
-            out((2, CHUNKS + 1, 128, 128), F32),
-            out((TOK, HERE), F32),
-            out((1, HERE), F32),
-            out((D, 1024), BF16),
-            out((HERE, D), BF16),
-            out((TOK, D), BF16),
-            out((ROWS, D), F32),
-            out((FFH, D), BF16),
-            out((FFH, D), BF16),
-            out((FFH, D), BF16),
-        ),
-        in_specs=[VM] * 8 + [SM, SM] + [VM] * 5,
-        out_specs=(VM, HB, VM, VM, VM, VM, VM, HB, HB, HB, VM, HB, HB, HB),
-        scratch_shapes=[
-            pltpu.VMEM((TOK, D), BF16),
-            pltpu.VMEM((D, 1024), BF16),
-            pltpu.VMEM((HERE, D), BF16),
-            *[pltpu.VMEM((FFH, D), BF16)] * 3,
-            *[pltpu.VMEM((TOK, D), BF16)] * 3,
-            pltpu.VMEM((2, CHUNKS, 128, 128), F32),
-            pltpu.VMEM((CHUNKS, 8, HERE), F32),
-            pltpu.VMEM((2, 128, 128), F32),
-            *exchange_scratch(),
-            *sixteen(),
-            *sixteen(),
-            *gather_semaphores(),
-            *gather_semaphores(),
-            *gather_semaphores(),
-            *gather_semaphores(),
-            *gather_semaphores(),
-            pltpu.SemaphoreType.DMA((7,)),
-        ],
-        compiler_params=pltpu.CompilerParams(
-            collective_id=0, has_side_effects=True, vmem_limit_bytes=58 * 1024 * 1024
-        ),
-    )(*arrays)
-
-
-def backward(
-    hn_in, dy_in, wg_in, wu_in, wd_in, resid, ffn_gain, wt, raw_in, run, mixed, states, gated, xn_in, w_in, hid,
-    total, gain, group_gain, lb, layer, seq,
-    block_out, grad_in, out_query, out_forget, out_input, out_outgate, out_output, out_bounds,
-    out_norm, out_group, out_ffn, out_mean, out_gate, out_up, out_down,
-    hn, dy, wg, wu, wd, hidden, dg, du, hidden_t, dg_t, du_t, gated_t, ps, slots, db, d_resid, hid_rows, raw,
-    draw, d_mixed, d_query, d_keys, d_values, back_update, decay, incoming, vec,
-    norm_terms, ffn_terms, group_total, bound_total,
-    msg, sib, slots3, give, take, ex_send, ex_recv, rs_s, rs_r, ag_s, ag_r, rs1_s, rs1_r, rs2_s, rs2_r,
-    a0, a1, a2, a3, a4, a5, a6, b0, b1, b2, b3, b4, b5, b6, c0, c1, c2, c3, c4, c5, c6,
-    e0, e1, e2, e3, e4, e5, e6, f3, f4, f5, f6, g3, g4, g5, g6,
-    t0, t1, t2, t3, t4, t5, t6, t7, t8, t9, local_sem,
-):
-    def load(source, to, k):
-        move = pltpu.make_async_copy(source, to, local_sem.at[k])
-        move.start()
-        return move
-
-    def quarter(ref, j):
-        return ref.at[pl.ds(256 * j, 256), :]
-
-    def place(ref, j):
-        row, column = lax.rem(j, 2) * 256, lax.div(j, 2) * 1024
-        return ref.at[pl.ds(pl.multiple_of(row, 256), 256), pl.ds(pl.multiple_of(column, 1024), 1024)]
-
-    def put(low, high):
-        def write_four(x):
-            low[:, 0:128], low[:, 128:256] = x[0:128], x[128:256]
-            high[:, 0:128], high[:, 128:256] = x[256:384], x[384:512]
-
-        return write_four
-
-    def add_to(low, high):
-        def add(x):
-            low[:, 0:128] += x[0:128]
-            low[:, 128:256] += x[128:256]
-            high[:, 0:128] += x[256:384]
-            high[:, 128:256] += x[384:512]
-
-        return add
-
-    p = Spot()
-    own = pl.multiple_of(p.head * ROWS, ROWS)
-    loads = [load(one, full, k) for k, (one, full) in enumerate(((wg_in, wg), (hn_in, hn), (wu_in, wu), (wd_in, wd), (dy_in, dy)))]
-    late = [load(hid.at[pl.ds(own, ROWS), :], hid_rows, 5), load(raw_in, raw, 6)]
-    arrive = greet(p.chips() + [p.sibling] + p.heads())
-    for move in loads:
-        move.wait()
+    spread0.collect()
+
     for low, high in ((0, 256), (256, 512), (512, FFH)):
         gate = mm(hn[...], wg[low:high, :], NT)
         up = mm(hn[...], wu[low:high, :], NT)
@@ -990,7 +933,6 @@
         dg[:, low:high] = (dh * up * slope(gate, s)).astype(BF16)
         du[:, low:high] = (dh * silu).astype(BF16)
 
-    arrive()
     scatter = HeadSum(p, ps, slots, rs_s, rs_r)
     for start, send in ((HALF, scatter.send_right), (0, scatter.send_left)):
 
@@ -1025,8 +967,8 @@
         wu[0:TOK, columns] = mm(hidden[...], wd[:, columns], NN).astype(BF16)
 
     sums[2].to_z()
-    late.append(load(xn_in, hn, 7))
-    late += [load(quarter(w_in, j), place(wd, j), 8 + j) for j in range(4)]
+    spread0.finish()
+    late = [load(xn_out, hn), load(w_out.at[0:TOK], wd.at[0:TOK])]
     scatter.collect()
     ffn_terms[...] = jnp.zeros_like(ffn_terms)
 
@@ -1048,11 +990,8 @@
     spread.send()
     spread.middle()
     sums[1].join()
-    late += [load(quarter(w_in, 4 + j), place(dy, j), 12 + j) for j in range(4)]
-    segments = Segments(p, seq)
-    soft, picked, bound = lower_bound(lb, layer[0])
+    late.append(load(w_out.at[TOK : 2 * TOK], dy))
     group_total[...] = jnp.zeros_like(group_total)
-    gated_t[...] = gated[...].T
     for move in late:
         move.wait()
     sums[2].join()
@@ -1064,11 +1003,8 @@
     def _(c):
         rows = pl.ds(pl.multiple_of(c * CHUNK, CHUNK), CHUNK)
         d_gated = mm(db[rows, :], wt[...], NT)
-        before, final = segments.before(c), segments.final(c)
-        carried = jnp.where(segments.column(c) == before, 1.0, 0.0)
+        carried = jnp.where(segments.column(c) == segments.before(c), 1.0, 0.0)
         running = run[rows, :]
-        rate = jnp.exp(running[127:128]) * jnp.where(final == before, 1.0, 0.0)
-        decay[c] = jnp.broadcast_to(rate, (8, HERE))
         for h in range(2):
             lanes = slice(h * 128, (h + 1) * 128)
             x, grad = mixed[rows, lanes], d_gated[:, lanes]
@@ -1088,22 +1024,22 @@
             query_raw = raw[rows, lanes]
             query = (query_raw * sigmoid(query_raw)).astype(BF16).astype(F32)
             high, low = halves(query * jnp.exp(running[:, lanes]) * carried)
-            back_update[h, c] = mm(back, high, TN) + mm(back, low, TN)
+            update[h, c] = mm(back, high, TN) + mm(back, low, TN)
 
     for h in range(2):
         lanes = slice(h * 128, (h + 1) * 128)
-        state, rate = back_update[h, CHUNKS - 1], decay[CHUNKS - 1, 0:1, lanes]
+        state, rate = update[h, CHUNKS - 1], decay[CHUNKS - 1, 0:1, lanes]
         for c in range(CHUNKS - 2, -1, -1):
-            state = state * decay[c, 0:1, lanes] + back_update[h, c]
+            state = state * decay[c, 0:1, lanes] + update[h, c]
             rate = rate * decay[c, 0:1, lanes]
-        msg[h, 0:128, :] = state
-        msg[h, 128:136, :] = jnp.broadcast_to(rate, (8, 128))
-    exchange = Exchange(p, msg, sib, slots3, give, take, ex_send, ex_recv, True)
-    exchange.to_sibling()
+        msg2[h, 0:128, :] = state
+        msg2[h, 128:136, :] = jnp.broadcast_to(rate, (8, 128))
+    exchange2 = Exchange(p, msg2, sib2, slots4, give2, take2, ex2_send, ex2_recv, True)
+    exchange2.to_sibling()
     results = (out_gate, out_up, out_down)
     for one, out in zip(sums[:2], results):
         one.to_x(write(out))
-    exchange.to_chips()
+    exchange2.to_chips()
 
     @pl.loop(0, CHUNKS)
     def _(c):
@@ -1141,7 +1077,7 @@
     second = DpSum(p, 512, b0, b1, b2, g3, g4, g5, g6)
     third = DpSum(p, HERE, e0, e1, e2, e3, e4, e5, e6)
     products_turned(hn, draw.at[:, 0:256], draw.at[:, 768:1024], a0)
-    exchange.result(incoming)
+    exchange2.result(incoming)
     first.to_sibling()
     sums[2].to_x(write(out_down))
     for one, out in zip(sums[:2], results):
@@ -1178,15 +1114,17 @@
                 forget_grad * (1.0 - bound[:, lanes]) * logistic[:, lanes] * rest
             ).astype(BF16)
             bound_total[:, lanes] += jnp.sum(forget_grad * rest, axis=0, keepdims=True)
-            incoming[h] = state * decay[c, 0:1, lanes] + back_update[h, c]
+            incoming[h] = state * decay[c, 0:1, lanes] + update[h, c]
 
     scatter2 = HeadSum(p, ps, slots, rs2_s, rs2_r)
-    for start, part, send in ((HALF, dy, scatter2.send_right), (0, wd, scatter2.send_left)):
-
-        @pl.loop(0, 4)
-        def _(j):
-            columns = pl.ds(pl.multiple_of(start + j * 256, 256), 256)
-            ps[:, columns] = mm(draw[...], place(part, j)[...], NT).astype(BF16)
+    for start, send in ((HALF, scatter2.send_right), (0, scatter2.send_left)):
+        for first_row, part in ((0, wd), (TOK, dy)):
+
+            @pl.loop(0, 2)
+            def _(j):
+                rows = pl.ds(pl.multiple_of(j * 256, 256), 256)
+                columns = pl.ds(pl.multiple_of(start + first_row + j * 256, 256), 256)
+                ps[:, columns] = mm(draw[...], part[rows, start : start + HALF], NT).astype(BF16)
 
         send()
     products_turned(hn, draw.at[:, 256:512], draw.at[:, 512:768], b0)
@@ -1257,7 +1195,7 @@
     spread.finish()
     scatter1.finish()
     scatter2.finish()
-    exchange.finish()
+    exchange2.finish()
     everywhere.finish()
     for one in (first, second, third, sums[2]):
         one.finish()
@@ -1282,29 +1220,34 @@
 )
 
 
-def call_backward(*arrays):
+def call_block(*arrays):
     sums = dp_sum_scratch(FFH)
     again = [pltpu.VMEM((512, 128), BF16)] * 2 + sixteen()
+    shapes = [*OUTS, ((TOK, D), BF16), ((2 * TOK, D), BF16)]
     return pl.pallas_call(
-        backward,
-        name="backward",
-        out_shape=[jax.ShapeDtypeStruct(*one) for one in OUTS],
-        in_specs=[HB, HB, HB, HB, HB, VM, VM, VM, HB, VM, VM, VM, VM, HB, HB, HB, VM, VM, VM, VM, SM, SM],
-        out_specs=[VM] * len(OUTS),
+        layer_block,
+        name="layer_block",
+        out_shape=[jax.ShapeDtypeStruct(*one) for one in shapes],
+        in_specs=[HB] * 10 + [VM] * 4 + [SM, SM],
+        out_specs=[VM] * len(OUTS) + [HB, HB],
         scratch_shapes=[
-            *[pltpu.VMEM((TOK, D), BF16)] * 2,
+            *[pltpu.VMEM((TOK, D), BF16)] * 3,
+            pltpu.VMEM((2 * TOK, D), BF16),
             *[pltpu.VMEM((FFH, D), BF16)] * 3,
+            pltpu.VMEM((HERE, D), BF16),
+            pltpu.VMEM((TOK, 1024), F32),
+            pltpu.VMEM((ROWS, D), BF16),
+            pltpu.VMEM((TOK, HERE), BF16),
+            pltpu.VMEM((HERE, TOK), BF16),
+            *[pltpu.VMEM((TOK, HERE), F32)] * 2,
+            pltpu.VMEM((2, CHUNKS + 1, 128, 128), F32),
+            pltpu.VMEM((2, CHUNKS, 128, 128), F32),
+            *[pltpu.VMEM((ROWS, D), F32)] * 2,
             *[pltpu.VMEM((TOK, FFH), BF16)] * 3,
             *[pltpu.VMEM((FFH, TOK), BF16)] * 3,
-            pltpu.VMEM((HERE, TOK), BF16),
-            *[pltpu.VMEM((TOK, D), BF16)] * 3,
-            pltpu.VMEM((ROWS, D), F32),
-            pltpu.VMEM((ROWS, D), BF16),
-            pltpu.VMEM((TOK, 1024), F32),
             pltpu.VMEM((TOK, 1024), BF16),
             pltpu.VMEM((TOK, HERE), BF16),
             *[pltpu.VMEM((TOK, HERE), F32)] * 3,
-            pltpu.VMEM((2, CHUNKS, 128, 128), F32),
             pltpu.VMEM((CHUNKS, 8, HERE), F32),
             pltpu.VMEM((2, 128, 128), F32),
             pltpu.VMEM((VEC, 128), F32),
@@ -1312,11 +1255,20 @@
             pltpu.VMEM((1, D), F32),
             pltpu.VMEM((1, 128), F32),
             pltpu.VMEM((1, HERE), F32),
+            pltpu.VMEM((1, HERE), F32),
             *exchange_scratch(),
+            *exchange_scratch(),
+            *sixteen(),
+            *sixteen(),
             *sixteen(),
             *sixteen(),
             *eight(),
             *sixteen(),
+            *gather_semaphores(),
+            *gather_semaphores(),
+            *gather_semaphores(),
+            *gather_semaphores(),
+            *gather_semaphores(),
             *sums,
             *sums,
             *sums,
@@ -1331,10 +1283,10 @@
             *eight(),
             pltpu.SemaphoreType.DMA((1,)),
             pltpu.SemaphoreType.DMA((1,)),
-            pltpu.SemaphoreType.DMA((16,)),
+            pltpu.SemaphoreType.DMA((20,)),
         ],
         compiler_params=pltpu.CompilerParams(
-            collective_id=1, has_side_effects=True, vmem_limit_bytes=60 * 1024 * 1024
+            collective_id=0, has_side_effects=True, vmem_limit_bytes=60 * 1024 * 1024
         ),
     )(*arrays)
 
@@ -1359,18 +1311,14 @@
     hidden_in, norm_gain, w_query, w_forget, w_input, w_outgate, lower_bounds, layer_index, group_gain,
     w_output, ffn_gain, w_gate, w_up, w_down, seq_lengths, grad_out,
 ):
-    norm_row, ffn_row, group_row = norm_gain.reshape(1, D), ffn_gain.reshape(1, D), group_gain.reshape(1, KDIM)
-    raw, xn, gated, mixed, states, run, total, w_all, wt_all, hn, resid, wg, wu, wd = call_forward(
-        hidden_in, norm_row, w_query, w_forget, w_input, w_outgate, w_output, lower_bounds, layer_index, seq_lengths,
-        group_row, ffn_row, w_gate.T, w_up.T, w_down,
+    arrays = call_block(
+        hidden_in, grad_out, w_query, w_forget, w_input, w_outgate, w_output, w_gate.T, w_up.T, w_down,
+        norm_gain.reshape(1, D), lower_bounds, group_gain.reshape(1, KDIM), ffn_gain.reshape(1, D), layer_index, seq_lengths,
     )
     (
         block_out, grad_in, grad_query, grad_forget, grad_input, grad_outgate, grad_output, grad_bounds,
         grad_norm, grad_group, grad_ffn, mean, grad_gate, grad_up, grad_down,
-    ) = call_results(call_backward(
-        hn, grad_out, wg, wu, wd, resid, ffn_row, wt_all, raw, run, mixed, states, gated, xn, w_all, hidden_in,
-        total, norm_row, group_row, lower_bounds, layer_index, seq_lengths,
-    ))
+    ) = call_results(arrays[: len(OUTS)])
     return (
         block_out,
         grad_in,

time: 231 us -> 219 us (0.948)
  Pallas kernels: 229 us -> 218 us
    pallas_call x2 -> x1, Pallas kernels: 226 us -> 214 us  [call_block(): pl.pallas_call(layer_block, name='layer_block', out_shape=[jax.ShapeDtype...]
where the time goes in v5:
time: 219 us
  Pallas kernels  218 us (100%)
    pallas_call x1, Pallas kernels, call_block(): pl.pallas_call(layer_block, name='layer_block', out_shape=[jax.ShapeDtype...  214 us

profile of v5, /device:TPU:1, one launch (start us, length us, event | category | flops | bytes accessed | tf_op | source)
XLA Modules:
  0.0 219.1 jit_solution(6968513216160859749)
XLA Ops:
  1.3 214.5 %layer_block.1 = (bf16[64,2048]{1,0:T(8,128)(2,1)}, f32[64,2048]{1,0:T(8,128)}, f32[128,256]{1,0:T(8,128)}, f32[128,256]{1,0:T(8,128)}, f32[128,256]{1,0:T(8,128...) custom-call(bf16[512,2048]{1,0:T(8,128)(2,1)} %hid.1, ...), custom_call_target="tpu_custom_call" | custom-call | tf_op jit(solution)/shard_map/layer_block/pallas_call | solution.py:1227
  215.8 3.2 %results.1 = (bf16[64,2048]{1,0:T(8,128)(2,1)}, f32[64,2048]{1,0:T(8,128)}, f32[128,256]{1,0:T(8,128)}, f32[128,256]{1,0:T(8,128)}, f32[128,256]{1,0:T(8,128)}, ...) custom-call(bf16[64,2048]{1,0:T(8,128)(2,1)} %get-tuple-element.45.r, ...), custom_call_target="tpu_custom_call" | custom-call | tf_op jit(solution)/shard_map/results/pallas_call | solution.py:1301

commit v6 on v5

--- a/solution.py
+++ b/solution.py
@@ -371,15 +371,19 @@
         self.send_right()
         self.send_left()
 
+    def join(self, k):
+        p = self.p
+        self.left_x(k).wait_recv()
+        mine = self.part(p.y_at(k) * 2 + p.xl, ROWS, False)
+        one = self.left_of(64 * k)
+        one[...] = (one[...].astype(F32) + mine[...].astype(F32)).astype(BF16)
+        if k:
+            self.left_y(k).start()
+
     def middle(self):
         p = self.p
-        for k in (2, 1, 3, 0):
-            self.left_x(k).wait_recv()
-            mine = self.part(p.y_at(k) * 2 + p.xl, ROWS, False)
-            one = self.left_of(64 * k)
-            one[...] = (one[...].astype(F32) + mine[...].astype(F32)).astype(BF16)
-            if k:
-                self.left_y(k).start()
+        for k in (2, 1, 3):
+            self.join(k)
         for k in (1, 3, 2):
             self.right_y(k).wait_recv()
 
@@ -393,6 +397,7 @@
         self.slots[384:448, HALF:] = total(1 - p.xl)
         self.right_x().start()
         self.slots[448:512, 0:HALF] = total(p.xl)
+        self.join(0)
 
     def collect(self):
         for k in (1, 3, 2):
@@ -728,12 +733,13 @@
 
 def layer_block(
     hid, dy_in, wq, wf, wi, wo, w_output, wg_in, wu_in, wd_in, gain, lb, group_gain, ffn_gain, layer, seq,
+    i0, i1, i2, i3, i4, i5, i6, i7, i8, i9, i10, i11, i12, i13, i14, xn_out, w_out,
     block_out, grad_in, out_query, out_forget, out_input, out_outgate, out_output, out_bounds,
-    out_norm, out_group, out_ffn, out_mean, out_gate, out_up, out_down, xn_out, w_out,
+    out_norm, out_group, out_ffn, out_mean, out_gate, out_up, out_down,
     ps, slots, hn, wide, wg, wu, wd, wt, raw, hid_rows, gated, gated_t, mixed, run, states, update, resid, d_resid,
     hidden, dg, du, hidden_t, dg_t, du_t, draw, d_mixed, d_query, d_keys, d_values, decay, incoming, vec,
     norm_terms, ffn_terms, group_total, bound_total, total,
-    msg, sib, slots3, give, take, ex_send, ex_recv, msg2, sib2, slots4, give2, take2, ex2_send, ex2_recv,
+    msg, sib, slots3, give, take, ex_send, ex_recv, sib2, slots4, take2, ex2_send, ex2_recv,
     rs0_s, rs0_r, ag0_s, ag0_r, rs_s, rs_r, ag_s, ag_r, rs1_s, rs1_r, rs2_s, rs2_r,
     ws, wr, wh, os, or_, oh, s0, r0, h0, s1, r1, h1, s2, r2, h2,
     a0, a1, a2, a3, a4, a5, a6, b0, b1, b2, b3, b4, b5, b6, c0, c1, c2, c3, c4, c5, c6,
@@ -748,6 +754,17 @@
         move.start()
         used.append(move)
         return move
+
+    emitted = []
+    made = (
+        block_out, grad_in, out_query, out_forget, out_input, out_outgate, out_output, out_bounds,
+        out_norm, out_group, out_ffn, out_mean, out_gate, out_up, out_down,
+    )
+    to_emit = (i0, i1, i2, i3, i4, i5, i6, i7, i8, i9, i10, i11, i12, i13, i14)
+
+    def emit(*which):
+        for k in which:
+            emitted.append(load(made[k], to_emit[k]))
 
     def put(low, high):
         def write_four(x):
@@ -800,10 +817,9 @@
     gather.last()
     spills = [load(xn, xn_out), load(wide, w_out)]
 
-    @pl.loop(0, 4)
-    def _(j):
-        columns = pl.ds(pl.multiple_of(j * 256, 256), 256)
-        other = pl.ds(pl.multiple_of(1024 + j * 256, 256), 256)
+    for j in range(4):
+        columns = slice(j * 256, (j + 1) * 256)
+        other = slice(1024 + j * 256, 1024 + (j + 1) * 256)
         raw[:, columns] = mm(xn[:, 0:1024], wide[:, columns], NN) + mm(xn[:, 1024:2048], wide[:, other], NN)
 
     later.second()
@@ -856,8 +872,6 @@
     gathers[0].second()
     later.fourth()
     exchange.result(incoming)
-    gathers[1].second()
-    gathers[2].second()
     for h in range(2):
         lanes = slice(h * 128, (h + 1) * 128)
         state = incoming[h]
@@ -881,6 +895,7 @@
             gate = raw[rows, 768 + h * 128 : 768 + (h + 1) * 128]
             gated[rows, lanes] = (x * scale * group_gain[...] * (gate * sigmoid(gate))).astype(BF16)
 
+    gathers[1].second()
     later.last()
 
     for move in spills:
@@ -888,16 +903,16 @@
     dy_load = load(dy_in, dy)
     scatter0 = HeadSum(p, ps, slots, rs0_s, rs0_r)
     for start, send in ((HALF, scatter0.send_right), (0, scatter0.send_left)):
-
-        @pl.loop(0, 4)
-        def _(j):
-            columns = pl.ds(pl.multiple_of(start + j * 256, 256), 256)
+        for j in range(4):
+            columns = slice(start + j * 256, start + (j + 1) * 256)
             ps[:, columns] = mm(gated[...], wt[:, columns], NN).astype(BF16)
 
         send()
+    gathers[2].second()
+    gathers[0].third()
     scatter0.middle()
-    for g in gathers:
-        g.third()
+    gathers[1].third()
+    gathers[2].third()
     scatter0.collect()
     own_rows.wait()
 
@@ -935,10 +950,8 @@
 
     scatter = HeadSum(p, ps, slots, rs_s, rs_r)
     for start, send in ((HALF, scatter.send_right), (0, scatter.send_left)):
-
-        @pl.loop(0, 4)
-        def _(j):
-            columns = pl.ds(pl.multiple_of(start + j * 256, 256), 256)
+        for j in range(4):
+            columns = slice(start + j * 256, start + (j + 1) * 256)
             ps[:, columns] = (mm(dg[...], wg[:, columns], NN) + mm(du[...], wu[:, columns], NN)).astype(BF16)
 
         send()
@@ -959,16 +972,6 @@
     products(hidden_t, dy, c0)
     sums[1].to_z()
     sums[2].to_sibling()
-    sums[0].join()
-
-    @pl.loop(0, 8)
-    def _(j):
-        columns = pl.ds(pl.multiple_of(j * 256, 256), 256)
-        wu[0:TOK, columns] = mm(hidden[...], wd[:, columns], NN).astype(BF16)
-
-    sums[2].to_z()
-    spread0.finish()
-    late = [load(xn_out, hn), load(w_out.at[0:TOK], wd.at[0:TOK])]
     scatter.collect()
     ffn_terms[...] = jnp.zeros_like(ffn_terms)
 
@@ -988,9 +991,18 @@
     scatter.finish()
     spread = HeadGather(p, db, ag_s, ag_r)
     spread.send()
+    sums[2].to_z()
     spread.middle()
+    sums[0].join()
+
+    @pl.loop(0, 8)
+    def _(j):
+        columns = pl.ds(pl.multiple_of(j * 256, 256), 256)
+        wu[0:TOK, columns] = mm(hidden[...], wd[:, columns], NN).astype(BF16)
+
     sums[1].join()
-    late.append(load(w_out.at[TOK : 2 * TOK], dy))
+    spread0.finish()
+    late = [load(xn_out, hn), load(w_out.at[0:TOK], wd.at[0:TOK]), load(w_out.at[TOK : 2 * TOK], dy)]
     group_total[...] = jnp.zeros_like(group_total)
     for move in late:
         move.wait()
@@ -1032,9 +1044,9 @@
         for c in range(CHUNKS - 2, -1, -1):
             state = state * decay[c, 0:1, lanes] + update[h, c]
             rate = rate * decay[c, 0:1, lanes]
-        msg2[h, 0:128, :] = state
-        msg2[h, 128:136, :] = jnp.broadcast_to(rate, (8, 128))
-    exchange2 = Exchange(p, msg2, sib2, slots4, give2, take2, ex2_send, ex2_recv, True)
+        msg[h, 0:128, :] = state
+        msg[h, 128:136, :] = jnp.broadcast_to(rate, (8, 128))
+    exchange2 = Exchange(p, msg, sib2, slots4, give, take2, ex2_send, ex2_recv, True)
     exchange2.to_sibling()
     results = (out_gate, out_up, out_down)
     for one, out in zip(sums[:2], results):
@@ -1082,6 +1094,7 @@
     sums[2].to_x(write(out_down))
     for one, out in zip(sums[:2], results):
         one.end(accumulate(out))
+    emit(12, 13)
     first.to_z()
     bound_total[...] = jnp.zeros_like(bound_total)
 
@@ -1119,17 +1132,18 @@
     scatter2 = HeadSum(p, ps, slots, rs2_s, rs2_r)
     for start, send in ((HALF, scatter2.send_right), (0, scatter2.send_left)):
         for first_row, part in ((0, wd), (TOK, dy)):
-
-            @pl.loop(0, 2)
-            def _(j):
-                rows = pl.ds(pl.multiple_of(j * 256, 256), 256)
-                columns = pl.ds(pl.multiple_of(start + first_row + j * 256, 256), 256)
+            for j in range(2):
+                rows = slice(j * 256, (j + 1) * 256)
+                columns = slice(start + first_row + j * 256, start + first_row + (j + 1) * 256)
                 ps[:, columns] = mm(draw[...], part[rows, start : start + HALF], NT).astype(BF16)
 
         send()
     products_turned(hn, draw.at[:, 256:512], draw.at[:, 512:768], b0)
     second.to_sibling()
     first.join()
+    products(gated_t, db, e0)
+    second.to_z()
+    third.to_sibling()
 
     @pl.loop(0, 8)
     def _(j):
@@ -1147,18 +1161,17 @@
     vec[35:36, :] = bound_total[:, 128:256]
     everywhere = Total(p, vec, t0, t1, t2, t3, t4, t5, t6, t7, t8.at[0], t9.at[0])
     everywhere.send()
-    second.to_z()
+    second.join()
+    third.to_z()
     scatter2.middle()
-    products(gated_t, db, e0)
-    third.to_sibling()
     everywhere.middle()
-    third.to_z()
+    third.join()
     everywhere.late()
     scatter1.middle()
-    second.join()
     sums[2].end(accumulate(out_down))
+    emit(14)
     first.to_x(put(out_query, out_outgate))
-    third.join()
+    second.to_x(put(out_forget, out_input))
     scatter2.collect()
 
     @pl.loop(0, 4)
@@ -1170,6 +1183,9 @@
         back = inverse * (scaled - normed * jnp.mean(scaled * normed, axis=-1, keepdims=True))
         grad_in[rows, :] = d_resid[rows, :] + back
 
+    emit(1)
+
+    third.to_x(write(out_output))
     scatter1.collect()
 
     @pl.loop(0, 4)
@@ -1177,8 +1193,8 @@
         rows = pl.ds(pl.multiple_of(i * 16, 16), 16)
         block_out[rows, :] = (resid[rows, :] + scatter1.rows(i * 16, 16)).astype(BF16)
 
-    second.to_x(put(out_forget, out_input))
-    third.to_x(write(out_output))
+    emit(0)
+
     all_of = everywhere.result()
     out_norm[...] = all_of[0:16]
     out_ffn[...] = all_of[16:32]
@@ -1188,10 +1204,14 @@
     for h in range(2):
         lanes = slice(h * 128, (h + 1) * 128)
         out_bounds[:, lanes] = soft[:, lanes] * (picked[:, lanes] - bound[:, lanes]) * all_of[34 + h : 35 + h]
+    emit(7, 8, 9, 10, 11)
 
     first.end(add_to(out_query, out_outgate))
+    emit(2, 5)
     second.end(add_to(out_forget, out_input))
+    emit(3, 4)
     third.end(accumulate(out_output))
+    emit(6)
     spread.finish()
     scatter1.finish()
     scatter2.finish()
@@ -1199,6 +1219,8 @@
     everywhere.finish()
     for one in (first, second, third, sums[2]):
         one.finish()
+    for move in emitted:
+        move.wait()
 
 
 OUTS = (
@@ -1229,8 +1251,9 @@
         name="layer_block",
         out_shape=[jax.ShapeDtypeStruct(*one) for one in shapes],
         in_specs=[HB] * 10 + [VM] * 4 + [SM, SM],
-        out_specs=[VM] * len(OUTS) + [HB, HB],
+        out_specs=[HB] * (len(OUTS) + 2),
         scratch_shapes=[
+            *[pltpu.VMEM(*one) for one in OUTS],
             *[pltpu.VMEM((TOK, D), BF16)] * 3,
             pltpu.VMEM((2 * TOK, D), BF16),
             *[pltpu.VMEM((FFH, D), BF16)] * 3,
@@ -1257,7 +1280,7 @@
             pltpu.VMEM((1, HERE), F32),
             pltpu.VMEM((1, HERE), F32),
             *exchange_scratch(),
-            *exchange_scratch(),
+            *[one for k, one in enumerate(exchange_scratch()) if k not in (0, 3)],
             *sixteen(),
             *sixteen(),
             *sixteen(),
@@ -1283,7 +1306,7 @@
             *eight(),
             pltpu.SemaphoreType.DMA((1,)),
             pltpu.SemaphoreType.DMA((1,)),
-            pltpu.SemaphoreType.DMA((20,)),
+            pltpu.SemaphoreType.DMA((32,)),
         ],
         compiler_params=pltpu.CompilerParams(
             collective_id=0, has_side_effects=True, vmem_limit_bytes=60 * 1024 * 1024
@@ -1292,9 +1315,17 @@
 
 
 def results(*refs):
-    half = len(refs) // 2
-    for one, out in zip(refs[:half], refs[half:]):
-        out[...] = one[...]
+    count, sems = len(OUTS), refs[-1]
+    ins, outs, held = refs[:count], refs[count : 2 * count], refs[2 * count : 3 * count]
+    reads = [pltpu.make_async_copy(ins[k], held[k], sems.at[0, k]) for k in range(count)]
+    writes = [pltpu.make_async_copy(held[k], outs[k], sems.at[1, k]) for k in range(count)]
+    for move in reads:
+        move.start()
+    for read, move in zip(reads, writes):
+        read.wait()
+        move.start()
+    for move in writes:
+        move.wait()
 
 
 def call_results(arrays):
@@ -1302,8 +1333,9 @@
         results,
         name="results",
         out_shape=[jax.ShapeDtypeStruct(*one) for one in OUTS],
-        in_specs=[VM] * len(OUTS),
-        out_specs=[VM] * len(OUTS),
+        in_specs=[HB] * len(OUTS),
+        out_specs=[HB] * len(OUTS),
+        scratch_shapes=[*[pltpu.VMEM(*one) for one in OUTS], pltpu.SemaphoreType.DMA((2, len(OUTS)))],
     )(*arrays)
 
 

time: 219 us -> 209 us (0.954)
  Pallas kernels: 218 us -> 208 us
    pallas_call x1, Pallas kernels: 214 us -> 205 us  [call_block(): pl.pallas_call(layer_block, name='layer_block', out_shape=[jax.ShapeDtype...]
where the time goes in v6:
time: 209 us
  Pallas kernels  208 us (100%)
    pallas_call x1, Pallas kernels, call_block(): pl.pallas_call(layer_block, name='layer_block', out_shape=[jax.ShapeDtype...  205 us

profile of v6, /device:TPU:1, one launch (start us, length us, event | category | flops | bytes accessed | tf_op | source)
XLA Modules:
  0.0 209.1 jit_solution(11040654373322785638)
XLA Ops:
  1.3 204.9 %layer_block.1 = (bf16[64,2048]{1,0:T(8,128)(2,1)}, f32[64,2048]{1,0:T(8,128)}, f32[128,256]{1,0:T(8,128)}, f32[128,256]{1,0:T(8,128)}, f32[128,256]{1,0:T(8,128...) custom-call(bf16[512,2048]{1,0:T(8,128)(2,1)} %hid.1, ...), custom_call_target="tpu_custom_call" | custom-call | tf_op jit(solution)/shard_map/layer_block/pallas_call | solution.py:1249
  206.2 2.8 %results.1 = (bf16[64,2048]{1,0:T(8,128)(2,1)}, f32[64,2048]{1,0:T(8,128)}, f32[128,256]{1,0:T(8,128)}, f32[128,256]{1,0:T(8,128)}, f32[128,256]{1,0:T(8,128)}, ...) custom-call(bf16[64,2048]{1,0:T(8,128)(2,1)} %get-tuple-element.45.r, ...), custom_call_target="tpu_custom_call" | custom-call | tf_op jit(solution)/shard_map/results/pallas_call | solution.py:1332

commit v7 on v6

--- a/solution.py
+++ b/solution.py
@@ -150,13 +150,58 @@
 
 
 class WideGather(Gather):
+    def __init__(self, spot, g, send, recv, half, offset=0):
+        super().__init__(spot, g, send, recv, half)
+        self.offset, self.middle = offset, 32
+
     def block(self, d, start=0, rows=0):
-        row, column = lax.rem(d, 8) * 128 + start, lax.div(d, 8) * 1024
-        return self.g.at[pl.ds(pl.multiple_of(row, 64), rows or 128), pl.ds(pl.multiple_of(column, 1024), 1024)]
+        row, column = lax.rem(d, 8) * 128 + (self.offset + start), lax.div(d, 8) * 1024
+        return self.g.at[pl.ds(pl.multiple_of(row, 32), rows or 64), pl.ds(pl.multiple_of(column, 1024), 1024)]
 
     def tile(self, d, k):
         row, column = lax.rem(d, 8) * 128, lax.div(d, 8) * 1024 + 256 * k
         return self.g.at[pl.ds(pl.multiple_of(row, 128), 128), pl.ds(pl.multiple_of(column, 256), 256)]
+
+
+class LowerGather(WideGather):
+    def first(self):
+        p = self.spot
+        self.push(p.dp, p.at(1, p.xh, p.core), 0)
+        self.push(p.dp, p.at(3, p.xh, p.core), 1)
+        self.push(p.dp, p.at(0, 1 - p.xh, p.core), 2)
+        self.push(p.dp, p.at(0, p.xh, 1 - p.core), 3)
+
+    def second(self):
+        p = self.spot
+        for part, (source, to) in enumerate(((3, 1), (1, 3))):
+            b = p.at(source, p.xh, p.core)
+            self.arrived(b)
+            self.push_half(b, p.at(to, p.xh, p.core), 4 + part, 0, part)
+            self.push(b, p.at(0, 1 - p.xh, p.core), 6 + part)
+            self.push(b, p.at(0, p.xh, 1 - p.core), 8 + part)
+
+    def third(self):
+        p = self.spot
+        b = p.at(2, p.xh, p.core)
+        self.arrived_halves(b, 0)
+        self.push(b, p.at(0, 1 - p.xh, p.core), 10)
+        self.push(b, p.at(0, p.xh, 1 - p.core), 11)
+
+    def fourth(self):
+        p = self.spot
+        for k, dz in enumerate((0, 3, 1, 2)):
+            b = p.at(dz, 1 - p.xh, p.core)
+            self.arrived(b)
+            self.push(b, p.at(0, p.xh, 1 - p.core), 12 + k)
+
+    def last(self):
+        p = self.spot
+        for dz in range(4):
+            for h in range(2):
+                self.arrived(p.at(dz, h, 1 - p.core))
+        for k in range(16):
+            b = self.block(0, 0, self.middle) if k in (4, 5) else self.block(0)
+            rcopy(b, b, self.s.at[k], self.r.at[0], p.sibling).wait_send()
 
 
 def gather_semaphores():
@@ -602,7 +647,7 @@
         where = {"dp": (p.z * 2 + 1 - p.xh) * 2 + p.core}
         return rcopy(self.xs, self.xr, self.s.at[10], self.r.at[10], where)
 
-    def to_x(self, put):
+    def to_x(self, put, go=True):
         p = self.p
         for part in range(2):
             self.near(part).wait_recv()
@@ -615,8 +660,12 @@
             return one
 
         self.xs[...] = total(1 - p.xh).astype(BF16)
+        if go:
+            self.go()
+        put(total(p.xh))
+
+    def go(self):
         self.last_move().start()
-        put(total(p.xh))
 
     def end(self, add):
         self.last_move().wait_recv()
@@ -741,7 +790,7 @@
     norm_terms, ffn_terms, group_total, bound_total, total,
     msg, sib, slots3, give, take, ex_send, ex_recv, sib2, slots4, take2, ex2_send, ex2_recv,
     rs0_s, rs0_r, ag0_s, ag0_r, rs_s, rs_r, ag_s, ag_r, rs1_s, rs1_r, rs2_s, rs2_r,
-    ws, wr, wh, os, or_, oh, s0, r0, h0, s1, r1, h1, s2, r2, h2,
+    ws, wr, wh, vs, vr, vh, os, or_, oh, s0, r0, h0, s1, r1, h1, s2, r2, h2,
     a0, a1, a2, a3, a4, a5, a6, b0, b1, b2, b3, b4, b5, b6, c0, c1, c2, c3, c4, c5, c6,
     e0, e1, e2, e3, e4, e5, e6, f3, f4, f5, f6, g3, g4, g5, g6,
     t0, t1, t2, t3, t4, t5, t6, t7, t8, t9, local_sem,
@@ -787,6 +836,7 @@
     own = pl.multiple_of(p.head * ROWS, ROWS)
     mine = pl.ds(pl.multiple_of(p.dp * 128, 128), 128)
     gather = WideGather(p, wide, ws, wr, wh)
+    lower = LowerGather(p, wide, vs, vr, vh, 64)
     loads = [load(one, gather.tile(p.dp, k)) for k, one in enumerate((wq, wf, wi, wo))]
     loads.append(load(hid, ps))
     own_blocks = [load(w_output, wt.at[:, mine])]
@@ -796,6 +846,7 @@
         move.wait()
     arrive()
     gather.first()
+    lower.first()
     loads[4].wait()
     later = Gather(p, wt, os, or_, oh, HERE)
     gathers = [Gather(p, wg, s0, r0, h0, FFH), Gather(p, wu, s1, r1, h1, FFH), Gather(p, wd, s2, r2, h2, FFH)]
@@ -808,13 +859,17 @@
         xn[rows, :] = (x * scale * gain[...]).astype(BF16)
 
     gather.second()
+    lower.second()
     gather.third()
+    lower.third()
     gather.fourth()
+    lower.fourth()
     for move in own_blocks:
         move.wait()
     later.first()
     gathers[0].first()
     gather.last()
+    lower.last()
     spills = [load(xn, xn_out), load(wide, w_out)]
 
     for j in range(4):
@@ -1050,8 +1105,10 @@
     exchange2.to_sibling()
     results = (out_gate, out_up, out_down)
     for one, out in zip(sums[:2], results):
-        one.to_x(write(out))
+        one.to_x(write(out), go=False)
     exchange2.to_chips()
+    for one in sums[:2]:
+        one.go()
 
     @pl.loop(0, CHUNKS)
     def _(c):
@@ -1138,12 +1195,9 @@
                 ps[:, columns] = mm(draw[...], part[rows, start : start + HALF], NT).astype(BF16)
 
         send()
+    first.join()
     products_turned(hn, draw.at[:, 256:512], draw.at[:, 512:768], b0)
     second.to_sibling()
-    first.join()
-    products(gated_t, db, e0)
-    second.to_z()
-    third.to_sibling()
 
     @pl.loop(0, 8)
     def _(j):
@@ -1161,17 +1215,20 @@
     vec[35:36, :] = bound_total[:, 128:256]
     everywhere = Total(p, vec, t0, t1, t2, t3, t4, t5, t6, t7, t8.at[0], t9.at[0])
     everywhere.send()
+    second.to_z()
+    products(gated_t, db, e0)
+    third.to_sibling()
     second.join()
+    scatter2.middle()
     third.to_z()
-    scatter2.middle()
     everywhere.middle()
+    first.to_x(put(out_query, out_outgate))
+    scatter1.middle()
+    everywhere.late()
+    second.to_x(put(out_forget, out_input))
     third.join()
-    everywhere.late()
-    scatter1.middle()
     sums[2].end(accumulate(out_down))
     emit(14)
-    first.to_x(put(out_query, out_outgate))
-    second.to_x(put(out_forget, out_input))
     scatter2.collect()
 
     @pl.loop(0, 4)
@@ -1292,6 +1349,7 @@
             *gather_semaphores(),
             *gather_semaphores(),
             *gather_semaphores(),
+            *gather_semaphores(),
             *sums,
             *sums,
             *sums,

time: 209 us -> 203 us (0.971)
  Pallas kernels: 208 us -> 201 us
    pallas_call x1, Pallas kernels: 205 us -> 198 us  [call_block(): pl.pallas_call(layer_block, name='layer_block', out_shape=[jax.ShapeDtype...]
where the time goes in v7:
time: 203 us
  Pallas kernels  201 us (99%)
    pallas_call x1, Pallas kernels, call_block(): pl.pallas_call(layer_block, name='layer_block', out_shape=[jax.ShapeDtype...  198 us

profile of v7, /device:TPU:1, one launch (start us, length us, event | category | flops | bytes accessed | tf_op | source)
XLA Modules:
  0.0 202.5 jit_solution(18183955220995951380)
XLA Ops:
  1.3 198.3 %layer_block.1 = (bf16[64,2048]{1,0:T(8,128)(2,1)}, f32[64,2048]{1,0:T(8,128)}, f32[128,256]{1,0:T(8,128)}, f32[128,256]{1,0:T(8,128)}, f32[128,256]{1,0:T(8,128...) custom-call(bf16[512,2048]{1,0:T(8,128)(2,1)} %hid.1, ...), custom_call_target="tpu_custom_call" | custom-call | tf_op jit(solution)/shard_map/layer_block/pallas_call | solution.py:1306
  199.6 2.8 %results.1 = (bf16[64,2048]{1,0:T(8,128)(2,1)}, f32[64,2048]{1,0:T(8,128)}, f32[128,256]{1,0:T(8,128)}, f32[128,256]{1,0:T(8,128)}, f32[128,256]{1,0:T(8,128)}, ...) custom-call(bf16[64,2048]{1,0:T(8,128)(2,1)} %get-tuple-element.45.r, ...), custom_call_target="tpu_custom_call" | custom-call | tf_op jit(solution)/shard_map/results/pallas_call | solution.py:1390

commit v8 on v7

--- a/solution.py
+++ b/solution.py
@@ -524,54 +524,73 @@
     def __init__(self, spot, full, send, recv):
         self.p, self.full, self.s, self.r = spot, full, send, recv
 
-    def block(self, h, right):
-        return self.full.at[pl.ds(pl.multiple_of(h * ROWS, ROWS), ROWS), pl.ds(HALF if right else 0, HALF)]
-
-    def along_y(self, k, xl, right, i):
-        p = self.p
-        b = self.block(p.y * 2 + xl, right)
-        return rcopy(b, b, self.s.at[i + k], self.r.at[i + k], {"head": p.y_at(k) * 2 + p.xl})
-
-    def beside(self, k, right, i):
-        p = self.p
-        b = self.block(p.y_at(k) * 2 + p.xl, right)
-        return rcopy(b, b, self.s.at[i + k], self.r.at[i + k], p.beside)
+    def block(self, dy, stream, start=0, rows=ROWS):
+        p = self.p
+        h = p.y_at(dy) * 2 + (1 - p.xl if stream == 2 else p.xl)
+        columns = pl.ds(0 if stream else HALF, HALF)
+        return self.full.at[pl.ds(pl.multiple_of(h * ROWS + start, 32), rows), columns]
+
+    def along_y(self, stream, k):
+        p = self.p
+        b, i = self.block(0, stream), 4 * stream + (k == 3)
+        return rcopy(b, b, self.s.at[i], self.r.at[i], {"head": p.y_at(k) * 2 + p.xl})
+
+    def onward(self, stream, part):
+        p = self.p
+        b, i = self.block(1 if part else 3, stream, 32 * part, 32), 4 * stream + 2 + part
+        return rcopy(b, b, self.s.at[i], self.r.at[i], {"head": p.y_at(3 if part else 1) * 2 + p.xl})
+
+    def beside(self, dy, stream):
+        b, i = self.block(dy, stream), 12 if stream else 13 + dy
+        return rcopy(b, b, self.s.at[i], self.r.at[i], self.p.beside)
 
     def send(self):
-        p = self.p
-        self.beside(0, False, 0).start()
-        for k in (2, 1, 3):
-            self.along_y(k, p.xl, True, 0).start()
-        self.beside(0, True, 4).start()
-        for k in (2, 1, 3):
-            self.along_y(k, p.xl, False, 8).start()
+        self.beside(0, 1).start()
+        for k in (1, 3):
+            self.along_y(0, k).start()
+        self.beside(0, 0).start()
+        for k in (1, 3):
+            self.along_y(1, k).start()
 
     def middle(self):
-        p = self.p
-        self.beside(0, False, 0).wait_recv()
-        for k in (2, 1, 3):
-            self.along_y(k, 1 - p.xl, False, 11).start()
-        for k in (1, 3, 2):
-            self.along_y(4 - k, p.xl, True, 0).wait_recv()
-            self.beside(k, True, 4).start()
+        self.beside(0, 1).wait_recv()
+        for k in (1, 3):
+            self.along_y(2, k).start()
+        for part in range(2):
+            self.along_y(0, 3 if part else 1).wait_recv()
+            self.onward(0, part).start()
+            self.beside(1 if part else 3, 0).start()
+        for part in range(2):
+            self.along_y(1, 3 if part else 1).wait_recv()
+            self.onward(1, part).start()
+
+    def late(self):
+        for part in range(2):
+            self.along_y(2, 3 if part else 1).wait_recv()
+            self.onward(2, part).start()
+        for part in range(2):
+            self.onward(0, part).wait_recv()
+        self.beside(2, 0).start()
 
     def collect(self):
-        p = self.p
-        self.beside(0, True, 4).wait_recv()
-        for k in (1, 3, 2):
-            self.along_y(k, p.xl, False, 8).wait_recv()
-            self.along_y(k, 1 - p.xl, False, 11).wait_recv()
-            self.beside(k, True, 4).wait_recv()
+        for dy in range(4):
+            self.beside(dy, 0).wait_recv()
+        for stream in (1, 2):
+            for part in range(2):
+                self.onward(stream, part).wait_recv()
 
     def finish(self):
-        p = self.p
-        self.beside(0, False, 0).wait_send()
-        for k in range(4):
-            self.beside(k, True, 4).wait_send()
-        for k in (1, 2, 3):
-            self.along_y(k, p.xl, True, 0).wait_send()
-            self.along_y(k, p.xl, False, 8).wait_send()
-            self.along_y(k, 1 - p.xl, False, 11).wait_send()
+        self.beside(0, 1).wait_send()
+        for dy in range(4):
+            self.beside(dy, 0).wait_send()
+        for stream in range(3):
+            for part in range(2):
+                self.along_y(stream, 3 if part else 1).wait_send()
+                self.onward(stream, part).wait_send()
+
+
+def twenty():
+    return [pltpu.SemaphoreType.DMA((20,)), pltpu.SemaphoreType.DMA((20,))]
 
 
 def sixteen():
@@ -889,24 +908,14 @@
         total[...] += jnp.sum(forget, axis=0, keepdims=True)
         running = summed_rows(True, jnp.log(forget))
         run[rows, :] = running
-        middle, ending = running[63:64], running[127:128]
-        lifted = query.astype(F32) * jnp.exp(running - middle)
-        lowered = keys.astype(F32) * jnp.exp(middle - running)
+        ending = running[127:128]
         tail = keys.astype(F32) * jnp.exp(ending - running)
-        column, row = segments.column(c), segments.row(c)
-        linked = (column == row) & (
-            lax.broadcasted_iota(jnp.int32, (CHUNK, CHUNK), 0)
-            >= lax.broadcasted_iota(jnp.int32, (CHUNK, CHUNK), 1)
-        )
         final = segments.final(c)
         rate = jnp.exp(ending) * jnp.where(final == segments.before(c), 1.0, 0.0)
         decay[c] = jnp.broadcast_to(rate, (8, HERE))
-        ends = jnp.where(column == final, 1.0, 0.0)
+        ends = jnp.where(segments.column(c) == final, 1.0, 0.0)
         for h in range(2):
             lanes = slice(h * 128, (h + 1) * 128)
-            scores = mm3(halves(lifted[:, lanes]), halves(lowered[:, lanes]), NT)
-            scores = jnp.where(linked, scores, 0.0)
-            mixed[rows, lanes] = mm2(halves(scores), values[:, lanes], NN)
             high, low = halves(tail[:, lanes] * ends)
             update[h, c] = mm(values[:, lanes], high, TN) + mm(values[:, lanes], low, TN)
 
@@ -921,6 +930,25 @@
     exchange = Exchange(p, msg, sib, slots3, give, take, ex_send, ex_recv, False)
     exchange.to_sibling()
     exchange.to_chips()
+
+    @pl.loop(0, CHUNKS)
+    def _(c):
+        rows = pl.ds(pl.multiple_of(c * CHUNK, CHUNK), CHUNK)
+        _, _, query, keys, values = gates(raw, bound, rows)
+        running = run[rows, :]
+        middle = running[63:64]
+        lifted = query.astype(F32) * jnp.exp(running - middle)
+        lowered = keys.astype(F32) * jnp.exp(middle - running)
+        linked = (segments.column(c) == segments.row(c)) & (
+            lax.broadcasted_iota(jnp.int32, (CHUNK, CHUNK), 0)
+            >= lax.broadcasted_iota(jnp.int32, (CHUNK, CHUNK), 1)
+        )
+        for h in range(2):
+            lanes = slice(h * 128, (h + 1) * 128)
+            scores = mm3(halves(lifted[:, lanes]), halves(lowered[:, lanes]), NT)
+            scores = jnp.where(linked, scores, 0.0)
+            mixed[rows, lanes] = mm2(halves(scores), values[:, lanes], NN)
+
     later.third()
     gathers[1].first()
     gathers[2].first()
@@ -986,6 +1014,7 @@
     spread0.middle()
     for g in gathers:
         g.fourth()
+    spread0.late()
     for g in gathers:
         g.last()
     dy_load.wait()
@@ -1049,6 +1078,7 @@
     sums[2].to_z()
     spread.middle()
     sums[0].join()
+    spread.late()
 
     @pl.loop(0, 8)
     def _(j):
@@ -1065,16 +1095,16 @@
     spread.collect()
     scatter1 = LateHeadSum(p, wu, wg, rs1_s, rs1_r)
     scatter1.send()
+    d_query[...] = mm(db[...], wt[...], NT)
 
     @pl.loop(0, CHUNKS)
     def _(c):
         rows = pl.ds(pl.multiple_of(c * CHUNK, CHUNK), CHUNK)
-        d_gated = mm(db[rows, :], wt[...], NT)
         carried = jnp.where(segments.column(c) == segments.before(c), 1.0, 0.0)
         running = run[rows, :]
         for h in range(2):
             lanes = slice(h * 128, (h + 1) * 128)
-            x, grad = mixed[rows, lanes], d_gated[:, lanes]
+            x, grad = mixed[rows, lanes], d_query[rows, lanes]
             gate = raw[rows, 768 + h * 128 : 768 + (h + 1) * 128]
             s = sigmoid(gate)
             inverse = lax.rsqrt(jnp.mean(x * x, axis=-1, keepdims=True) + EPS)
@@ -1339,9 +1369,9 @@
             *exchange_scratch(),
             *[one for k, one in enumerate(exchange_scratch()) if k not in (0, 3)],
             *sixteen(),
+            *twenty(),
             *sixteen(),
-            *sixteen(),
-            *sixteen(),
+            *twenty(),
             *eight(),
             *sixteen(),
             *gather_semaphores(),

time: 203 us -> 198 us (0.975)
  Pallas kernels: 201 us -> 195 us
    pallas_call x1, Pallas kernels: 198 us -> 193 us  [call_block(): pl.pallas_call(layer_block, name='layer_block', out_shape=[jax.ShapeDtype...]
where the time goes in v8:
time: 198 us; the launch traced here: 197 us
  Pallas kernels  195 us (98%)
    pallas_call x1, Pallas kernels, call_block(): pl.pallas_call(layer_block, name='layer_block', out_shape=[jax.ShapeDtype...  193 us

profile of v8, /device:TPU:1, one launch (start us, length us, event | category | flops | bytes accessed | tf_op | source)
XLA Modules:
  0.0 196.9 jit_solution(4880560678230393532)
XLA Ops:
  1.3 192.6 %layer_block.1 = (bf16[64,2048]{1,0:T(8,128)(2,1)}, f32[64,2048]{1,0:T(8,128)}, f32[128,256]{1,0:T(8,128)}, f32[128,256]{1,0:T(8,128)}, f32[128,256]{1,0:T(8,128...) custom-call(bf16[512,2048]{1,0:T(8,128)(2,1)} %hid.1, ...), custom_call_target="tpu_custom_call" | custom-call | tf_op jit(solution)/shard_map/layer_block/pallas_call | solution.py:1336
  193.9 2.8 %results.1 = (bf16[64,2048]{1,0:T(8,128)(2,1)}, f32[64,2048]{1,0:T(8,128)}, f32[128,256]{1,0:T(8,128)}, f32[128,256]{1,0:T(8,128)}, f32[128,256]{1,0:T(8,128)}, ...) custom-call(bf16[64,2048]{1,0:T(8,128)(2,1)} %get-tuple-element.45.r, ...), custom_call_target="tpu_custom_call" | custom-call | tf_op jit(solution)/shard_map/results/pallas_call | solution.py:1420

commit v9 on v8

--- a/solution.py
+++ b/solution.py
@@ -953,8 +953,8 @@
     gathers[1].first()
     gathers[2].first()
     gathers[0].second()
+    exchange.result(incoming)
     later.fourth()
-    exchange.result(incoming)
     for h in range(2):
         lanes = slice(h * 128, (h + 1) * 128)
         state = incoming[h]
@@ -992,8 +992,8 @@
 
         send()
     gathers[2].second()
+    scatter0.middle()
     gathers[0].third()
-    scatter0.middle()
     gathers[1].third()
     gathers[2].third()
     scatter0.collect()
@@ -1249,8 +1249,8 @@
     products(gated_t, db, e0)
     third.to_sibling()
     second.join()
+    third.to_z()
     scatter2.middle()
-    third.to_z()
     everywhere.middle()
     first.to_x(put(out_query, out_outgate))
     scatter1.middle()

time: 198 us -> 197 us (level)
  no operation moved by 1% of the time
where the time goes in v9:
time: 197 us
  Pallas kernels  196 us (99%)
    pallas_call x1, Pallas kernels, call_block(): pl.pallas_call(layer_block, name='layer_block', out_shape=[jax.ShapeDtype...  193 us

profile of v9, /device:TPU:1, one launch (start us, length us, event | category | flops | bytes accessed | tf_op | source)
XLA Modules:
  0.0 197.1 jit_solution(4123427624946388625)
XLA Ops:
  1.3 192.8 %layer_block.1 = (bf16[64,2048]{1,0:T(8,128)(2,1)}, f32[64,2048]{1,0:T(8,128)}, f32[128,256]{1,0:T(8,128)}, f32[128,256]{1,0:T(8,128)}, f32[128,256]{1,0:T(8,128...) custom-call(bf16[512,2048]{1,0:T(8,128)(2,1)} %hid.1, ...), custom_call_target="tpu_custom_call" | custom-call | tf_op jit(solution)/shard_map/layer_block/pallas_call | solution.py:1336
  194.1 2.8 %results.1 = (bf16[64,2048]{1,0:T(8,128)(2,1)}, f32[64,2048]{1,0:T(8,128)}, f32[128,256]{1,0:T(8,128)}, f32[128,256]{1,0:T(8,128)}, f32[128,256]{1,0:T(8,128)}, ...) custom-call(bf16[64,2048]{1,0:T(8,128)(2,1)} %get-tuple-element.45.r, ...), custom_call_target="tpu_custom_call" | custom-call | tf_op jit(solution)/shard_map/results/pallas_call | solution.py:1420
